TPU v7x, 32 devices: a whole 2x2x4 slice. The times are simulated.
32 devices in a mesh: ctx: 2 (over y), fsdp: 16 (over z, x, core).
Axes of the slice: x: 2, y: 2, z: 4, core: 2. Of those that a mesh axis runs over, the one named last changes fastest.
Arguments:
- tokens: bfloat16 [16, 256, 2048], P('fsdp', 'ctx'), may hold values from -6 to 6
- attn_norm: bfloat16 [2048], P(('ctx', 'fsdp')), may hold values from 0.5 to 1.5
- w_query: bfloat16 [2048, 3072], P(('ctx', 'fsdp')), may hold values from -0.125 to 0.125
- w_latent: bfloat16 [2048, 576], P(('ctx', 'fsdp')), may hold values from -0.125 to 0.125
- latent_norm: bfloat16 [512], P(('ctx', 'fsdp')), may hold values from 0.5 to 1.5
- w_expand: bfloat16 [512, 4096], P(('ctx', 'fsdp')), may hold values from -0.25 to 0.25
- w_output: bfloat16 [2048, 2048], P(('ctx', 'fsdp')), may hold values from -1 to 1
- ffn_norm: bfloat16 [2048], P(('ctx', 'fsdp')), may hold values from 0.5 to 1.5
- w_router: bfloat16 [2048, 16], P(('ctx', 'fsdp')), may hold values from -0.0625 to 0.0625
- shared_gate: bfloat16 [2048, 2816], P(('ctx', 'fsdp')), may hold values from -0.125 to 0.125
- shared_up: bfloat16 [2048, 2816], P(('ctx', 'fsdp')), may hold values from -0.125 to 0.125
- shared_down: bfloat16 [2816, 2048], P(('ctx', 'fsdp')), may hold values from -0.21875 to 0.21875
- expert_gate: bfloat16 [16, 2048, 1408], P('fsdp', 'ctx'), may hold values from -0.125 to 0.125
- expert_up: bfloat16 [16, 2048, 1408], P('fsdp', 'ctx'), may hold values from -0.125 to 0.125
- expert_down: bfloat16 [16, 1408, 2048], P('fsdp', 'ctx'), may hold values from -1.75 to 1.75
- out_grad: bfloat16 [16, 256, 2048], P('fsdp', 'ctx'), may hold values from -6 to 6
- seq_length: int32 [16], P('fsdp'), may hold values from 129 to 256, as said below
- expert_ids: int32 [16, 256, 6], P('fsdp', 'ctx'), may hold values from 0 to 15, all different within a row
- fill_order: int32 [16, 1536], P('fsdp', 'ctx'), may hold values from 0 to 1535, each once within a row
Outputs:
- output: bfloat16 [16, 256, 2048], P('fsdp', 'ctx')
- input_grad: bfloat16 [16, 256, 2048], P('fsdp', 'ctx')
- attn_norm_grad: float32 [2048], P(('ctx', 'fsdp'))
- w_query_grad: float32 [2048, 3072], P(('ctx', 'fsdp'))
- w_latent_grad: float32 [2048, 576], P(('ctx', 'fsdp'))
- latent_norm_grad: float32 [512], P(('ctx', 'fsdp'))
- w_expand_grad: float32 [512, 4096], P(('ctx', 'fsdp'))
- w_output_grad: float32 [2048, 2048], P(('ctx', 'fsdp'))
- ffn_norm_grad: float32 [2048], P(('ctx', 'fsdp'))
- w_router_grad: float32 [2048, 16], P(('ctx', 'fsdp'))
- shared_gate_grad: float32 [2048, 2816], P(('ctx', 'fsdp'))
- shared_up_grad: float32 [2048, 2816], P(('ctx', 'fsdp'))
- shared_down_grad: float32 [2816, 2048], P(('ctx', 'fsdp'))
- expert_gate_grad: float32 [16, 2048, 1408], P('fsdp', 'ctx')
- expert_up_grad: float32 [16, 2048, 1408], P('fsdp', 'ctx')
- expert_down_grad: float32 [16, 1408, 2048], P('fsdp', 'ctx')
Inputs may be any that keep to these rules, and one draw needn't show every extreme that they name: `seq_length`: every sequence ends on its last device's block; some sequence uses all 256 positions. `expert_ids`: each token names 6 different experts. `fill_order`: each sequence's entries are all different.
All inputs are finite; a program needn't handle non-finite values.
Results may differ from a plain program's by a relative error of at most 0.02.
Values may be sent and summed in bfloat16 or wider, within the bound.
No kernel may reach another device: no remote copies, remote signals or barrier semaphores. Data moves between devices by JAX's collectives and lax.ppermute only.
A program may use at most 384 MiB of HBM per device.

v0:
```python
import jax
import jax.numpy as jnp
from jax import lax
from jax.sharding import PartitionSpec as P

HEADS = 16
NOPE = 128
ROPE = 64
VDIM = 128
KVR = 512
TOPK = 6


EPSILON = 1e-06
ROPE_BASE = 10000.0
NEGATIVE_FILL = -1e30


def matrix_product(left, right):
    return jnp.dot(left, right, preferred_element_type=jnp.float32)


def rms_norm(values, gain):
    return values * lax.rsqrt(jnp.mean(values * values, axis=-1, keepdims=True) + EPSILON) * gain


def norm_back(values, gain, grad_out):
    inverse = lax.rsqrt(jnp.mean(values * values, axis=-1, keepdims=True) + EPSILON)
    normed = values * inverse
    gain_grad = jnp.sum(grad_out * normed, axis=0)
    scaled = grad_out * gain
    input_grad = inverse * (scaled - normed * jnp.mean(scaled * normed, axis=-1, keepdims=True))
    return (input_grad, gain_grad)


def rope_tables(positions, width):
    half = width // 2
    freqs = ROPE_BASE ** (-jnp.arange(half, dtype=jnp.float32) / half)
    angles = positions.astype(jnp.float32)[:, None] * freqs[None, :]
    return (jnp.cos(angles), jnp.sin(angles))


def rotate(values, cosine, sine):
    half = values.shape[-1] // 2
    first = values[..., :half]
    second = values[..., half:]
    return jnp.concatenate(
        [first * cosine - second * sine, second * cosine + first * sine], axis=-1
    )


def rotate_back(grads, cosine, sine):
    half = grads.shape[-1] // 2
    first = grads[..., :half]
    second = grads[..., half:]
    return jnp.concatenate(
        [first * cosine + second * sine, second * cosine - first * sine], axis=-1
    )


def slot_rank(expert_flat, priority):
    same = (expert_flat[:, None] == expert_flat[None, :]) & (priority[None, :] < priority[:, None])
    return jnp.sum(same.astype(jnp.int32), axis=1)


def swish_gradients(d_act, gate_val, up_val):
    sigma = jax.nn.sigmoid(gate_val)
    d_gate = (d_act * up_val * sigma * (1.0 + gate_val * (1.0 - sigma))).astype(jnp.bfloat16)
    d_up = (d_act * gate_val * sigma).astype(jnp.bfloat16)
    return (d_gate, d_up)


def local(
    tokens,
    attn_norm,
    w_query,
    w_latent,
    latent_norm,
    w_expand,
    w_output,
    ffn_norm,
    w_router,
    shared_gate,
    shared_up,
    shared_down,
    expert_gate,
    expert_up,
    expert_down,
    out_grad,
    seq_length,
    expert_ids,
    fill_order,
):
    input_rows = tokens[0].astype(jnp.float32)
    tok_count = input_rows.shape[0]
    width = input_rows.shape[1]
    n_experts = expert_gate.shape[0] * lax.axis_size("fsdp")
    capacity = tok_count * TOPK // n_experts
    pair_count = tok_count * TOPK
    softmax_scale = (NOPE + ROPE) ** (-0.5)
    positions = lax.axis_index("ctx") * tok_count + jnp.arange(tok_count, dtype=jnp.int32)
    seq_used = seq_length[0]
    valid = (positions < seq_used).astype(jnp.float32)
    cosine, sine = rope_tables(positions, ROPE)
    attention_gain, wq_full, wkva_full, latent_gain, wkvb_full, wo_full = (
        lax.all_gather(attn_norm, ("ctx", "fsdp"), axis=0, tiled=True),
        lax.all_gather(w_query, ("ctx", "fsdp"), axis=0, tiled=True),
        lax.all_gather(w_latent, ("ctx", "fsdp"), axis=0, tiled=True),
        lax.all_gather(latent_norm, ("ctx", "fsdp"), axis=0, tiled=True),
        lax.all_gather(w_expand, ("ctx", "fsdp"), axis=0, tiled=True),
        lax.all_gather(w_output, ("ctx", "fsdp"), axis=0, tiled=True),
    )
    attention_gain = attention_gain.astype(jnp.float32)
    latent_gain = latent_gain.astype(jnp.float32)
    h_attn = rms_norm(input_rows, attention_gain).astype(jnp.bfloat16)
    query_raw = matrix_product(h_attn, wq_full).reshape(tok_count, HEADS, NOPE + ROPE)
    query_rot = jnp.concatenate(
        [
            query_raw[..., :NOPE],
            rotate(query_raw[..., NOPE:], cosine[:, None, :], sine[:, None, :]),
        ],
        axis=-1,
    ).astype(jnp.bfloat16)
    latent_in = matrix_product(h_attn, wkva_full)
    latent_raw = latent_in[:, :KVR]
    latent = rms_norm(latent_raw, latent_gain).astype(jnp.bfloat16)
    key_rope = rotate(latent_in[:, KVR:], cosine, sine).astype(jnp.bfloat16)
    latent_all, rope_all = (
        lax.all_gather(latent, "ctx", axis=0, tiled=True),
        lax.all_gather(key_rope, "ctx", axis=0, tiled=True),
    )
    expand_all = matrix_product(latent_all, wkvb_full).astype(jnp.bfloat16)
    seq_total = expand_all.shape[0]
    expand_heads = jnp.transpose(expand_all.reshape(seq_total, HEADS, NOPE + VDIM), (1, 0, 2))
    nope_heads = expand_heads[..., :NOPE]
    value_heads = expand_heads[..., NOPE:]
    query_heads = jnp.transpose(query_rot, (1, 0, 2))
    key_pos = jnp.arange(seq_total, dtype=jnp.int32)
    allowed = (key_pos[None, :] <= positions[:, None]) & (key_pos[None, :] < seq_used)

    def head_scores(query_h, nope_h):
        keys = jnp.concatenate([nope_h, rope_all], axis=-1)
        scores = matrix_product(query_h, keys.T) * softmax_scale
        return (jnp.where(allowed, scores, NEGATIVE_FILL), keys)

    def head_forward(items):
        query_h, nope_h, value_h = items
        scores, keys = head_scores(query_h, nope_h)
        highest_score = jnp.max(scores, axis=-1, keepdims=True)
        expo = jnp.exp(scores - highest_score)
        total = jnp.sum(expo, axis=-1, keepdims=True)
        probs = (expo / total).astype(jnp.bfloat16)
        attended_h = matrix_product(probs, value_h).astype(jnp.bfloat16)
        return (attended_h, highest_score[:, 0] + jnp.log(total[:, 0]))

    attended_heads, lse_heads = lax.map(head_forward, (query_heads, nope_heads, value_heads))
    attended = jnp.transpose(attended_heads, (1, 0, 2)).reshape(tok_count, HEADS * VDIM)
    middle = input_rows + matrix_product(attended, wo_full)
    feedforward_gain, router_full, sgate_full, sup_full, sdown_full = (
        lax.all_gather(ffn_norm, ("ctx", "fsdp"), axis=0, tiled=True),
        lax.all_gather(w_router, ("ctx", "fsdp"), axis=0, tiled=True),
        lax.all_gather(shared_gate, ("ctx", "fsdp"), axis=0, tiled=True),
        lax.all_gather(shared_up, ("ctx", "fsdp"), axis=0, tiled=True),
        lax.all_gather(shared_down, ("ctx", "fsdp"), axis=0, tiled=True),
    )
    feedforward_gain = feedforward_gain.astype(jnp.float32)
    expert_gate_gathered, expert_up_gathered, expert_down_gathered = (
        lax.all_gather(expert_gate, "ctx", axis=1, tiled=True),
        lax.all_gather(expert_up, "ctx", axis=1, tiled=True),
        lax.all_gather(expert_down, "ctx", axis=1, tiled=True),
    )
    expert_gate_matrix = expert_gate_gathered[0]
    expert_up_matrix = expert_up_gathered[0]
    edown_w = expert_down_gathered[0]
    h_ffn = rms_norm(middle, feedforward_gain).astype(jnp.bfloat16)
    gates = jax.nn.softmax(matrix_product(h_ffn, router_full), axis=-1)
    route_ids = expert_ids[0]
    onehot = (
        route_ids[:, :, None] == jnp.arange(n_experts, dtype=jnp.int32)[None, None, :]
    ).astype(jnp.float32)
    chosen = jnp.einsum("tke,te->tk", onehot, gates, precision=lax.Precision.HIGHEST)
    shared_gate_val = matrix_product(h_ffn, sgate_full)
    shared_up_val = matrix_product(h_ffn, sup_full)
    shared_act = (jax.nn.silu(shared_gate_val) * shared_up_val).astype(jnp.bfloat16)
    shared_out = matrix_product(shared_act, sdown_full)
    flat_ids = route_ids.reshape(pair_count)
    ranks = slot_rank(flat_ids, fill_order[0])
    kept = ranks < capacity
    dest = jnp.where(kept, flat_ids * capacity + ranks, n_experts * capacity)
    pair_token = jnp.arange(pair_count) // TOPK
    slot_total = n_experts * capacity
    send_rows = (
        jnp.zeros((slot_total + 1, width), jnp.bfloat16)
        .at[dest]
        .set(h_ffn[pair_token])[:slot_total]
    )
    received = lax.all_to_all(
        send_rows.reshape(n_experts, capacity, width),
        "fsdp",
        split_axis=0,
        concat_axis=0,
        tiled=True,
    )
    token_rows = received.reshape(-1, width)
    expert_gate_value = matrix_product(token_rows, expert_gate_matrix)
    expert_up_value = matrix_product(token_rows, expert_up_matrix)
    expert_act = (jax.nn.silu(expert_gate_value) * expert_up_value).astype(jnp.bfloat16)
    expert_output = matrix_product(expert_act, edown_w).astype(jnp.bfloat16)
    returned = lax.all_to_all(
        expert_output.reshape(received.shape), "fsdp", split_axis=0, concat_axis=0, tiled=True
    ).reshape(slot_total, width)
    zero_row = jnp.zeros((1, width), jnp.bfloat16)
    pair_out = (
        jnp.concatenate([returned, zero_row], axis=0)[dest]
        .astype(jnp.float32)
        .reshape(tok_count, TOPK, width)
    )
    kept_pairs = kept.reshape(tok_count, TOPK).astype(jnp.float32)
    pair_weight = chosen * kept_pairs
    routed = jnp.einsum("tk,tkd->td", pair_weight, pair_out, precision=lax.Precision.HIGHEST)
    output = (middle + shared_out + routed).astype(jnp.bfloat16)
    grad_y = out_grad[0].astype(jnp.float32) * valid[:, None]
    d_chosen = jnp.sum(pair_out * grad_y[:, None, :], axis=-1) * kept_pairs
    d_gates = jnp.einsum("tk,tke->te", d_chosen, onehot, precision=lax.Precision.HIGHEST)
    d_logits = gates * (d_gates - jnp.sum(gates * d_gates, axis=-1, keepdims=True))
    pair_grad_rows = (
        (pair_weight[:, :, None] * grad_y[:, None, :])
        .reshape(pair_count, width)
        .astype(jnp.bfloat16)
    )
    send_grads = (
        jnp.zeros((slot_total + 1, width), jnp.bfloat16).at[dest].set(pair_grad_rows)[:slot_total]
    )
    grad_rows = lax.all_to_all(
        send_grads.reshape(n_experts, capacity, width),
        "fsdp",
        split_axis=0,
        concat_axis=0,
        tiled=True,
    ).reshape(-1, width)
    d_edown = matrix_product(expert_act.T, grad_rows)
    expert_activation_grad = matrix_product(grad_rows, edown_w.T)
    expert_gate_value_grad, expert_up_value_grad = swish_gradients(
        expert_activation_grad, expert_gate_value, expert_up_value
    )
    d_egate = matrix_product(token_rows.T, expert_gate_value_grad)
    expert_up_weight_grad = matrix_product(token_rows.T, expert_up_value_grad)
    row_gradients = (
        matrix_product(expert_gate_value_grad, expert_gate_matrix.T)
        + matrix_product(expert_up_value_grad, expert_up_matrix.T)
    ).astype(jnp.bfloat16)
    back_rows = lax.all_to_all(
        row_gradients.reshape(received.shape), "fsdp", split_axis=0, concat_axis=0, tiled=True
    ).reshape(slot_total, width)
    d_pairs = (
        jnp.concatenate([back_rows, zero_row], axis=0)[dest]
        .astype(jnp.float32)
        .reshape(tok_count, TOPK, width)
    )
    d_h_ffn = jnp.sum(d_pairs, axis=1)
    expert_gate_weight_gradient, expert_up_weight_gradient, expert_down_weight_gradient = (
        lax.psum_scatter(
            d_egate[None].astype(jnp.bfloat16), "ctx", scatter_dimension=1, tiled=True
        ).astype(jnp.float32),
        lax.psum_scatter(
            expert_up_weight_grad[None].astype(jnp.bfloat16), "ctx", scatter_dimension=1, tiled=True
        ).astype(jnp.float32),
        lax.psum_scatter(
            d_edown[None].astype(jnp.bfloat16), "ctx", scatter_dimension=1, tiled=True
        ).astype(jnp.float32),
    )
    d_shared_out = grad_y.astype(jnp.bfloat16)
    d_sdown = matrix_product(shared_act.T, d_shared_out)
    d_shared_act = matrix_product(d_shared_out, sdown_full.T)
    d_sgate_val, d_sup_val = swish_gradients(d_shared_act, shared_gate_val, shared_up_val)
    d_sgate = matrix_product(h_ffn.T, d_sgate_val)
    d_sup = matrix_product(h_ffn.T, d_sup_val)
    d_h_ffn = (
        d_h_ffn + matrix_product(d_sgate_val, sgate_full.T) + matrix_product(d_sup_val, sup_full.T)
    )
    d_router = jnp.dot(h_ffn.astype(jnp.float32).T, d_logits, precision=lax.Precision.HIGHEST)
    d_h_ffn = d_h_ffn + jnp.dot(
        d_logits, router_full.astype(jnp.float32).T, precision=lax.Precision.HIGHEST
    )
    d_mid_norm, d_g_ffn = norm_back(middle, feedforward_gain, d_h_ffn)
    grad_mid = grad_y + d_mid_norm
    gffn_grad, router_grad, sgate_grad, sup_grad, sdown_grad = (
        lax.psum_scatter(d_g_ffn, ("ctx", "fsdp"), scatter_dimension=0, tiled=True),
        lax.psum_scatter(d_router, ("ctx", "fsdp"), scatter_dimension=0, tiled=True),
        lax.psum_scatter(d_sgate, ("ctx", "fsdp"), scatter_dimension=0, tiled=True),
        lax.psum_scatter(d_sup, ("ctx", "fsdp"), scatter_dimension=0, tiled=True),
        lax.psum_scatter(d_sdown, ("ctx", "fsdp"), scatter_dimension=0, tiled=True),
    )
    d_attn_out = grad_mid.astype(jnp.bfloat16)
    d_wo = matrix_product(attended.T, d_attn_out)
    d_attended = matrix_product(d_attn_out, wo_full.T).astype(jnp.bfloat16)
    d_attended_heads = jnp.transpose(d_attended.reshape(tok_count, HEADS, VDIM), (1, 0, 2))

    def head_backward(items):
        query_h, nope_h, value_h, dout_h, lse_h = items
        scores, keys = head_scores(query_h, nope_h)
        probs = jnp.exp(scores - lse_h[:, None])
        d_value = matrix_product(probs.astype(jnp.bfloat16).T, dout_h)
        d_probs = matrix_product(dout_h, value_h.T)
        delta = jnp.sum(probs * d_probs, axis=-1, keepdims=True)
        d_scores = (probs * (d_probs - delta)).astype(jnp.bfloat16)
        d_query = matrix_product(d_scores, keys) * softmax_scale
        d_keys = matrix_product(d_scores.T, query_h) * softmax_scale
        return (d_query, d_keys[:, :NOPE], d_keys[:, NOPE:], d_value)

    d_query_heads, d_nope_heads, d_rope_heads, d_value_heads = lax.map(
        head_backward, (query_heads, nope_heads, value_heads, d_attended_heads, lse_heads)
    )
    d_expand_part = (
        jnp.transpose(jnp.concatenate([d_nope_heads, d_value_heads], axis=-1), (1, 0, 2))
        .reshape(seq_total, HEADS * (NOPE + VDIM))
        .astype(jnp.bfloat16)
    )
    d_rope_all = jnp.sum(d_rope_heads, axis=0)
    d_wkvb = matrix_product(latent_all.T, d_expand_part)
    d_latent_part = matrix_product(d_expand_part, wkvb_full.T)
    d_latent, d_rope = (
        lax.psum_scatter(
            d_latent_part.astype(jnp.bfloat16), "ctx", scatter_dimension=0, tiled=True
        ).astype(jnp.float32),
        lax.psum_scatter(
            d_rope_all.astype(jnp.bfloat16), "ctx", scatter_dimension=0, tiled=True
        ).astype(jnp.float32),
    )
    d_latent_raw, d_g_latent = norm_back(latent_raw, latent_gain, d_latent)
    d_rope_raw = rotate_back(d_rope, cosine, sine)
    d_latent_in = jnp.concatenate([d_latent_raw, d_rope_raw], axis=-1).astype(jnp.bfloat16)
    d_wkva = matrix_product(h_attn.T, d_latent_in)
    d_h_attn = matrix_product(d_latent_in, wkva_full.T)
    d_query = jnp.transpose(d_query_heads, (1, 0, 2))
    d_query_raw = jnp.concatenate(
        [
            d_query[..., :NOPE],
            rotate_back(d_query[..., NOPE:], cosine[:, None, :], sine[:, None, :]),
        ],
        axis=-1,
    )
    d_query_low = d_query_raw.reshape(tok_count, HEADS * (NOPE + ROPE)).astype(jnp.bfloat16)
    d_wq = matrix_product(h_attn.T, d_query_low)
    d_h_attn = d_h_attn + matrix_product(d_query_low, wq_full.T)
    d_in_norm, d_g_attn = norm_back(input_rows, attention_gain, d_h_attn)
    input_grad = (grad_mid + d_in_norm).astype(jnp.bfloat16)
    gattn_grad, wq_grad, wkva_grad, glatent_grad, wkvb_grad, wo_grad = (
        lax.psum_scatter(d_g_attn, ("ctx", "fsdp"), scatter_dimension=0, tiled=True),
        lax.psum_scatter(d_wq, ("ctx", "fsdp"), scatter_dimension=0, tiled=True),
        lax.psum_scatter(d_wkva, ("ctx", "fsdp"), scatter_dimension=0, tiled=True),
        lax.psum_scatter(d_g_latent, ("ctx", "fsdp"), scatter_dimension=0, tiled=True),
        lax.psum_scatter(d_wkvb, ("ctx", "fsdp"), scatter_dimension=0, tiled=True),
        lax.psum_scatter(d_wo, ("ctx", "fsdp"), scatter_dimension=0, tiled=True),
    )
    return (
        output[None],
        input_grad[None],
        gattn_grad,
        wq_grad,
        wkva_grad,
        glatent_grad,
        wkvb_grad,
        wo_grad,
        gffn_grad,
        router_grad,
        sgate_grad,
        sup_grad,
        sdown_grad,
        expert_gate_weight_gradient,
        expert_up_weight_gradient,
        expert_down_weight_gradient,
    )


def solution(mesh):
    in_specs = (
        P("fsdp", "ctx", None),
        P(("ctx", "fsdp")),
        P(("ctx", "fsdp"), None),
        P(("ctx", "fsdp"), None),
        P(("ctx", "fsdp")),
        P(("ctx", "fsdp"), None),
        P(("ctx", "fsdp"), None),
        P(("ctx", "fsdp")),
        P(("ctx", "fsdp"), None),
        P(("ctx", "fsdp"), None),
        P(("ctx", "fsdp"), None),
        P(("ctx", "fsdp"), None),
        P("fsdp", "ctx", None),
        P("fsdp", "ctx", None),
        P("fsdp", "ctx", None),
        P("fsdp", "ctx", None),
        P("fsdp"),
        P("fsdp", "ctx", None),
        P("fsdp", "ctx"),
    )
    out_specs = (
        P("fsdp", "ctx", None),
        P("fsdp", "ctx", None),
        P(("ctx", "fsdp")),
        P(("ctx", "fsdp"), None),
        P(("ctx", "fsdp"), None),
        P(("ctx", "fsdp")),
        P(("ctx", "fsdp"), None),
        P(("ctx", "fsdp"), None),
        P(("ctx", "fsdp")),
        P(("ctx", "fsdp"), None),
        P(("ctx", "fsdp"), None),
        P(("ctx", "fsdp"), None),
        P(("ctx", "fsdp"), None),
        P("fsdp", "ctx", None),
        P("fsdp", "ctx", None),
        P("fsdp", "ctx", None),
    )
    return jax.shard_map(local, mesh=mesh, in_specs=in_specs, out_specs=out_specs, check_vma=False)
```

profile of v0, /device:TPU:1, one launch (start us, length us, event | category | flops | bytes accessed | tf_op | source)
XLA Modules:
  0.0 2979.7 jit_solution(18068733911754037854)
XLA Ops:
  15.0 40.8 %all-reduce.9 = (bf16[2048]{0:T(1024)(128)(2,1)S(1)}, bf16[512]{0:T(512)(128)(2,1)S(1)}, bf16[2048]{0:T(1024)(128)(2,1)S(1)}) all-reduce(bf16[2048]{0:T(1024)(128)(2,1)S(1)} %dynamic-update-slice, bf16[512]{0:T(512)(128)(2,1)S(1)} %dynamic-update-slice.1, ...), channel_id=1, replica_groups=mesh['ctx'=2,'fsdp'=16] {'ctx','fsdp'}, use_global_device_ids=true, to_apply=%add.2 | all-reduce | flops 4608 | bytes 18432
  57.8 41.9 %all-gather = bf16[32,64,16]{1,2,0:T(8,128)(2,1)S(1)} all-gather(bf16[1,64,16]{1,2,0:T(8,128)(2,1)S(1)} %bitcast.318), channel_id=1, replica_groups=mesh['ctx'=2,'fsdp'=16] {'ctx','fsdp'}, dimensions={0}, use_global_device_ids=true | all-gather | bytes 67584 | tf_op jit(solution)/shard_map/all_gather | solution.py:161
  143.0 92.3 %all-gather.12.cloned.1.call-done = bf16[2048,3072]{1,0:T(8,128)(2,1)} async-done(((bf16[64,3072]{1,0:T(8,128)(2,1)}), bf16[2048,3072]{1,0:T(8,128)(2,1)}) %all-gather.12.cloned.1.call-update) | async-done | bytes 12582928 | tf_op jit(solution)/shard_map/all_gather | solution.py:107
  235.3 17.0 copy.76
  260.5 62.2 %while.30 = (s32[]{:T(128)}, bf16[16,128,128]{1,2,0:T(8,128)(2,1)S(1)}, f32[16,128]{1,0:T(8,128)}, bf16[16,128,192]{2,1,0:T(8,128)(2,1)}, bf16[16,256,128]{2,1,0...) while((s32[]{:T(128)}, ...), condition=%wide.region_5.6_spmd.clone, body=%wide.region_2.5_spmd.clone.sunk | while | flops 21512064 | bytes 924793 | solution.py:156
  331.2 14.0 scatter_custom_fusion.1
  354.8 22.5 scatter_custom_fusion
  381.2 32.3 %all-to-all-done.2 = bf16[16,48,2048]{2,1,0:T(8,128)(2,1)} async-done(((bf16[16,48,2048]{2,1,0:T(8,128)(2,1)}), bf16[16,48,2048]{2,1,0:T(8,128)(2,1)}, u32[]{:S(2)}, u32[]{:S(2)}) %all-to-all-start.2) | async-done | bytes 3145760 | tf_op jit(solution)/shard_map/all_to_all | solution.py:234
  413.6 15.1 all-to-all-start
  438.4 25.6 all-gather.28.cloned.1.call-done
  463.9 24.5 all-to-all-done
  498.1 41.9 %all-gather.26.cloned.1.call-done = bf16[1,2048,1408]{2,1,0:T(8,128)(2,1)} async-done(((bf16[1,1024,1408]{2,1,0:T(8,128)(2,1)}), bf16[1,2048,1408]{2,1,0:T(8,128)(2,1)}) %all-gather.26.cloned.1.call-update) | async-done | bytes 5767184 | tf_op jit(solution)/shard_map/all_gather | solution.py:168
  540.0 13.0 multiply_convert_fusion.3
  586.7 83.2 %all-to-all-done.1 = bf16[16,48,2048]{2,1,0:T(8,128)(2,1)} async-done(((bf16[16,48,2048]{2,1,0:T(8,128)(2,1)}), bf16[16,48,2048]{2,1,0:T(8,128)(2,1)}, u32[]{:S(2)}, u32[]{:S(2)}) %all-to-all-start.1) | async-done | bytes 3145760 | tf_op jit(solution)/shard_map/all_to_all | solution.py:209
  669.9 20.7 all-to-all-start.3
  696.9 122.7 %all-gather.22.cloned.1.call-done = bf16[2048,2816]{1,0:T(8,128)(2,1)} async-done(((bf16[64,2816]{1,0:T(8,128)(2,1)}), bf16[2048,2816]{1,0:T(8,128)(2,1)}) %all-gather.22.cloned.1.call-update) | async-done | bytes 11534352 | tf_op jit(solution)/shard_map/all_gather | solution.py:163
  826.7 85.6 %all-gather.24.cloned.1.call-done = bf16[2816,2048]{1,0:T(8,128)(2,1)} async-done(((bf16[88,2048]{1,0:T(8,128)(2,1)}), bf16[2816,2048]{1,0:T(8,128)(2,1)}) %all-gather.24.cloned.1.call-update) | async-done | bytes 11534352 | tf_op jit(solution)/shard_map/all_gather | solution.py:164
  979.8 126.1 %while.31 = (s32[]{:T(128)}, f32[16,128,192]{1,2,0:T(8,128)}, bf16[16,256,128]{1,2,0:T(8,128)(2,1)}, f32[16,256,64]{1,2,0:T(8,128)}, bf16[16,256,128]{1,2,0:T(8,...) while((s32[]{:T(128)}, f32[16,128,192]{1,2,0:T(8,128)}, ...), condition=%wide.region_18.19_spmd.clone, body=%wide.region_16.18_spmd.clone.sunk | while | flops 55353216 | bytes 2269069 | solution.py:311
  1182.5 10.6 fusion.159
  1204.7 10.6 fusion.108
  1239.3 23.0 reduce-scatter.44.cloned.1.call-done
  1266.9 43.2 %all-reduce.8 = (f32[2048]{0:T(1024)S(1)}, f32[512]{0:T(512)S(1)}, f32[2048]{0:T(1024)S(1)}) all-reduce(f32[2048]{0:T(1024)S(1)} %get-tuple-element.272, f32[512]{0:T(512)S(1)} %get-tuple-element.274, f32[2048]{0:T(1024)S(1)} %get-tuple-element.270), channel_id=4, replica_groups=mesh['ctx'=2,'fsdp'=16] {'ctx','fsdp'}, use_global_device_ids=true, to_apply=%region_25.26.clone | all-reduce | flops 4608 | bytes 36864
  1313.0 26.6 reduce-scatter.38.cloned.1.call-done
  1344.7 68.8 %reduce-scatter.34.cloned.1.call-done = bf16[1,1024,1408]{2,1,0:T(8,128)(2,1)} async-done(((bf16[1,2048,1408]{2,1,0:T(8,128)(2,1)}), bf16[1,1024,1408]{2,1,0:T(8,128)(2,1)}) %reduce-scatter.34.cloned.1.call-update) | async-done | bytes 2883600 | tf_op jit(solution)/shard_map/reduce_scatter | solution.py:262
  1418.2 68.9 %reduce-scatter.36.cloned.1.call-done = bf16[1,1024,1408]{2,1,0:T(8,128)(2,1)} async-done(((bf16[1,2048,1408]{2,1,0:T(8,128)(2,1)}), bf16[1,1024,1408]{2,1,0:T(8,128)(2,1)}) %reduce-scatter.36.cloned.1.call-update) | async-done | bytes 2883600 | tf_op jit(solution)/shard_map/reduce_scatter | solution.py:265
  1491.8 135.7 %reduce-scatter.22.cloned.1.call-done = f32[64,576]{1,0:T(8,128)} async-done(((f32[2048,576]{1,0:T(8,128)}), f32[64,576]{1,0:T(8,128)}) %reduce-scatter.22.cloned.1.call-update) | async-done | bytes 147472 | tf_op jit(solution)/shard_map/reduce_scatter | solution.py:351
  1627.5 148.4 %reduce-scatter.24.cloned.1.call-done = f32[16,4096]{1,0:T(8,128)} async-done(((f32[512,4096]{1,0:T(8,128)}), f32[16,4096]{1,0:T(8,128)}) %reduce-scatter.24.cloned.1.call-update) | async-done | bytes 262160 | tf_op jit(solution)/shard_map/reduce_scatter | solution.py:353
  1775.9 188.7 %reduce-scatter.26.cloned.1.call-done = f32[64,2048]{1,0:T(8,128)} async-done(((f32[2048,2048]{1,0:T(8,128)}), f32[64,2048]{1,0:T(8,128)}) %reduce-scatter.26.cloned.1.call-update) | async-done | bytes 524304 | tf_op jit(solution)/shard_map/reduce_scatter | solution.py:354
  1964.6 253.4 %reduce-scatter.20.cloned.1.call-done = f32[64,3072]{1,0:T(8,128)} async-done(((f32[2048,3072]{1,0:T(8,128)}), f32[64,3072]{1,0:T(8,128)}) %reduce-scatter.20.cloned.1.call-update) | async-done | bytes 786448 | tf_op jit(solution)/shard_map/reduce_scatter | solution.py:350
  2218.0 251.7 %reduce-scatter.28.cloned.1.call-done = f32[64,2816]{1,0:T(8,128)} async-done(((f32[2048,2816]{1,0:T(8,128)}), f32[64,2816]{1,0:T(8,128)}) %reduce-scatter.28.cloned.1.call-update) | async-done | bytes 720912 | tf_op jit(solution)/shard_map/reduce_scatter | solution.py:290
  2469.6 251.5 %reduce-scatter.30.cloned.1.call-done = f32[64,2816]{1,0:T(8,128)} async-done(((f32[2048,2816]{1,0:T(8,128)}), f32[64,2816]{1,0:T(8,128)}) %reduce-scatter.30.cloned.1.call-update) | async-done | bytes 720912 | tf_op jit(solution)/shard_map/reduce_scatter | solution.py:291
  2721.2 251.5 %reduce-scatter.32.cloned.1.call-done = f32[88,2048]{1,0:T(8,128)} async-done(((f32[2816,2048]{1,0:T(8,128)}), f32[88,2048]{1,0:T(8,128)}) %reduce-scatter.32.cloned.1.call-update) | async-done | bytes 720912 | tf_op jit(solution)/shard_map/reduce_scatter | solution.py:292
  (605 shorter events, 536.7 us)
Async XLA Ops:
  7.2 108.3 %all-gather.14.cloned.1.call-start = ((), (), s32[]{:S(2)}) async-start(), calls=%async_computation.18 | async-start | bytes 2703360 | tf_op jit(solution)/shard_map/all_gather | solution.py:108
  7.9 129.9 %all-gather.16.cloned.1.call-start = ((), (), s32[]{:S(2)}) async-start(), calls=%async_computation.19 | async-start | bytes 4325376 | tf_op jit(solution)/shard_map/all_gather | solution.py:110
  8.7 226.6 %all-gather.12.cloned.1.call-start = ((), (), s32[]{:S(2)}) async-start(), calls=%async_computation.17 | async-start | bytes 12976128 | tf_op jit(solution)/shard_map/all_gather | solution.py:107
  9.4 313.4 %all-gather.18.cloned.1.call-start = ((), (), s32[]{:S(2)}) async-start(), calls=%async_computation.20 | async-start | bytes 8650752 | tf_op jit(solution)/shard_map/all_gather | solution.py:111
  10.0 418.6 %all-gather.30.cloned.1.call-start = ((), (), s32[]{:S(2)}) async-start(), calls=%async_computation.26 | async-start | bytes 8650752 | tf_op jit(solution)/shard_map/all_gather | solution.py:170
  10.6 453.3 %all-gather.28.cloned.1.call-start = ((), (), s32[]{:S(2)}) async-start(), calls=%async_computation.25 | async-start | bytes 8650752 | tf_op jit(solution)/shard_map/all_gather | solution.py:169
  11.2 528.8 %all-gather.26.cloned.1.call-start = ((), (), s32[]{:S(2)}) async-start(), calls=%async_computation.24 | async-start | bytes 8650752 | tf_op jit(solution)/shard_map/all_gather | solution.py:168
  12.0 679.0 %all-gather.20.cloned.1.call-start = ((), (), s32[]{:S(2)}) async-start(), calls=%async_computation.21 | async-start | bytes 11894784 | tf_op jit(solution)/shard_map/all_gather | solution.py:162
  12.7 806.9 %all-gather.22.cloned.1.call-start = ((), (), s32[]{:S(2)}) async-start(), calls=%async_computation.22 | async-start | bytes 11894784 | tf_op jit(solution)/shard_map/all_gather | solution.py:163
  55.8 196.5 %copy-start.25 = (f32[2048]{0:T(1024)}, f32[2048]{0:T(1024)S(1)}, u32[]{:S(2)}) copy-start(f32[2048]{0:T(1024)S(1)} %convert_element_type.202) | copy-start | bytes 24580
  56.0 196.3 %copy-start.38 = (f32[128]{0:T(128)}, f32[128]{0:T(128)S(1)}, u32[]{:S(2)}) copy-start(f32[128]{0:T(128)S(1)} %add_rsqrt_fusion.2) | copy-start | bytes 1540
  119.6 139.5 %copy-start.34 = (f32[128,32]{0,1:T(8,128)}, f32[128,32]{0,1:T(8,128)S(1)}, u32[]{:S(2)}) copy-start(f32[128,32]{0,1:T(8,128)S(1)} %get-tuple-element.347) | copy-start | bytes 49156
  330.0 489.6 %copy-start.2 = (bf16[128,2048]{1,0:T(8,128)(2,1)}, bf16[128,2048]{1,0:T(8,128)(2,1)S(1)}, u32[]{:S(2)}) copy-start(bf16[128,2048]{1,0:T(8,128)(2,1)S(1)} %multiply_convert_fusion.9) | copy-start | bytes 1572868
  349.2 64.4 %all-to-all-start.2 = ((bf16[16,48,2048]{2,1,0:T(8,128)(2,1)}), bf16[16,48,2048]{2,1,0:T(8,128)(2,1)}, u32[]{:S(2)}, u32[]{:S(2)}) async-start(bf16[16,48,2048]{2,1,0:T(8,128)(2,1)} %bitcast.298), calls=%async_computation.2 | async-start | bytes 6291456 | tf_op jit(solution)/shard_map/all_to_all | solution.py:234
  353.7 558.6 %all-gather.24.cloned.1.call-start = ((), (), s32[]{:S(2)}) async-start(), calls=%async_computation.23 | async-start | bytes 11894784 | tf_op jit(solution)/shard_map/all_gather | solution.py:164
  413.6 74.9 %all-to-all-start = ((bf16[16,48,2048]{2,1,0:T(8,128)(2,1)}), bf16[16,48,2048]{2,1,0:T(8,128)(2,1)}, u32[]{:S(2)}, u32[]{:S(2)}) async-start(bf16[16,48,2048]{2,1,0:T(8,128)(2,1)} %bitcast.299), calls=%async_computation | async-start | bytes 6291456 | tf_op jit(solution)/shard_map/all_to_all | solution.py:197
  563.0 106.9 %all-to-all-start.1 = ((bf16[16,48,2048]{2,1,0:T(8,128)(2,1)}), bf16[16,48,2048]{2,1,0:T(8,128)(2,1)}, u32[]{:S(2)}, u32[]{:S(2)}) async-start(bf16[16,48,2048]{2,1,0:T(8,128)(2,1)} %bitcast.309), calls=%async_computation.1 | async-start | bytes 6291456 | tf_op jit(solution)/shard_map/all_to_all | solution.py:209
  669.9 269.5 %all-to-all-start.3 = ((bf16[16,48,2048]{2,1,0:T(8,128)(2,1)}), bf16[16,48,2048]{2,1,0:T(8,128)(2,1)}, u32[]{:S(2)}, u32[]{:S(2)}) async-start(bf16[16,48,2048]{2,1,0:T(8,128)(2,1)} %bitcast.308), calls=%async_computation.3 | async-start | bytes 6291456 | tf_op jit(solution)/shard_map/all_to_all | solution.py:252
  690.6 452.6 %reduce-scatter.42.cloned.1.call-start = ((), (), s32[]{:S(2)}) async-start(), calls=%async_computation.38 | async-start | bytes 98304
  696.9 215.4 %copy-start.45 = (f32[128]{0:T(128)S(1)}, f32[128]{0:T(128)}, u32[]{:S(2)}) copy-start(f32[128]{0:T(128)} %copy-done.44) | copy-start | bytes 1540
  1107.9 36.5 %reduce-scatter.40.cloned.1.call-start = ((), (), s32[]{:S(2)}) async-start(), calls=%async_computation.37 | async-start | bytes 393216
  1113.2 149.1 %reduce-scatter.44.cloned.1.call-start = ((), (), s32[]{:S(2)}) async-start(), calls=%async_computation.39 | async-start | bytes 1081344
  1115.1 224.5 %reduce-scatter.38.cloned.1.call-start = ((), (), s32[]{:S(2)}) async-start(), calls=%async_computation.36 | async-start | bytes 8650752 | tf_op jit(solution)/shard_map/reduce_scatter | solution.py:268
  1125.0 288.5 %reduce-scatter.34.cloned.1.call-start = ((), (), s32[]{:S(2)}) async-start(), calls=%async_computation.34 | async-start | bytes 8650752 | tf_op jit(solution)/shard_map/reduce_scatter | solution.py:262
  1134.0 353.0 %reduce-scatter.36.cloned.1.call-start = ((), (), s32[]{:S(2)}) async-start(), calls=%async_computation.35 | async-start | bytes 8650752 | tf_op jit(solution)/shard_map/reduce_scatter | solution.py:265
  1143.2 484.3 %reduce-scatter.22.cloned.1.call-start = ((), (), s32[]{:S(2)}) async-start(), calls=%async_computation.28 | async-start | bytes 5406720 | tf_op jit(solution)/shard_map/reduce_scatter | solution.py:351
  1152.2 623.7 %reduce-scatter.24.cloned.1.call-start = ((), (), s32[]{:S(2)}) async-start(), calls=%async_computation.29 | async-start | bytes 8650752 | tf_op jit(solution)/shard_map/reduce_scatter | solution.py:353
  1159.3 805.3 %reduce-scatter.26.cloned.1.call-start = ((), (), s32[]{:S(2)}) async-start(), calls=%async_computation.30 | async-start | bytes 17301504 | tf_op jit(solution)/shard_map/reduce_scatter | solution.py:354
  1168.6 1049.3 %reduce-scatter.20.cloned.1.call-start = ((), (), s32[]{:S(2)}) async-start(), calls=%async_computation.27 | async-start | bytes 25952256 | tf_op jit(solution)/shard_map/reduce_scatter | solution.py:350
  1182.5 1287.1 %reduce-scatter.28.cloned.1.call-start = ((), (), s32[]{:S(2)}) async-start(), calls=%async_computation.31 | async-start | bytes 23789568 | tf_op jit(solution)/shard_map/reduce_scatter | solution.py:290
  1193.1 1528.0 %reduce-scatter.30.cloned.1.call-start = ((), (), s32[]{:S(2)}) async-start(), calls=%async_computation.32 | async-start | bytes 23789568 | tf_op jit(solution)/shard_map/reduce_scatter | solution.py:291
  1203.7 1769.1 %reduce-scatter.32.cloned.1.call-start = ((), (), s32[]{:S(2)}) async-start(), calls=%async_computation.33 | async-start | bytes 23789568 | tf_op jit(solution)/shard_map/reduce_scatter | solution.py:292
  (59 other events, 1027.9 us)
Sparse Core Ops, SparseCore 0:
  10.9 60.4 all-gather.13
  74.3 63.4 all-gather.15
  140.7 94.6 all-gather.11
  238.0 75.8 all-gather.17
  315.3 72.7 all-gather.29
  389.4 74.4 all-gather.27
  465.5 74.4 all-gather.25
  542.8 137.8 all-gather.19
  683.7 135.9 all-gather.21
  822.3 89.9 all-gather.23
  1108.0 7.3 reduce-scatter.41
  1118.1 12.1 reduce-scatter.39
  1132.6 129.6 reduce-scatter.43
  1265.0 74.5 reduce-scatter.37
  1342.4 71.0 reduce-scatter.33
  1415.7 71.3 reduce-scatter.35
  1489.9 137.5 reduce-scatter.21
  1630.3 145.5 reduce-scatter.23
  1778.8 185.7 reduce-scatter.25
  1972.6 245.3 reduce-scatter.19
  2220.9 248.7 reduce-scatter.27
  2472.5 248.6 reduce-scatter.29
  2724.0 248.6 reduce-scatter.31
where the time goes:
time: 2990 us; the launch traced here: 2980 us
  waiting for transfers between devices  2190 us (73%)
  matrix products  357 us (12%)
  local copies, waits for them, and re-layouts  175 us (6%)
  blocking collectives  135 us (5%)
  other arithmetic  55.3 us (2%)
  starting transfers between devices  48.2 us (2%)
    dot_general x143, matrix products, matrix_product(): return jnp.dot(left, right, preferred_element_type=jnp.float32)  348 us
    reduce_scatter x1, waiting for transfers between devices, local(): lax.psum_scatter(d_wq, ('ctx', 'fsdp'), scatter_dimension=0, tiled=True)  253 us
    reduce_scatter x1, waiting for transfers between devices, local(): lax.psum_scatter(d_sgate, ('ctx', 'fsdp'), scatter_dimension=0, tiled=True)  252 us
    reduce_scatter x1, waiting for transfers between devices, local(): lax.psum_scatter(d_sdown, ('ctx', 'fsdp'), scatter_dimension=0, tiled=True)  252 us
    reduce_scatter x1, waiting for transfers between devices, local(): lax.psum_scatter(d_sup, ('ctx', 'fsdp'), scatter_dimension=0, tiled=True)  252 us
    reduce_scatter x1, waiting for transfers between devices, local(): lax.psum_scatter(d_wo, ('ctx', 'fsdp'), scatter_dimension=0, tiled=True)  189 us
    reduce_scatter x1, waiting for transfers between devices, local(): lax.psum_scatter(d_wkvb, ('ctx', 'fsdp'), scatter_dimension=0, tiled=True)  148 us
    reduce_scatter x1, waiting for transfers between devices, local(): lax.psum_scatter(d_wkva, ('ctx', 'fsdp'), scatter_dimension=0, tiled=True)  136 us
  transfers between devices with their start and end apart: 27, of which 20 were waited for; matrix products, arithmetic and copies ran while one was open for 14% of the time, Pallas kernels for 0%

commit v1 on v0

--- a/solution.py
+++ b/solution.py
@@ -1,6 +1,9 @@
 import jax
 import jax.numpy as jnp
 from jax import lax
+from jax.experimental import pallas as pl
+from jax.experimental.pallas import tpu as pltpu
+from jax.sharding import Mesh
 from jax.sharding import PartitionSpec as P
 
 HEADS = 16
@@ -70,7 +73,7 @@
     return (d_gate, d_up)
 
 
-def local(
+def local_weights(
     tokens,
     attn_norm,
     w_query,
@@ -373,7 +376,607 @@
     )
 
 
-def solution(mesh):
+ALL = ("y", "z", "x", "c")
+PLANE = ("y", "x", "c")
+FSDP = ("z", "x", "c")
+BF = jnp.bfloat16
+F32 = jnp.float32
+PAIRS = 8
+SEQ_BLOCKS = 2
+
+
+def swap(value, axis):
+    return lax.ppermute(value, axis, [(0, 1), (1, 0)])
+
+
+def swap_zq(value):
+    pairs = [(z * 4 + q, q * 4 + z) for z in range(4) for q in range(4)]
+    return lax.ppermute(value, FSDP, pairs)
+
+
+def spread(value, axes):
+    return lax.all_to_all(value, axes, split_axis=0, concat_axis=0, tiled=True)
+
+
+def gather_z(value):
+    return spread(jnp.broadcast_to(value[None], (4,) + value.shape), "z")
+
+
+def plane_gather(block):
+    half = block.shape[0] // 2
+    by_x = swap(block, "x")
+    by_y = swap(block, "y")
+    diag_x = swap(by_y[:half], "x")
+    diag_y = swap(by_x[half:], "y")
+    near = jnp.concatenate([block, by_x, by_y, diag_x, diag_y], axis=0)
+    far = swap(near, "c")
+    return jnp.concatenate([near, far], axis=0)
+
+
+def plane_reduce(part):
+    rows = part.shape[0] // 8
+    half = rows // 2
+    got = swap(part[4 * rows :], "c")
+    total = part[: 4 * rows].astype(F32) + got.astype(F32)
+    own = total[:rows]
+    to_x = total[rows : 2 * rows]
+    to_y = total[2 * rows : 3 * rows]
+    diag = total[3 * rows :].astype(BF)
+    got_x = swap(diag[:half], "x").astype(F32)
+    got_y = swap(diag[half:], "y").astype(F32)
+    to_y = jnp.concatenate([to_y[:half] + got_x, to_y[half:]], axis=0).astype(BF)
+    to_x = jnp.concatenate([to_x[:half], to_x[half:] + got_y], axis=0).astype(BF)
+    return own + swap(to_x, "x").astype(F32) + swap(to_y, "y").astype(F32)
+
+
+def dot_nt(left, right):
+    return lax.dot_general(left, right, (((1,), (1,)), ((), ())), preferred_element_type=F32)
+
+
+def dot_tn(left, right):
+    return lax.dot_general(left, right, (((0,), (0,)), ((), ())), preferred_element_type=F32)
+
+
+def attention_probs(meta, seq, query, expand, rope_ref, head):
+    count = query.shape[0]
+    half = count // 2
+    keys = jnp.concatenate(
+        [expand[:, 256 * head : 256 * head + 128], rope_ref[0, :, head].reshape(count, 128)], axis=1
+    )
+    rows = lax.broadcasted_iota(jnp.int32, (count, count), 0)
+    cols = lax.broadcasted_iota(jnp.int32, (count, count), 1)
+    own = meta[4]
+    row_pos = jnp.where(rows < half, rows + own * half, rows - half + (1 - own) * half)
+    col_pos = jnp.where(cols < half, cols + own * half, cols - half + (1 - own) * half)
+    allowed = (col_pos <= row_pos) & (col_pos < meta[seq])
+    queries = jnp.concatenate(
+        [query[:, 128 * head : 128 * head + 128], query[:, 256:384]], axis=1
+    )
+    scores = dot_nt(queries, keys) * (NOPE + ROPE) ** (-0.5)
+    scores = jnp.where(allowed, scores, NEGATIVE_FILL)
+    expo = jnp.exp(scores - jnp.max(scores, axis=-1, keepdims=True))
+    probs = expo / jnp.sum(expo, axis=-1, keepdims=True)
+    return probs, queries, keys
+
+
+def attend_kernel(meta, query_ref, expand_ref, rope_ref, out_ref):
+    seq = pl.program_id(0) * 2 + pl.program_id(1)
+    half = query_ref.shape[2]
+    query = query_ref[0].reshape(2 * half, 384)
+    expand = expand_ref[0].reshape(2 * half, 512)
+    for head in range(2):
+        probs, _, _ = attention_probs(meta, seq, query, expand, rope_ref, head)
+        values = expand[:, 256 * head + 128 : 256 * head + 256]
+        attended = jnp.dot(probs.astype(BF), values, preferred_element_type=F32).astype(BF)
+        out_ref[0, :, :, 128 * head : 128 * head + 128] = attended.reshape(2, half, 128)
+
+
+def attend_back_kernel(
+    meta, query_ref, expand_ref, rope_ref, dout_ref, cos_ref, sin_ref, dq_ref, dkv_ref, dkr_ref
+):
+    seq = pl.program_id(0) * 2 + pl.program_id(1)
+    half = query_ref.shape[2]
+    count = 2 * half
+    scale = (NOPE + ROPE) ** (-0.5)
+    query = query_ref[0].reshape(count, 384)
+    expand = expand_ref[0].reshape(count, 512)
+    dout = dout_ref[0].reshape(count, 256)
+    cosine = cos_ref[0].reshape(count, 128)
+    sine = sin_ref[0].reshape(count, 128)
+    lane = lax.broadcasted_iota(jnp.int32, (count, 128), 1)
+    first = (lane % 64) < 32
+    dq_rope = jnp.zeros((count, 128), F32)
+    dk_rope = jnp.zeros((count, 128), F32)
+    for head in range(2):
+        probs, queries, keys = attention_probs(meta, seq, query, expand, rope_ref, head)
+        values = expand[:, 256 * head + 128 : 256 * head + 256]
+        dout_h = dout[:, 128 * head : 128 * head + 128]
+        d_value = dot_tn(probs.astype(BF), dout_h)
+        d_probs = dot_nt(dout_h, values)
+        delta = jnp.sum(probs * d_probs, axis=-1, keepdims=True)
+        d_scores = (probs * (d_probs - delta)).astype(BF)
+        d_query = jnp.dot(d_scores, keys, preferred_element_type=F32) * scale
+        d_keys = dot_tn(d_scores, queries) * scale
+        dq_ref[0, :, :, 128 * head : 128 * head + 128] = (
+            d_query[:, :128].astype(BF).reshape(2, half, 128)
+        )
+        dq_rope = dq_rope + d_query[:, 128:]
+        dk_rope = dk_rope + jnp.where(first == (head == 0), d_keys[:, 128:], 0.0)
+        dkv_ref[0, :, :, 256 * head : 256 * head + 128] = (
+            d_keys[:, :128].astype(BF).reshape(2, half, 128)
+        )
+        dkv_ref[0, :, :, 256 * head + 128 : 256 * head + 256] = d_value.astype(BF).reshape(
+            2, half, 128
+        )
+    dq_rope = dq_rope * cosine - pltpu.roll(dq_rope, 64, 1) * sine
+    dq_ref[0, :, :, 256:384] = dq_rope.astype(BF).reshape(2, half, 128)
+    dkr_ref[0] = dk_rope.reshape(2, half, 128)
+
+
+def seq_spec(half, width):
+    return pl.BlockSpec((1, 2, half, width), lambda c, x, meta: (c, 0, x, 0))
+
+
+def attend(meta, query, expand, ropes):
+    half = query.shape[0] // 8
+    grid_spec = pltpu.PrefetchScalarGridSpec(
+        num_scalar_prefetch=1,
+        grid=(2, 2),
+        in_specs=[
+            seq_spec(half, 384),
+            seq_spec(half, 512),
+            pl.BlockSpec((1, 2, 2, half, 128), lambda c, x, meta: (c, 0, 0, x, 0)),
+        ],
+        out_specs=seq_spec(half, 256),
+    )
+    return pl.pallas_call(
+        attend_kernel,
+        grid_spec=grid_spec,
+        out_shape=jax.ShapeDtypeStruct((2, 2, 2 * half, 256), BF),
+        name="attend",
+    )(
+        meta,
+        query.reshape(2, 2, 2 * half, 384),
+        expand.reshape(2, 2, 2 * half, 512),
+        ropes,
+    ).reshape(8 * half, 256)
+
+
+def attend_back(meta, query, expand, ropes, dout, cosine, sine):
+    half = query.shape[0] // 8
+    grid_spec = pltpu.PrefetchScalarGridSpec(
+        num_scalar_prefetch=1,
+        grid=(2, 2),
+        in_specs=[
+            seq_spec(half, 384),
+            seq_spec(half, 512),
+            pl.BlockSpec((1, 2, 2, half, 128), lambda c, x, meta: (c, 0, 0, x, 0)),
+            seq_spec(half, 256),
+            seq_spec(half, 128),
+            seq_spec(half, 128),
+        ],
+        out_specs=[seq_spec(half, 384), seq_spec(half, 512), seq_spec(half, 128)],
+    )
+    d_query, d_expand, d_rope = pl.pallas_call(
+        attend_back_kernel,
+        grid_spec=grid_spec,
+        out_shape=[
+            jax.ShapeDtypeStruct((2, 2, 2 * half, 384), BF),
+            jax.ShapeDtypeStruct((2, 2, 2 * half, 512), BF),
+            jax.ShapeDtypeStruct((2, 2, 2 * half, 128), F32),
+        ],
+        name="attend_back",
+    )(
+        meta,
+        query.reshape(2, 2, 2 * half, 384),
+        expand.reshape(2, 2, 2 * half, 512),
+        ropes,
+        dout.reshape(2, 2, 2 * half, 256),
+        cosine.reshape(2, 2, 2 * half, 128),
+        sine.reshape(2, 2, 2 * half, 128),
+    )
+    return (
+        d_query.reshape(8 * half, 384),
+        d_expand.reshape(8 * half, 512),
+        d_rope.reshape(8 * half, 128),
+    )
+
+
+def pick_kernel(pick_ref, rows_ref, out_ref):
+    out_ref[0] = jnp.dot(pick_ref[0], rows_ref[0], preferred_element_type=F32).astype(BF)
+
+
+def pick_rows(pick, rows):
+    blocks, cap, count = pick.shape
+    width = rows.shape[-1]
+    return pl.pallas_call(
+        pick_kernel,
+        grid=(blocks,),
+        in_specs=[
+            pl.BlockSpec((1, cap, count), lambda b: (b, 0, 0)),
+            pl.BlockSpec((1, count, width), lambda b: (b, 0, 0)),
+        ],
+        out_specs=pl.BlockSpec((1, cap, width), lambda b: (b, 0, 0)),
+        out_shape=jax.ShapeDtypeStruct((blocks, cap, width), BF),
+        name="pick_rows",
+    )(pick, rows.reshape(blocks, count, width)).reshape(blocks * cap, width)
+
+
+def merge_kernel(left_ref, right_ref, pick_ref, rows_ref, out_ref):
+    total = jnp.dot(left_ref[...], right_ref[...], preferred_element_type=F32)
+    out_ref[...] = (total + dot_tn(pick_ref[0], rows_ref[0])).astype(BF)
+
+
+def merge_rows(left, right, pick, rows):
+    blocks, cap, count = pick.shape
+    depth, width = right.shape
+    return pl.pallas_call(
+        merge_kernel,
+        grid=(blocks,),
+        in_specs=[
+            pl.BlockSpec((count, depth), lambda b: (b, 0)),
+            pl.BlockSpec((depth, width), lambda b: (0, 0)),
+            pl.BlockSpec((1, cap, count), lambda b: (b, 0, 0)),
+            pl.BlockSpec((1, cap, width), lambda b: (b, 0, 0)),
+        ],
+        out_specs=pl.BlockSpec((count, width), lambda b: (b, 0)),
+        out_shape=jax.ShapeDtypeStruct((blocks * count, width), BF),
+        name="merge_rows",
+    )(left, right, pick, rows.reshape(blocks, cap, width))
+
+
+def local_tokens(
+    tokens,
+    attn_norm,
+    w_query,
+    w_latent,
+    latent_norm,
+    w_expand,
+    w_output,
+    ffn_norm,
+    w_router,
+    shared_gate,
+    shared_up,
+    shared_down,
+    expert_gate,
+    expert_up,
+    expert_down,
+    out_grad,
+    seq_length,
+    expert_ids,
+    fill_order,
+):
+    tok = tokens.shape[1]
+    width = tokens.shape[2]
+    n_dev = 32
+    n_experts = 16
+    n_blocks = n_dev
+    capacity = tok * TOPK // n_experts
+    pair_count = tok * TOPK
+    my_y = lax.axis_index("y")
+    my_x = lax.axis_index("x")
+    my_c = lax.axis_index("c")
+    my_z = lax.axis_index("z")
+    own_tokens = tokens[0]
+    input_rows = own_tokens.astype(F32)
+
+    route_ids = expert_ids[0]
+    flat_ids = route_ids.reshape(pair_count)
+    ranks = slot_rank(flat_ids, fill_order[0]).reshape(tok, TOPK)
+    kept = ranks < capacity
+    same = route_ids[:, :, None] == jnp.arange(n_experts, dtype=jnp.int32)[None, None, :]
+    slot_plus = jnp.sum(
+        jnp.where(same & kept[:, :, None], ranks[:, :, None] + 1, 0), axis=1
+    )
+    slot_table = (slot_plus - 1).astype(BF)
+
+    n_small = [tok, attn_norm.shape[0], ffn_norm.shape[0], latent_norm.shape[0], 16, w_router.size]
+    small_all = jnp.concatenate(
+        [
+            attn_norm,
+            ffn_norm,
+            latent_norm,
+            jnp.broadcast_to(seq_length.astype(BF), (16,)),
+            w_router.reshape(-1),
+        ]
+    )
+    to_each = jnp.concatenate(
+        [
+            jnp.concatenate([slot_table.T, slot_table.T], axis=0),
+            jnp.broadcast_to(small_all[None], (n_dev, small_all.shape[0])),
+        ],
+        axis=1,
+    )
+    small = spread(to_each, ALL)
+    cuts = [sum(n_small[: i + 1]) for i in range(len(n_small))]
+    slot_of = small[:, : cuts[0]]
+    attention_gain = small[:, cuts[0] : cuts[1]].reshape(-1).astype(F32)
+    feedforward_gain = small[:, cuts[1] : cuts[2]].reshape(-1).astype(F32)
+    latent_gain = small[:, cuts[2] : cuts[3]].reshape(-1).astype(F32)
+    lengths = small[:16, cuts[3]].astype(jnp.int32)
+    router = small[:, cuts[4] : cuts[5]].reshape(width, n_experts)
+
+    def head_columns(value):
+        rows = value.shape[0]
+        view = value.reshape(rows, PAIRS, 2, NOPE + ROPE)
+        nope = view[..., :NOPE].reshape(rows, PAIRS, 2 * NOPE)
+        rope = view[..., NOPE:].reshape(rows, PAIRS, 2, 2, ROPE // 2)
+        rope = jnp.transpose(rope, (0, 1, 3, 2, 4)).reshape(rows, PAIRS, 2 * ROPE)
+        return jnp.concatenate([nope, rope], axis=-1)
+
+    def by_pair(value):
+        return jnp.transpose(value, (1, 0, 2))
+
+    def natural_rows(value):
+        rows = value.shape[2]
+        view = value.reshape(4, 2, 4, rows, value.shape[-1])
+        return jnp.transpose(view, (1, 0, 2, 3, 4)).reshape(n_dev * rows, value.shape[-1])
+
+    wq = natural_rows(gather_z(spread(by_pair(head_columns(w_query)), PLANE)))
+    we = natural_rows(
+        gather_z(spread(by_pair(w_expand.reshape(w_expand.shape[0], PAIRS, 512)), PLANE))
+    )
+    wo = gather_z(swap_zq(w_output)).reshape(2 * VDIM, width)
+    wl = lax.all_gather(w_latent, ALL, axis=0, tiled=True)
+
+    plane_tokens = plane_gather(own_tokens)
+    h_attn = rms_norm(plane_tokens.astype(F32), attention_gain).astype(BF)
+    half_pos = jnp.arange(tok, dtype=jnp.int32)
+    pos_own = my_y * tok + half_pos
+    pos_far = (1 - my_y) * tok + half_pos
+    cos_own, sin_own = rope_tables(pos_own, ROPE)
+    cos_far, sin_far = rope_tables(pos_far, ROPE)
+
+    def plane_rows(own, far):
+        return jnp.concatenate([own, own, far, far] * 2, axis=0)
+
+    cos_rows = plane_rows(cos_own, cos_far)
+    sin_rows = plane_rows(sin_own, sin_far)
+    cos_pair = jnp.concatenate([cos_rows] * 4, axis=1)
+    sin_pair = jnp.concatenate([-sin_rows, -sin_rows, sin_rows, sin_rows], axis=1)
+    query_raw = matrix_product(h_attn, wq)
+    query_rope = query_raw[:, 256:]
+    query_rope_swapped = jnp.concatenate([query_rope[:, 64:], query_rope[:, :64]], axis=1)
+    query = jnp.concatenate(
+        [query_raw[:, :256], query_rope * cos_pair + query_rope_swapped * sin_pair], axis=1
+    ).astype(BF)
+    latent_in = matrix_product(h_attn, wl)
+    latent = rms_norm(latent_in[:, :KVR], latent_gain).astype(BF)
+    key_rope = rotate(latent_in[:, KVR:], cos_rows, sin_rows).astype(BF)
+    key_a, key_b = key_rope[:, :32], key_rope[:, 32:]
+    blank = jnp.zeros_like(key_a)
+    ropes = jnp.stack(
+        [
+            jnp.concatenate([key_a, blank, key_b, blank], axis=1).reshape(2, 2, 2 * tok, 128),
+            jnp.concatenate([blank, key_a, blank, key_b], axis=1).reshape(2, 2, 2 * tok, 128),
+        ],
+        axis=2,
+    )
+    expand = matrix_product(latent, we).astype(BF)
+    my_seq = my_z * 4 + my_x * 2 + my_c
+    meta = jnp.stack(
+        [
+            lengths[my_seq],
+            lengths[my_z * 4 + (1 - my_x) * 2 + my_c],
+            lengths[my_z * 4 + my_x * 2 + (1 - my_c)],
+            lengths[my_z * 4 + (1 - my_x) * 2 + (1 - my_c)],
+            my_y.astype(jnp.int32),
+        ]
+    )
+    attended = attend(meta, query, expand, ropes)
+    middle = input_rows + plane_reduce(matrix_product(attended, wo).astype(BF))
+
+    h_ffn = rms_norm(middle, feedforward_gain).astype(BF)
+    gates = jax.nn.softmax(matrix_product(h_ffn, router), axis=-1)
+    valid = (pos_own < seq_length[0]).astype(F32)
+    grad_y = out_grad[0].astype(F32) * valid[:, None]
+    grad_low = grad_y.astype(BF)
+    all_grad = lax.all_gather(grad_low, ALL, axis=0, tiled=True)
+    all_ffn = lax.all_gather(h_ffn, ALL, axis=0, tiled=True)
+    gate_of = spread(jnp.concatenate([gates.T, gates.T], axis=0), ALL)
+
+    n_shared = shared_down.shape[0]
+
+    def hidden_columns(value):
+        return jnp.transpose(value.reshape(value.shape[0], n_dev, n_shared), (1, 0, 2))
+
+    shared_in = spread(
+        jnp.concatenate([hidden_columns(shared_gate), hidden_columns(shared_up)], axis=2), ALL
+    ).reshape(width, 2 * n_shared)
+
+    def half_columns(value):
+        return lax.all_to_all(value[0], "y", split_axis=1, concat_axis=0, tiled=True)
+
+    gate_w = half_columns(expert_gate)
+    up_w = half_columns(expert_up)
+    down_w = expert_down[0]
+
+    slots = lax.broadcasted_iota(jnp.int32, (n_blocks, capacity, tok), 1)
+    taken = slot_of.astype(jnp.int32)[:, None, :] == slots
+    pick = taken.astype(BF)
+    rows = pick_rows(pick, all_ffn)
+    grad_rows = pick_rows(pick, all_grad)
+    gate_slot = jnp.sum(jnp.where(taken, gate_of[:, None, :], 0.0), axis=2).reshape(-1, 1)
+    gate_val = matrix_product(rows, gate_w)
+    up_val = matrix_product(rows, up_w)
+    act = jax.nn.silu(gate_val) * up_val
+    act_weighted = (act * gate_slot).astype(BF)
+    d_act = dot_nt(grad_rows, down_w)
+    d_gate_slot = jnp.sum(act * d_act, axis=1)
+    d_gate_val, d_up_val = swish_gradients(d_act * gate_slot, gate_val, up_val)
+    pair_rows = matrix_product(act_weighted, down_w).astype(BF)
+    d_rows = (dot_nt(d_gate_val, gate_w) + dot_nt(d_up_val, up_w)).astype(BF)
+
+    shared_val = matrix_product(all_ffn, shared_in)
+    shared_gate_val = shared_val[:, :n_shared]
+    shared_up_val = shared_val[:, n_shared:]
+    shared_act = (jax.nn.silu(shared_gate_val) * shared_up_val).astype(BF)
+    d_shared_act = dot_nt(all_grad, shared_down)
+    d_sgate_val, d_sup_val = swish_gradients(d_shared_act, shared_gate_val, shared_up_val)
+    d_shared_val = jnp.concatenate([d_sgate_val, d_sup_val], axis=1)
+
+    d_gate_of = jnp.sum(
+        jnp.where(taken, d_gate_slot.reshape(n_blocks, capacity)[:, :, None], 0.0), axis=1
+    )
+    d_chosen = spread(d_gate_of, ALL)
+    d_gates = (d_chosen[:n_experts] + d_chosen[n_experts:]).T
+
+    dh_part = merge_rows(d_shared_val, shared_in.T, pick, d_rows)
+    d_h_ffn = lax.psum_scatter(dh_part, ALL, scatter_dimension=0, tiled=True).astype(F32)
+    out_part = merge_rows(shared_act, shared_down, pick, pair_rows)
+    output = (
+        middle + lax.psum_scatter(out_part, ALL, scatter_dimension=0, tiled=True).astype(F32)
+    ).astype(BF)
+
+    d_down_w = dot_tn(act_weighted, grad_rows)
+    d_gate_w = dot_tn(rows, d_gate_val).astype(BF)
+    d_up_w = dot_tn(rows, d_up_val).astype(BF)
+
+    def whole_columns(value):
+        return lax.all_to_all(value, "y", split_axis=0, concat_axis=1, tiled=True).astype(F32)
+
+    d_expert_gate = whole_columns(d_gate_w)
+    d_expert_up = whole_columns(d_up_w)
+    d_shared_down = dot_tn(shared_act, all_grad)
+    d_shared_in = spread(
+        dot_tn(all_ffn, d_shared_val).astype(BF).reshape(n_dev, width // n_dev, 2 * n_shared), ALL
+    ).astype(F32)
+
+    def shared_columns(value):
+        return jnp.transpose(value, (1, 0, 2)).reshape(width // n_dev, n_dev * n_shared)
+
+    d_shared_gate = shared_columns(d_shared_in[..., :n_shared])
+    d_shared_up = shared_columns(d_shared_in[..., n_shared:])
+
+    d_logits = gates * (d_gates - jnp.sum(gates * d_gates, axis=-1, keepdims=True))
+    d_router = jnp.dot(h_ffn.astype(F32).T, d_logits, precision=lax.Precision.HIGHEST)
+    d_h_ffn = d_h_ffn + jnp.dot(
+        d_logits, router.astype(F32).T, precision=lax.Precision.HIGHEST
+    )
+    d_mid_norm, d_g_ffn = norm_back(middle, feedforward_gain, d_h_ffn)
+    grad_mid = grad_y + d_mid_norm
+    early = jnp.sum(
+        spread(
+            jnp.concatenate([d_g_ffn.reshape(n_dev, -1), d_router.reshape(n_dev, -1)], axis=1), ALL
+        ),
+        axis=0,
+    )
+    gffn_grad = early[: width // n_dev]
+    router_grad = early[width // n_dev :].reshape(width // n_dev, n_experts)
+
+    plane_dout = plane_gather(grad_mid.astype(BF))
+
+    def reduce_z(value):
+        got = spread(value.astype(BF), "z")
+        return jnp.sum(got.astype(F32), axis=0).astype(BF)
+
+    def to_owners(value, rows_each):
+        view = value.reshape(2, 4, 4, rows_each, value.shape[-1])
+        view = jnp.transpose(view, (1, 0, 2, 3, 4)).reshape(4, 8, rows_each, value.shape[-1])
+        return jnp.transpose(spread(reduce_z(view), PLANE).astype(F32), (1, 0, 2))
+
+    d_wo = dot_tn(attended, plane_dout)
+    wo_grad = swap_zq(reduce_z(d_wo.reshape(4, -1, width))).astype(F32)
+    d_attended = dot_nt(plane_dout, wo).astype(BF)
+    d_query, d_expand, d_rope = attend_back(
+        meta, query, expand, ropes, d_attended, cos_pair, sin_pair
+    )
+    d_latent_part = dot_nt(d_expand, we)
+    d_rope = jnp.concatenate(
+        [d_rope[:, :32] + d_rope[:, 32:64], d_rope[:, 64:96] + d_rope[:, 96:]], axis=1
+    )
+    d_low = plane_reduce(jnp.concatenate([d_latent_part, d_rope], axis=1).astype(BF))
+    d_latent_raw, d_g_latent = norm_back(latent_in[:tok, :KVR], latent_gain, d_low[:, :KVR])
+    d_rope_raw = rotate_back(d_low[:, KVR:], cos_own, sin_own)
+    d_latent_in = jnp.concatenate([d_latent_raw, d_rope_raw], axis=-1).astype(BF)
+    d_hattn = plane_reduce(dot_nt(d_query, wq).astype(BF)) + dot_nt(d_latent_in, wl)
+    d_wl = dot_tn(h_attn[:tok], d_latent_in).astype(BF)
+    wl_grad = lax.psum_scatter(d_wl, ALL, scatter_dimension=0, tiled=True).astype(F32)
+    we_grad = to_owners(dot_tn(latent, d_expand), w_expand.shape[0]).reshape(w_expand.shape)
+    wq_grad = to_owners(dot_tn(h_attn, d_query), w_query.shape[0])
+    d_nope = wq_grad[..., : 2 * NOPE].reshape(-1, PAIRS, 2, NOPE)
+    d_wrope = wq_grad[..., 2 * NOPE :].reshape(-1, PAIRS, 2, 2, ROPE // 2)
+    d_wrope = jnp.transpose(d_wrope, (0, 1, 3, 2, 4)).reshape(-1, PAIRS, 2, ROPE)
+    wq_grad = jnp.concatenate([d_nope, d_wrope], axis=-1).reshape(w_query.shape)
+    d_in_norm, d_g_attn = norm_back(input_rows, attention_gain, d_hattn)
+    input_grad = (grad_mid + d_in_norm).astype(BF)
+    late = jnp.sum(
+        spread(
+            jnp.concatenate([d_g_attn.reshape(n_dev, -1), d_g_latent.reshape(n_dev, -1)], axis=1),
+            ALL,
+        ),
+        axis=0,
+    )
+    return (
+        output[None],
+        input_grad[None],
+        late[: width // n_dev],
+        wq_grad,
+        wl_grad,
+        late[width // n_dev :],
+        we_grad,
+        wo_grad,
+        gffn_grad,
+        router_grad,
+        d_shared_gate,
+        d_shared_up,
+        d_shared_down,
+        d_expert_gate[None],
+        d_expert_up[None],
+        d_down_w[None],
+    )
+
+
+def tokens_plan(mesh):
+    fine = Mesh(mesh.devices.reshape(2, 4, 2, 2), ALL)
+    rows = P(FSDP, "y", None)
+    vector = P(ALL)
+    matrix = P(ALL, None)
+    in_specs = (
+        rows,
+        vector,
+        matrix,
+        matrix,
+        vector,
+        matrix,
+        matrix,
+        vector,
+        matrix,
+        matrix,
+        matrix,
+        matrix,
+        rows,
+        rows,
+        rows,
+        rows,
+        P(FSDP),
+        rows,
+        P(FSDP, "y"),
+    )
+    out_specs = (
+        rows,
+        rows,
+        vector,
+        matrix,
+        matrix,
+        vector,
+        matrix,
+        matrix,
+        vector,
+        matrix,
+        matrix,
+        matrix,
+        matrix,
+        rows,
+        rows,
+        rows,
+    )
+    return jax.shard_map(
+        local_tokens, mesh=fine, in_specs=in_specs, out_specs=out_specs, check_vma=False
+    )
+
+
+def weights_plan(mesh):
     in_specs = (
         P("fsdp", "ctx", None),
         P(("ctx", "fsdp")),
@@ -413,4 +1016,10 @@
         P("fsdp", "ctx", None),
         P("fsdp", "ctx", None),
     )
-    return jax.shard_map(local, mesh=mesh, in_specs=in_specs, out_specs=out_specs, check_vma=False)
+    return jax.shard_map(local_weights, mesh=mesh, in_specs=in_specs, out_specs=out_specs, check_vma=False)
+
+
+def solution(mesh):
+    if mesh.shape["ctx"] == 2 and mesh.shape["fsdp"] == 16:
+        return tokens_plan(mesh)
+    return weights_plan(mesh)

time: 2990 us -> 1290 us (0.43)
  waiting for transfers between devices: 2190 us -> 565 us
  matrix products: 357 us -> 161 us
  blocking collectives: 135 us -> 0 us
  Pallas kernels: 0 us -> 119 us
  starting transfers between devices: 48.2 us -> 138 us
  other arithmetic: 55.3 us -> 99.6 us
    reduce_scatter x10 -> x3, waiting for transfers between devices: 1650 us -> 300 us  [the longest x1 186 us: local_tokens(): lax.psum_scatter(out_part, ALL, scatter_dimension=0, tiled=True).astype(F32)]
    all_gather x10 -> x3, waiting for transfers between devices: 377 us -> 0.02 us  [the longest x1 0.02 us: local_tokens(): all_grad = lax.all_gather(grad_low, ALL, axis=0, tiled=True)]
    dot_general x143 -> x9, matrix products: 348 us -> 48.6 us  [matrix_product(): return jnp.dot(left, right, preferred_element_type=jnp.float32)]
    pallas_call x0 -> x6, Pallas kernels: none -> 119 us  [the longest x2 55.9 us: merge_rows(): pl.pallas_call(merge_kernel, grid=(blocks,), in_specs=[pl.BlockSpec((coun...]
    dot_general x4 -> x19, matrix products: 7.87 us -> 113 us  [the longest x9 60.7 us: dot_tn(): lax.dot_general(left, right, (((0,), (0,)), ((), ())), preferred_element_...]
    all_to_all x4 -> x21, waiting for transfers between devices: 140 us -> 232 us  [the longest x17 133 us: spread(): return lax.all_to_all(value, axes, split_axis=0, concat_axis=0, tiled=True)]
    unnamed x2 -> x0, blocking collectives: 84 us -> none
    all_to_all x4 -> x21, starting transfers between devices: 46.5 us -> 103 us  [the longest x17 83.7 us: spread(): return lax.all_to_all(value, axes, split_axis=0, concat_axis=0, tiled=True)]
  transfers between devices with their start and end apart: 27 -> 54, of which waited for: 20 -> 27; matrix products, arithmetic and copies ran while one was open for 14% -> 29% of each run, Pallas kernels for 0% -> 7%
where the time goes in v1:
time: 1290 us; the launch traced here: 1270 us
  waiting for transfers between devices  565 us (44%)
  local copies, waits for them, and re-layouts  173 us (13%)
  matrix products  161 us (12%)
  starting transfers between devices  138 us (11%)
  Pallas kernels  119 us (9%)
  other arithmetic  99.6 us (8%)
  between operations  16.8 us (1%)
    reduce_scatter x1, waiting for transfers between devices, local_tokens(): lax.psum_scatter(out_part, ALL, scatter_dimension=0, tiled=True).astype(F32)  186 us
    all_to_all x17, waiting for transfers between devices, spread(): return lax.all_to_all(value, axes, split_axis=0, concat_axis=0, tiled=True)  133 us
    reduce_scatter x1, waiting for transfers between devices, local_tokens(): lax.psum_scatter(dh_part, ALL, scatter_dimension=0, tiled=True).astype(F32)  110 us
    all_to_all x17, starting transfers between devices, spread(): return lax.all_to_all(value, axes, split_axis=0, concat_axis=0, tiled=True)  83.7 us
    all_to_all x2, waiting for transfers between devices, half_columns(): lax.all_to_all(value[0], 'y', split_axis=1, concat_axis=0, tiled=True)  74.9 us
    unnamed x215, local copies, waits for them, and re-layouts  62.7 us
    dot_general x9, matrix products, dot_tn(): lax.dot_general(left, right, (((0,), (0,)), ((), ())), preferred_element_...  60.7 us
    pallas_call x2, Pallas kernels, merge_rows(): pl.pallas_call(merge_kernel, grid=(blocks,), in_specs=[pl.BlockSpec((coun...  55.9 us
  transfers between devices with their start and end apart: 54, of which 27 were waited for; matrix products, arithmetic and copies ran while one was open for 29% of the time, Pallas kernels for 7%

profile of v1, /device:TPU:1, one launch (start us, length us, event | category | flops | bytes accessed | tf_op | source)
XLA Modules:
  0.0 1272.4 jit_solution(11885072918618334818)
XLA Ops:
  77.4 6.5 all-to-all-done.4
  108.2 48.6 %all-to-all-done.2 = bf16[4,8,64,384]{3,2,1,0:T(8,128)(2,1)} async-done(((bf16[4,8,64,384]{3,2,1,0:T(8,128)(2,1)}), bf16[4,8,64,384]{3,2,1,0:T(8,128)(2,1)}, u32[]{:S(2)}, u32[]{:S(2)}) %all-to-all-start.2) | async-done | bytes 1572896 | tf_op jit(solution)/shard_map/all_to_all | solution.py:398
  210.1 6.5 attend.1
  237.9 9.8 collective-permute-done.10
  272.4 35.8 %all-to-all-done.6 = bf16[32,64,176]{2,1,0:T(8,128)(2,1)} async-done(((bf16[32,64,176]{2,1,0:T(8,128)(2,1)}), bf16[32,64,176]{2,1,0:T(8,128)(2,1)}, u32[]{:S(2)}, u32[]{:S(2)}) %all-to-all-start.6) | async-done | bytes 720928 | tf_op jit(solution)/shard_map/all_to_all | solution.py:398
  317.9 42.2 %all-to-all-done.7 = bf16[1024,2,704]{0,2,1:T(8,128)(2,1)} async-done(((bf16[1024,2,704]{0,2,1:T(8,128)(2,1)}), bf16[1024,2,704]{0,2,1:T(8,128)(2,1)}, u32[]{:S(2)}, u32[]{:S(2)}) %all-to-all-start.7) | async-done | bytes 2883616 | tf_op jit(solution)/shard_map/all_to_all | solution.py:788
  373.8 32.7 %all-to-all-done.8 = bf16[1024,2,704]{0,2,1:T(8,128)(2,1)} async-done(((bf16[1024,2,704]{0,2,1:T(8,128)(2,1)}), bf16[1024,2,704]{0,2,1:T(8,128)(2,1)}, u32[]{:S(2)}, u32[]{:S(2)}) %all-to-all-start.8) | async-done | bytes 2883616 | tf_op jit(solution)/shard_map/all_to_all | solution.py:788
  415.4 23.4 %pick_rows.3 = bf16[32,48,2048]{2,1,0:T(8,128)(2,1)} custom-call(bf16[32,48,128]{2,1,0:T(8,128)(2,1)} %fusion.28.pick_ref, bf16[32,128,2048]{2,1,0:T(8,128)(2,1)} %bitcast.230), custom_call_target="tpu_custom_call" | custom-call | tf_op jit(solution)/shard_map/pick_rows/pallas_call | solution.py:592
  438.8 23.4 %pick_rows.2 = bf16[32,48,2048]{2,1,0:T(8,128)(2,1)} custom-call(bf16[32,48,128]{2,1,0:T(8,128)(2,1)} %fusion.28.pick_ref, bf16[32,128,2048]{2,1,0:T(8,128)(2,1)} %bitcast.235), custom_call_target="tpu_custom_call" | custom-call | tf_op jit(solution)/shard_map/pick_rows/pallas_call | solution.py:592
  462.2 7.8 fusion.78
  474.8 6.7 multiply_reduce_fusion
  489.9 8.1 fusion.79
  498.0 12.7 fusion.76
  510.8 8.6 multiply_convert_fusion.4
  523.3 10.1 add_convert_fusion
  533.4 28.1 %merge_rows.3 = bf16[4096,2048]{1,0:T(8,128)(2,1)} custom-call(bf16[4096,176]{1,0:T(8,128)(2,1)} %pad_maximum_fusion.left_ref, bf16[176,2048]{1,0:T(8,128)(2,1)} %bitcast.265, bf16[32,48,128]{2,1,0:T(8,128)(2,1)} %fusion.28.pick_ref, bf16[32,48,2048]{2,1,0:T(8,128)(2,1)} %bitcast.256), custom_call_target="tpu_custom_call" | custom-call | tf_op jit(solution)/shard_map/merge_rows/pallas_call | solution.py:613
  561.5 10.8 convolution_convert_fusion
  572.3 27.8 %merge_rows.2 = bf16[4096,2048]{1,0:T(8,128)(2,1)} custom-call(bf16[4096,88]{1,0:T(8,128)(2,1)} %get-tuple-element.141.left_ref, bf16[88,2048]{1,0:T(8,128)(2,1)} %right_ref.1, bf16[32,48,128]{2,1,0:T(8,128)(2,1)} %fusion.28.pick_ref, bf16[32,48,2048]{2,1,0:T(8,128)(2,1)} %bitcast.257), custom_call_target="tpu_custom_call" | custom-call | tf_op jit(solution)/shard_map/merge_rows/pallas_call | solution.py:613
  607.8 6.6 copy.336
  618.5 6.4 all-to-all-start.10
  625.0 10.5 convolution_convert_fusion.6
  635.5 110.0 %reduce-scatter.6.cloned.1.call-done = bf16[128,2048]{1,0:T(8,128)(2,1)} async-done(((bf16[4096,2048]{1,0:T(8,128)(2,1)}), bf16[128,2048]{1,0:T(8,128)(2,1)}) %reduce-scatter.6.cloned.1.call-update) | async-done | bytes 524304 | tf_op jit(solution)/shard_map/reduce_scatter | solution.py:825
  747.2 186.0 %reduce-scatter.4.cloned.1.call-done = bf16[128,2048]{1,0:T(8,128)(2,1)} async-done(((bf16[4096,2048]{1,0:T(8,128)(2,1)}), bf16[128,2048]{1,0:T(8,128)(2,1)}) %reduce-scatter.4.cloned.1.call-update) | async-done | bytes 524304 | tf_op jit(solution)/shard_map/reduce_scatter | solution.py:828
  938.8 9.2 convolution_convert_fusion.3
  981.5 12.6 convolution_bitcast_fusion
  995.5 6.5 all-to-all-done.18
  1015.5 9.4 attend_back.1
  1054.9 21.1 %all-to-all-done.19 = bf16[2,1024,704]{1,2,0:T(8,128)(2,1)} async-done(((bf16[2,1024,704]{1,2,0:T(8,128)(2,1)}), bf16[2,1024,704]{1,2,0:T(8,128)(2,1)}, u32[]{:S(2)}, u32[]{:S(2)}) %all-to-all-start.19) | async-done | bytes 2883616 | tf_op jit(solution)/shard_map/all_to_all | solution.py:836
  1101.7 6.7 all-to-all-done.14
  1128.5 9.9 all-to-all-done.16
  1142.9 10.0 fusion.80
  1223.2 6.7 all-to-all-done.13
  (519 shorter events, 494.3 us)
Async XLA Ops:
  7.2 178.2 %all-gather.4.cloned.1.call-start = ((), (), s32[]{:S(2)}) async-start(), calls=%async_computation.24 | async-start | bytes 2703360 | tf_op jit(solution)/shard_map/all_gather | solution.py:720
  7.9 407.4 %all-gather.8.cloned.1.call-start = ((), (), s32[]{:S(2)}) async-start(), calls=%async_computation.27 | async-start | bytes 17301504 | tf_op jit(solution)/shard_map/all_gather | solution.py:774
  11.3 55.9 %collective-permute-start = (bf16[128,2048]{1,0:T(8,128)(2,1)}, bf16[128,2048]{1,0:T(8,128)(2,1)}, u32[]{:S(2)}, u32[]{:S(2)}) collective-permute-start(bf16[128,2048]{1,0:T(8,128)(2,1)} %bitcast.241), channel_id=1, source_target_pairs={{0,2},{2,0},{1,3},{3,1},{4,6},{6,4},{5,7},{7,5},{8,10},{10,8},{9,1... | collective-permute-start | bytes 1572872 | tf_op jit(solution)/shard_map/ppermute | solution.py:389
  13.4 55.7 %collective-permute-start.1 = (bf16[128,2048]{1,0:T(8,128)(2,1)}, bf16[128,2048]{1,0:T(8,128)(2,1)}, u32[]{:S(2)}, u32[]{:S(2)}) collective-permute-start(bf16[128,2048]{1,0:T(8,128)(2,1)} %bitcast.242), channel_id=1, source_target_pairs={{0,16},{16,0},{1,17},{17,1},{2,18},{18,2},{3,19},{19,3},{4,20},{20... | collective-permute-start | bytes 1572872 | tf_op jit(solution)/shard_map/ppermute | solution.py:389
  20.8 87.4 %collective-permute-start.5 = (bf16[64,2048]{1,0:T(8,128)(2,1)}, bf16[64,2048]{1,0:T(8,128)(2,1)}, u32[]{:S(2)}, u32[]{:S(2)}) collective-permute-start(bf16[64,2048]{1,0:T(8,128)(2,1)} %param.25), channel_id=1, source_target_pairs={{0,0},{1,4},{2,8},{3,12},{4,1},{5,5},{6,9},{7,13},{8,2},{9,6},{10,... | collective-permute-start | bytes 786440 | tf_op jit(solution)/shard_map/ppermute | solution.py:394
  62.1 21.9 %all-to-all-start.4 = ((bf16[4,8,16,512]{3,2,1,0:T(8,128)(2,1)}), bf16[4,8,16,512]{3,2,1,0:T(8,128)(2,1)S(1)}, u32[]{:S(2)}, u32[]{:S(2)}) async-start(bf16[4,8,16,512]{3,2,1,0:T(8,128)(2,1)} %broadcast_in_dim.64), calls=%async_computation.4 | async-start | bytes 1048576 | tf_op jit(solution)/shard_map/all_to_all | solution.py:398
  68.9 21.8 %collective-permute-start.3 = (bf16[64,2048]{1,0:T(8,128)(2,1)}, bf16[64,2048]{1,0:T(8,128)(2,1)}, u32[]{:S(2)}, u32[]{:S(2)}) collective-permute-start(bf16[64,2048]{1,0:T(8,128)(2,1)} %slice.333), channel_id=1, source_target_pairs={{0,16},{16,0},{1,17},{17,1},{2,18},{18,2},{3,19},{19,3},{4,20},{20... | collective-permute-start | bytes 786440 | tf_op jit(solution)/shard_map/ppermute | solution.py:389
  86.3 70.5 %all-to-all-start.2 = ((bf16[4,8,64,384]{3,2,1,0:T(8,128)(2,1)}), bf16[4,8,64,384]{3,2,1,0:T(8,128)(2,1)}, u32[]{:S(2)}, u32[]{:S(2)}) async-start(bf16[4,8,64,384]{3,2,1,0:T(8,128)(2,1)} %broadcast_in_dim.63), calls=%async_computation.2 | async-start | bytes 3145728 | tf_op jit(solution)/shard_map/all_to_all | solution.py:398
  92.5 72.2 %collective-permute-start.4 = (bf16[512,2048]{1,0:T(8,128)(2,1)}, bf16[512,2048]{1,0:T(8,128)(2,1)}, u32[]{:S(2)}, u32[]{:S(2)}) collective-permute-start(bf16[512,2048]{1,0:T(8,128)(2,1)} %get-tuple-element.188), channel_id=1, source_target_pairs={{0,1},{1,0},{2,3},{3,2},{4,5},{5,4},{6,7},{7,6},{8,9},{9,8},{10,11... | collective-permute-start | bytes 6291464 | tf_op jit(solution)/shard_map/ppermute | solution.py:389
  158.9 57.7 %all-to-all-start.5 = ((bf16[4,64,2048]{2,1,0:T(8,128)(2,1)}), bf16[4,64,2048]{2,1,0:T(8,128)(2,1)}, u32[]{:S(2)}, u32[]{:S(2)}) async-start(bf16[4,64,2048]{2,1,0:T(8,128)(2,1)} %broadcast_in_dim.66), calls=%async_computation.5 | async-start | bytes 2097152 | tf_op jit(solution)/shard_map/all_to_all | solution.py:398
  163.1 275.7 %all-gather.6.cloned.1.call-start = ((), (), s32[]{:S(2)}) async-start(), calls=%async_computation.25 | async-start | bytes 17301504 | tf_op jit(solution)/shard_map/all_gather | solution.py:775
  261.5 46.7 %all-to-all-start.6 = ((bf16[32,64,176]{2,1,0:T(8,128)(2,1)}), bf16[32,64,176]{2,1,0:T(8,128)(2,1)}, u32[]{:S(2)}, u32[]{:S(2)}) async-start(bf16[32,64,176]{2,1,0:T(8,128)(2,1)} %pad_maximum_fusion.2), calls=%async_computation.6 | async-start | bytes 2097152 | tf_op jit(solution)/shard_map/all_to_all | solution.py:398
  308.2 51.9 %all-to-all-start.7 = ((bf16[1024,2,704]{0,2,1:T(8,128)(2,1)}), bf16[1024,2,704]{0,2,1:T(8,128)(2,1)}, u32[]{:S(2)}, u32[]{:S(2)}) async-start(bf16[1024,2,704]{0,2,1:T(8,128)(2,1)} %bitcast.239), calls=%async_computation.7 | async-start | bytes 5767168 | tf_op jit(solution)/shard_map/all_to_all | solution.py:788
  360.1 46.4 %all-to-all-start.8 = ((bf16[1024,2,704]{0,2,1:T(8,128)(2,1)}), bf16[1024,2,704]{0,2,1:T(8,128)(2,1)}, u32[]{:S(2)}, u32[]{:S(2)}) async-start(bf16[1024,2,704]{0,2,1:T(8,128)(2,1)} %bitcast.238), calls=%async_computation.8 | async-start | bytes 5767168 | tf_op jit(solution)/shard_map/all_to_all | solution.py:788
  411.3 70.2 %all-to-all-start.9 = ((f32[32,1,128]{2,1,0:T(1,128)}), f32[32,1,128]{2,1,0:T(1,128)S(1)}, u32[]{:S(2)}, u32[]{:S(2)}) async-start(f32[32,1,128]{2,1,0:T(1,128)} %bitcast.40), calls=%async_computation.9 | async-start | bytes 32768 | tf_op jit(solution)/shard_map/all_to_all | solution.py:398
  415.3 330.2 %reduce-scatter.6.cloned.1.call-start = ((), (), s32[]{:S(2)}) async-start(), calls=%async_computation.28 | async-start | bytes 17301504 | tf_op jit(solution)/shard_map/reduce_scatter | solution.py:825
  561.5 371.7 %reduce-scatter.4.cloned.1.call-start = ((), (), s32[]{:S(2)}) async-start(), calls=%async_computation.26 | async-start | bytes 17301504 | tf_op jit(solution)/shard_map/reduce_scatter | solution.py:828
  959.7 48.1 %collective-permute-start.15 = (bf16[512,2048]{1,0:T(8,128)(2,1)}, bf16[512,2048]{1,0:T(8,128)(2,1)}, u32[]{:S(2)}, u32[]{:S(2)}) collective-permute-start(bf16[512,2048]{1,0:T(8,128)(2,1)} %get-tuple-element.184), channel_id=1, source_target_pairs={{0,1},{1,0},{2,3},{3,2},{4,5},{5,4},{6,7},{7,6},{8,9},{9,8},{10,11... | collective-permute-start | bytes 6291464 | tf_op jit(solution)/shard_map/ppermute | solution.py:389
  970.2 31.8 %all-to-all-start.18 = ((bf16[32,64,176]{2,1,0:T(8,128)(2,1)}), bf16[32,64,176]{2,1,0:T(8,128)(2,1)S(1)}, u32[]{:S(2)}, u32[]{:S(2)}) async-start(bf16[32,64,176]{2,1,0:T(8,128)(2,1)} %bitcast.86), calls=%async_computation.21 | async-start | bytes 2097152 | tf_op jit(solution)/shard_map/all_to_all | solution.py:398
  1002.9 36.3 %all-to-all-start.20 = ((bf16[2,1024,704]{1,2,0:T(8,128)(2,1)}), bf16[2,1024,704]{1,2,0:T(8,128)(2,1)S(1)}, u32[]{:S(2)}, u32[]{:S(2)}) async-start(bf16[2,1024,704]{1,2,0:T(8,128)(2,1)} %bitcast.237), calls=%async_computation.23 | async-start | bytes 5767168 | tf_op jit(solution)/shard_map/all_to_all | solution.py:836
  1039.2 36.9 %all-to-all-start.19 = ((bf16[2,1024,704]{1,2,0:T(8,128)(2,1)}), bf16[2,1024,704]{1,2,0:T(8,128)(2,1)}, u32[]{:S(2)}, u32[]{:S(2)}) async-start(bf16[2,1024,704]{1,2,0:T(8,128)(2,1)} %bitcast.236), calls=%async_computation.22 | async-start | bytes 5767168 | tf_op jit(solution)/shard_map/all_to_all | solution.py:836
  1048.0 33.6 %collective-permute-start.21 = (bf16[512,576]{0,1:T(8,128)(2,1)S(1)}, bf16[512,576]{0,1:T(8,128)(2,1)}, u32[]{:S(2)}, u32[]{:S(2)}) collective-permute-start(bf16[512,576]{0,1:T(8,128)(2,1)S(1)} %slice.378), channel_id=1, source_target_pairs={{0,1},{1,0},{2,3},{3,2},{4,5},{5,4},{6,7},{7,6},{8,9},{9,8},{10,11... | collective-permute-start | bytes 1769480 | tf_op jit(solution)/shard_map/ppermute | solution.py:389
  1100.5 20.4 %collective-permute-start.25 = (bf16[128,576]{0,1:T(8,128)(2,1)}, bf16[128,576]{0,1:T(8,128)(2,1)}, u32[]{:S(2)}, u32[]{:S(2)}) collective-permute-start(bf16[128,576]{0,1:T(8,128)(2,1)} %pad_maximum_fusion.15), channel_id=1, source_target_pairs={{0,16},{16,0},{1,17},{17,1},{2,18},{18,2},{3,19},{19,3},{4,20},{20... | collective-permute-start | bytes 442376 | tf_op jit(solution)/shard_map/ppermute | solution.py:389
  1108.5 29.9 %all-to-all-start.16 = ((bf16[4,64,2048]{2,1,0:T(8,128)(2,1)}), bf16[4,64,2048]{2,1,0:T(8,128)(2,1)}, u32[]{:S(2)}, u32[]{:S(2)}) async-start(bf16[4,64,2048]{2,1,0:T(8,128)(2,1)} %fusion.8), calls=%async_computation.19 | async-start | bytes 2097152 | tf_op jit(solution)/shard_map/all_to_all | solution.py:398
  1112.7 150.7 %reduce-scatter.8.cloned.1.call-start = ((), (), s32[]{:S(2)}) async-start(), calls=%async_computation.29 | async-start | bytes 2703360 | tf_op jit(solution)/shard_map/reduce_scatter | solution.py:894
  1120.1 33.1 %collective-permute-start.16 = (bf16[512,2048]{1,0:T(8,128)(2,1)}, bf16[512,2048]{1,0:T(8,128)(2,1)}, u32[]{:S(2)}, u32[]{:S(2)}) collective-permute-start(bf16[512,2048]{1,0:T(8,128)(2,1)} %slice.364), channel_id=1, source_target_pairs={{0,1},{1,0},{2,3},{3,2},{4,5},{5,4},{6,7},{7,6},{8,9},{9,8},{10,11... | collective-permute-start | bytes 6291464 | tf_op jit(solution)/shard_map/ppermute | solution.py:389
  1138.3 64.3 %all-to-all-start.12 = ((bf16[4,8,64,384]{3,2,1,0:T(8,128)(2,1)}), bf16[4,8,64,384]{3,2,1,0:T(8,128)(2,1)}, u32[]{:S(2)}, u32[]{:S(2)}) async-start(bf16[4,8,64,384]{3,2,1,0:T(8,128)(2,1)} %bitcast.245), calls=%async_computation.14 | async-start | bytes 3145728 | tf_op jit(solution)/shard_map/all_to_all | solution.py:398
  1158.7 42.4 %collective-permute-start.19 = (bf16[64,2048]{1,0:T(8,128)(2,1)}, bf16[64,2048]{1,0:T(8,128)(2,1)}, u32[]{:S(2)}, u32[]{:S(2)}) collective-permute-start(bf16[64,2048]{1,0:T(8,128)(2,1)} %get-tuple-element.150), channel_id=1, source_target_pairs={{0,2},{2,0},{1,3},{3,1},{4,6},{6,4},{5,7},{7,5},{8,10},{10,8},{9,1... | collective-permute-start | bytes 786440 | tf_op jit(solution)/shard_map/ppermute | solution.py:389
  1158.7 42.4 %collective-permute-start.17 = (bf16[64,2048]{1,0:T(8,128)(2,1)}, bf16[64,2048]{1,0:T(8,128)(2,1)}, u32[]{:S(2)}, u32[]{:S(2)}) collective-permute-start(bf16[64,2048]{1,0:T(8,128)(2,1)} %get-tuple-element.151), channel_id=1, source_target_pairs={{0,16},{16,0},{1,17},{17,1},{2,18},{18,2},{3,19},{19,3},{4,20},{20... | collective-permute-start | bytes 786440 | tf_op jit(solution)/shard_map/ppermute | solution.py:389
  1195.7 26.7 %collective-permute-start.26 = (bf16[64,2048]{1,0:T(8,128)(2,1)S(1)}, bf16[64,2048]{1,0:T(8,128)(2,1)S(1)}, u32[]{:S(2)}, u32[]{:S(2)}) collective-permute-start(bf16[64,2048]{1,0:T(8,128)(2,1)S(1)} %reduce_sum.240), channel_id=1, source_target_pairs={{0,0},{1,4},{2,8},{3,12},{4,1},{5,5},{6,9},{7,13},{8,2},{9,6},{10,... | collective-permute-start | bytes 786440 | tf_op jit(solution)/shard_map/ppermute | solution.py:394
  1209.3 27.0 %collective-permute-start.20 = (bf16[128,2048]{1,0:T(8,128)(2,1)}, bf16[128,2048]{1,0:T(8,128)(2,1)}, u32[]{:S(2)}, u32[]{:S(2)}) collective-permute-start(bf16[128,2048]{1,0:T(8,128)(2,1)} %pad_maximum_fusion.11), channel_id=1, source_target_pairs={{0,16},{16,0},{1,17},{17,1},{2,18},{18,2},{3,19},{19,3},{4,20},{20... | collective-permute-start | bytes 1572872 | tf_op jit(solution)/shard_map/ppermute | solution.py:389
  1220.2 20.8 %collective-permute-start.18 = (bf16[128,2048]{1,0:T(8,128)(2,1)}, bf16[128,2048]{1,0:T(8,128)(2,1)}, u32[]{:S(2)}, u32[]{:S(2)}) collective-permute-start(bf16[128,2048]{1,0:T(8,128)(2,1)} %pad_maximum_fusion.10), channel_id=1, source_target_pairs={{0,2},{2,0},{1,3},{3,1},{4,6},{6,4},{5,7},{7,5},{8,10},{10,8},{9,1... | collective-permute-start | bytes 1572872 | tf_op jit(solution)/shard_map/ppermute | solution.py:389
  (116 other events, 3446.8 us)
Sparse Core Ops, SparseCore 0:
  11.0 67.3 all-gather.3
  81.8 155.3 all-gather.7
  253.5 151.4 all-gather.5
  561.6 183.8 reduce-scatter.5
  747.7 185.4 reduce-scatter.3
  1128.6 134.8 reduce-scatter.7

commit v2 on v0

--- a/solution.py
+++ b/solution.py
@@ -1,6 +1,9 @@
 import jax
 import jax.numpy as jnp
 from jax import lax
+from jax.experimental import pallas as pl
+from jax.experimental.pallas import tpu as pltpu
+from jax.sharding import Mesh
 from jax.sharding import PartitionSpec as P
 
 HEADS = 16
@@ -70,7 +73,7 @@
     return (d_gate, d_up)
 
 
-def local(
+def local_weights(
     tokens,
     attn_norm,
     w_query,
@@ -373,7 +376,1008 @@
     )
 
 
-def solution(mesh):
+ALL = ("y", "z", "x", "c")
+PLANE = ("y", "x", "c")
+FSDP = ("z", "x", "c")
+BF = jnp.bfloat16
+F32 = jnp.float32
+PAIRS = 8
+SEQ_BLOCKS = 2
+
+
+def swap(value, axis):
+    return lax.ppermute(value, axis, [(0, 1), (1, 0)])
+
+
+def swap_zq(value):
+    pairs = [(z * 4 + q, q * 4 + z) for z in range(4) for q in range(4)]
+    return lax.ppermute(value, FSDP, pairs)
+
+
+def spread(value, axes):
+    return lax.all_to_all(value, axes, split_axis=0, concat_axis=0, tiled=True)
+
+
+def shift_z(value, step):
+    return lax.ppermute(value, "z", [(i, (i + step) % 4) for i in range(4)])
+
+
+class Chain:
+    def __init__(self, hops):
+        self.hops = hops
+        self.pending = next(hops)
+        self.result = None
+        self.ended = False
+
+    def advance(self, arrived):
+        if self.ended:
+            return
+        try:
+            self.pending = self.hops.send(arrived)
+        except StopIteration as stop:
+            self.pending, self.result, self.ended = [], stop.value, True
+
+
+def tick(values, *chains):
+    values, arrived = lax.optimization_barrier((values, [chain.pending for chain in chains]))
+    for chain, parts in zip(chains, arrived):
+        chain.advance(parts)
+    return values
+
+
+def one_hop(*parts):
+    return (yield list(parts))
+
+
+def swap_both(value):
+    return lax.ppermute(value, ("y", "x"), [(i, 3 - i) for i in range(4)])
+
+
+def gather_hops(block, last=None):
+    if last is None:
+        near = yield [swap(block, "y"), swap(block, "x"), swap_both(block)]
+        near = [block, *near]
+        far = yield [swap(part, "c") for part in near]
+        return near + far
+    by_x, by_y = yield [swap(block, "x"), swap(block, "y")]
+    (diag,) = yield [swap(by_x, "y") if last == "y" else swap(by_y, "x")]
+    near = [block, by_y, by_x, diag]
+    far = yield [swap(part, "c") for part in near]
+    return near + far
+
+
+def add(*parts):
+    return sum(part.astype(F32) for part in parts)
+
+
+def reduce_hops(parts, first):
+    got = yield [swap(part, "c") for part in parts[4:]]
+    diag = add(parts[3], got[3]).astype(BF)
+    if first is None:
+        came = yield [
+            swap(add(parts[1], got[1]).astype(BF), "y"),
+            swap(add(parts[2], got[2]).astype(BF), "x"),
+            swap_both(diag),
+        ]
+        return add(parts[0], got[0], *came)
+    if first == "y":
+        (got_diag,) = yield [swap(diag, "y")]
+        to_y = add(parts[1], got[1]).astype(BF)
+        to_x = add(parts[2], got[2], got_diag).astype(BF)
+    else:
+        (got_diag,) = yield [swap(diag, "x")]
+        to_x = add(parts[2], got[2]).astype(BF)
+        to_y = add(parts[1], got[1], got_diag).astype(BF)
+    got_x, got_y = yield [swap(to_x, "x"), swap(to_y, "y")]
+    return add(parts[0], got[0], got_x, got_y)
+
+
+def home_hops(parts, first, step):
+    total = yield from reduce_hops(parts, first)
+    if step:
+        (total,) = yield [shift_z(total.astype(BF), -step)]
+    return total
+
+
+def at_plane(step):
+    return (lax.axis_index("z") + step) % 4
+
+
+def line_hops(value):
+    ups = [(i, i + 1) for i in range(3)]
+    downs = [(i + 1, i) for i in range(3)]
+    up, down = [value], [value]
+    for _ in range(3):
+        came = yield [lax.ppermute(up[-1], "z", ups), lax.ppermute(down[-1], "z", downs)]
+        up.append(came[0])
+        down.append(came[1])
+    result = jnp.zeros((4,) + value.shape, value.dtype)
+    result = lax.dynamic_update_index_in_dim(result, value, at_plane(0), 0)
+    for hop in range(1, 4):
+        result = lax.dynamic_update_index_in_dim(
+            result, up[hop] + down[4 - hop], at_plane(4 - hop), 0
+        )
+    return result
+
+
+def direct_hops(value):
+    came = yield [shift_z(value, step) for step in range(1, 4)]
+    result = jnp.zeros((4,) + value.shape, value.dtype)
+    result = lax.dynamic_update_index_in_dim(result, value, at_plane(0), 0)
+    for step in range(1, 4):
+        result = lax.dynamic_update_index_in_dim(result, came[step - 1], at_plane(4 - step), 0)
+    return result
+
+
+def sum_hops(value):
+    came = [lax.dynamic_index_in_dim(value, at_plane(0), 0, keepdims=False)]
+    for step in (1, 3, 2):
+        part = lax.dynamic_index_in_dim(value, at_plane(step), 0, keepdims=False)
+        came += yield [shift_z(part, step)]
+    return add(*came).astype(BF)
+
+
+def dot_nt(left, right):
+    return lax.dot_general(left, right, (((1,), (1,)), ((), ())), preferred_element_type=F32)
+
+
+def dot_tn(left, right):
+    return lax.dot_general(left, right, (((0,), (0,)), ((), ())), preferred_element_type=F32)
+
+
+LIMIT = 60 * 1024 * 1024
+VMEM_SPEC = pl.BlockSpec(memory_space=pltpu.VMEM)
+SMEM_SPEC = pl.BlockSpec(memory_space=pltpu.SMEM)
+ANY_SPEC = pl.BlockSpec(memory_space=pl.ANY)
+STEPS = (0, 1, 2, 3)
+ROWS = 128
+SEQ = 256
+
+
+def columns(step, size):
+    return pl.ds(pl.multiple_of(step * size, size), size)
+
+
+def attention_probs(meta, seq, query, expand, ropes, head):
+    count = query.shape[0]
+    half = count // 2
+    keys = jnp.concatenate(
+        [expand[:, 256 * head : 256 * head + 128], ropes[:, 128 * head : 128 * head + 128]], axis=1
+    )
+    rows = lax.broadcasted_iota(jnp.int32, (count, count), 0)
+    cols = lax.broadcasted_iota(jnp.int32, (count, count), 1)
+    own = meta[4]
+    row_pos = jnp.where(rows < half, rows + own * half, rows - half + (1 - own) * half)
+    col_pos = jnp.where(cols < half, cols + own * half, cols - half + (1 - own) * half)
+    allowed = (col_pos <= row_pos) & (col_pos < meta[seq])
+    queries = jnp.concatenate(
+        [query[:, 128 * head : 128 * head + 128], query[:, 256:384]], axis=1
+    )
+    scores = dot_nt(queries, keys) * (NOPE + ROPE) ** (-0.5)
+    scores = jnp.where(allowed, scores, NEGATIVE_FILL)
+    expo = jnp.exp(scores - jnp.max(scores, axis=-1, keepdims=True))
+    probs = expo / jnp.sum(expo, axis=-1, keepdims=True)
+    return probs, queries, keys
+
+
+def attend_kernel(meta, *refs):
+    tokens = refs[:8]
+    gain, latent_gain, wq, wl, we, cos_ref, sin_ref = refs[8:15]
+    h_ref, query_ref, latent_ref, rope_ref, expand_ref, attended_ref, raw_ref = refs[15:22]
+    for block in range(8):
+        value = tokens[block][...].astype(F32)
+        inverse = lax.rsqrt(jnp.mean(value * value, axis=-1, keepdims=True) + EPSILON)
+        h_ref[pl.ds(block * ROWS, ROWS), :] = (value * inverse * gain[...]).astype(BF)
+
+    def sequence(seq, carry):
+        rows = pl.ds(pl.multiple_of(seq * SEQ, SEQ), SEQ)
+        h_seq = h_ref[rows, :]
+        cosine, sine = cos_ref[...], sin_ref[...]
+        raw = jnp.dot(h_seq, wq[...], preferred_element_type=F32)
+        rope = raw[:, 256:]
+        rope = rope * cosine + pltpu.roll(rope, 64, 1) * sine
+        query = jnp.concatenate([raw[:, :256], rope], axis=1).astype(BF)
+        query_ref[rows, :] = query
+        latent_in = jnp.dot(h_seq, wl[...], preferred_element_type=F32)
+        value = latent_in[:, :KVR]
+
+        @pl.when(seq == 0)
+        def _():
+            raw_ref[...] = value[:ROWS]
+
+        inverse = lax.rsqrt(jnp.mean(value * value, axis=-1, keepdims=True) + EPSILON)
+        latent = (value * inverse * latent_gain[...]).astype(BF)
+        latent_ref[rows, :] = latent
+        ropes = []
+        for head in range(2):
+            key = latent_in[:, KVR + 128 * head : KVR + 128 * head + 128]
+            ropes.append(key * cosine + pltpu.roll(key, 64, 1) * sine)
+        ropes = jnp.concatenate(ropes, axis=1).astype(BF)
+        rope_ref[rows, :] = ropes
+        expand = jnp.dot(latent, we[...], preferred_element_type=F32).astype(BF)
+        expand_ref[rows, :] = expand
+        for head in range(2):
+            probs, _, _ = attention_probs(meta, seq, query, expand, ropes, head)
+            values = expand[:, 256 * head + 128 : 256 * head + 256]
+            attended_ref[rows, 128 * head : 128 * head + 128] = jnp.dot(
+                probs.astype(BF), values, preferred_element_type=F32
+            ).astype(BF)
+        return carry
+
+    lax.fori_loop(0, 4, sequence, 0)
+
+
+def project_kernel(attended_ref, wo, *outs):
+    def project(step, carry):
+        cols = columns(step, 256)
+        part = jnp.dot(attended_ref[...], wo[:, cols], preferred_element_type=F32).astype(BF)
+        for block in range(8):
+            outs[block][:, cols] = part[block * ROWS : (block + 1) * ROWS]
+        return carry
+
+    lax.fori_loop(0, wo.shape[1] // 256, project, 0)
+
+
+def project(attended, wo):
+    width = wo.shape[1]
+    return pl.pallas_call(
+        project_kernel,
+        in_specs=[VMEM_SPEC] * 2,
+        out_specs=[VMEM_SPEC] * 8,
+        out_shape=[jax.ShapeDtypeStruct((ROWS, width), BF)] * 8,
+        compiler_params=pltpu.CompilerParams(vmem_limit_bytes=LIMIT),
+        cost_estimate=pl.CostEstimate(
+            flops=10**9, bytes_accessed=6 * 10**6, transcendentals=0
+        ),
+        name="project",
+    )(attended, wo)
+
+
+def attend(meta, tokens, gain, latent_gain, wq, wl, we, cosine, sine):
+    width = wq.shape[0]
+    shape = jax.ShapeDtypeStruct
+    return pl.pallas_call(
+        attend_kernel,
+        in_specs=[SMEM_SPEC] + [VMEM_SPEC] * 15,
+        out_specs=[VMEM_SPEC] * 7,
+        out_shape=[
+            shape((8 * ROWS, width), BF),
+            shape((8 * ROWS, 384), BF),
+            shape((8 * ROWS, KVR), BF),
+            shape((8 * ROWS, 256), BF),
+            shape((8 * ROWS, 512), BF),
+            shape((8 * ROWS, 256), BF),
+            shape((ROWS, KVR), F32),
+        ],
+        compiler_params=pltpu.CompilerParams(vmem_limit_bytes=LIMIT),
+        cost_estimate=pl.CostEstimate(
+            flops=14 * 10**9, bytes_accessed=24 * 10**6, transcendentals=10**6
+        ),
+        name="attend",
+    )(meta, *tokens, gain[None], latent_gain[None], wq, wl, we, cosine, sine)
+
+
+def attend_back_kernel(meta, *refs):
+    douts = refs[:8]
+    query_ref, rope_ref, expand_ref, wq, we, wo, cos_ref, sin_ref = refs[8:16]
+    dq_ref, dkv_ref = refs[16:18]
+    lows = refs[18:26]
+    hats = refs[26:34]
+    dout_ref, datt_ref, low_ref = refs[34:37]
+    scale = (NOPE + ROPE) ** (-0.5)
+    for block in range(8):
+        dout_ref[pl.ds(block * ROWS, ROWS), :] = douts[block][...]
+    datt_ref[...] = dot_nt(dout_ref[...], wo[...]).astype(BF)
+
+    def sequence(seq, carry):
+        rows = pl.ds(pl.multiple_of(seq * SEQ, SEQ), SEQ)
+        cosine, sine = cos_ref[...], sin_ref[...]
+        query, expand, ropes = query_ref[rows, :], expand_ref[rows, :], rope_ref[rows, :]
+        lane = lax.broadcasted_iota(jnp.int32, (SEQ, 128), 1)
+        first = (lane % 64) < 32
+        dq_rope = jnp.zeros((SEQ, 128), F32)
+        dk_rope = jnp.zeros((SEQ, 128), F32)
+        for head in range(2):
+            probs, queries, keys = attention_probs(meta, seq, query, expand, ropes, head)
+            values = expand[:, 256 * head + 128 : 256 * head + 256]
+            dout = datt_ref[rows, 128 * head : 128 * head + 128]
+            d_value = dot_tn(probs.astype(BF), dout)
+            d_probs = dot_nt(dout, values)
+            delta = jnp.sum(probs * d_probs, axis=-1, keepdims=True)
+            d_scores = (probs * (d_probs - delta)).astype(BF)
+            d_query = jnp.dot(d_scores, keys, preferred_element_type=F32) * scale
+            d_keys = dot_tn(d_scores, queries) * scale
+            dq_ref[rows, 128 * head : 128 * head + 128] = d_query[:, :128].astype(BF)
+            dq_rope = dq_rope + d_query[:, 128:]
+            dk_rope = dk_rope + jnp.where(first == (head == 0), d_keys[:, 128:], 0.0)
+            dkv_ref[rows, 256 * head : 256 * head + 128] = d_keys[:, :128].astype(BF)
+            dkv_ref[rows, 256 * head + 128 : 256 * head + 256] = d_value.astype(BF)
+        dq_rope = dq_rope * cosine - pltpu.roll(dq_rope, 64, 1) * sine
+        dq_ref[rows, 256:384] = dq_rope.astype(BF)
+        both = jnp.where(first, dk_rope + pltpu.roll(dk_rope, 96, 1), 0.0)
+        low_ref[rows, :KVR] = dot_nt(dkv_ref[rows, :], we[...]).astype(BF)
+        low_ref[rows, KVR:] = both.astype(BF)
+        return carry
+
+    lax.fori_loop(0, 4, sequence, 0)
+    for block in range(8):
+        lows[block][...] = low_ref[pl.ds(block * ROWS, ROWS), :]
+
+    def project(step, carry):
+        cols = columns(step, 256)
+        part = dot_nt(dq_ref[...], wq[cols, :]).astype(BF)
+        for block in range(8):
+            hats[block][:, cols] = part[block * ROWS : (block + 1) * ROWS]
+        return carry
+
+    lax.fori_loop(0, wq.shape[0] // 256, project, 0)
+
+
+def attend_back(meta, douts, query, ropes, expand, wq, we, wo, cosine, sine):
+    width = wq.shape[0]
+    shape = jax.ShapeDtypeStruct
+    out = pl.pallas_call(
+        attend_back_kernel,
+        in_specs=[SMEM_SPEC] + [VMEM_SPEC] * 16,
+        out_specs=[VMEM_SPEC] * 18,
+        out_shape=[
+            shape((8 * ROWS, 384), BF),
+            shape((8 * ROWS, 512), BF),
+        ]
+        + [shape((ROWS, KVR + 128), BF)] * 8
+        + [shape((ROWS, width), BF)] * 8,
+        scratch_shapes=[
+            pltpu.VMEM((8 * ROWS, width), BF),
+            pltpu.VMEM((8 * ROWS, 256), BF),
+            pltpu.VMEM((8 * ROWS, KVR + 128), BF),
+        ],
+        compiler_params=pltpu.CompilerParams(vmem_limit_bytes=LIMIT),
+        cost_estimate=pl.CostEstimate(
+            flops=14 * 10**9, bytes_accessed=24 * 10**6, transcendentals=10**6
+        ),
+        name="attend_back",
+    )(meta, *douts, query, ropes, expand, wq, we, wo, cosine, sine)
+    return out[:2], out[2:10], out[10:]
+
+
+def taken_slots(slot_ref, index, block, cap):
+    slots = lax.broadcasted_iota(jnp.int32, (cap, ROWS), 0).astype(F32)
+    return slot_ref[pl.ds(index[block], 1), :] == slots
+
+
+def ffn_kernel(index, *refs):
+    tokens = refs[:8]
+    grads = refs[8:16]
+    slot_ref, wg, wu, wd, si, sd = refs[16:22]
+    refs = refs[23:] if len(refs) == 48 else refs[22:]
+    out_ref, rows_ref, grows_ref, aw_ref, dg_ref, du_ref, dsi_ref, dsd_ref = refs[:8]
+    dhs = refs[8:16]
+    h_ref, g_ref, part_ref, pair_ref, drow_ref, dslot_ref, put_ref, weight_ref, sems = refs[16:25]
+    cap = rows_ref.shape[0] // 8
+    width = g_ref.shape[1]
+    copies = []
+    for block in range(8):
+        here = pl.ds(block * ROWS, ROWS)
+        copies.append(pltpu.make_async_copy(tokens[block], h_ref.at[here, :], sems.at[block]))
+        copies.append(pltpu.make_async_copy(grads[block], g_ref.at[here, :], sems.at[8 + block]))
+    for copy in copies:
+        copy.start()
+    for copy in copies:
+        copy.wait()
+    lane = lax.broadcasted_iota(jnp.int32, (cap, ROWS), 1)
+    mine = (lane < 48) & (lane % 16 == index[8])
+    for block in range(8):
+        here = pl.ds(block * ROWS, ROWS)
+        inside = pl.ds(block * cap, cap)
+        pick = taken_slots(slot_ref, index, block, cap).astype(F32)
+        put_ref[here, :cap] = pick.T.astype(BF)
+        pick = pick.astype(BF)
+        picked = jnp.dot(pick, h_ref[here, :], preferred_element_type=F32)
+        rows_ref[inside, :] = picked[:, :width].astype(BF)
+        grows_ref[inside, :] = jnp.dot(pick, g_ref[here, :], preferred_element_type=F32).astype(BF)
+        weight = jnp.sum(jnp.where(mine, picked[:, width:], 0.0), axis=1, keepdims=True)
+        weight_ref[inside, :] = jnp.broadcast_to(weight, (cap, ROWS))
+    weight = weight_ref[:, :1]
+    d_slot = jnp.zeros((8 * cap, 1), F32)
+    for step in range(wg.shape[1] // 256):
+        cols = slice(step * 256, step * 256 + 256)
+        gate = jnp.dot(rows_ref[...], wg[:, cols], preferred_element_type=F32)
+        up = jnp.dot(rows_ref[...], wu[:, cols], preferred_element_type=F32)
+        d_act = dot_nt(grows_ref[...], wd[cols, :])
+        sigma = jax.nn.sigmoid(gate)
+        act = gate * sigma * up
+        d_slot = d_slot + jnp.sum(act * d_act, axis=1, keepdims=True)
+        d_act = d_act * weight
+        aw_ref[:, cols] = (act * weight).astype(BF)
+        dg_ref[:, cols] = (d_act * up * sigma * (1.0 + gate * (1.0 - sigma))).astype(BF)
+        du_ref[:, cols] = (d_act * gate * sigma).astype(BF)
+    lane = lax.broadcasted_iota(jnp.int32, (8 * cap, ROWS), 1)
+    high = d_slot.astype(BF).astype(F32)
+    dslot_ref[...] = jnp.where(
+        lane == index[8], high, jnp.where(lane == 64 + index[8], d_slot - high, 0.0)
+    ).astype(BF)
+    for block in range(8):
+        here = pl.ds(block * ROWS, ROWS)
+        dhs[block][:, width:] = jnp.dot(
+            put_ref[here, :cap], dslot_ref[pl.ds(block * cap, cap), :], preferred_element_type=F32
+        ).astype(BF)
+    shared = jnp.dot(h_ref[:, :width], si[...], preferred_element_type=F32)
+    d_act = dot_nt(g_ref[...], sd[...])
+    gate, up = shared[:, :128], shared[:, 128:]
+    sigma = jax.nn.sigmoid(gate)
+    act = (gate * sigma * up).astype(BF)
+    d_gate = d_act * up * sigma * (1.0 + gate * (1.0 - sigma))
+    d_up = d_act * gate * sigma
+    d_both = jnp.concatenate([d_gate, d_up], axis=1).astype(BF)
+    turned = d_both.T
+    act_turned = act.T
+
+    def tile(step, carry):
+        cols = columns(step, 256)
+        pair_ref[...] = jnp.dot(aw_ref[...], wd[:, cols], preferred_element_type=F32).astype(BF)
+        drow_ref[...] = (dot_nt(dg_ref[...], wg[cols, :]) + dot_nt(du_ref[...], wu[cols, :])).astype(
+            BF
+        )
+        from_shared = jnp.dot(act, sd[:, cols], preferred_element_type=F32)
+        back_shared = dot_nt(d_both, si[cols, :])
+        for block in range(8):
+            here = slice(block * ROWS, (block + 1) * ROWS)
+            inside = slice(block * cap, (block + 1) * cap)
+            put = put_ref[here, :cap]
+            part_ref[here, cols] = (
+                from_shared[here]
+                + jnp.dot(put, pair_ref[inside, :], preferred_element_type=F32)
+            ).astype(BF)
+            dhs[block][:, cols] = (
+                back_shared[here]
+                + jnp.dot(put, drow_ref[inside, :], preferred_element_type=F32)
+            ).astype(BF)
+        dsi_ref[:, cols] = jnp.dot(turned, h_ref[:, cols], preferred_element_type=F32)
+        dsd_ref[:, cols] = jnp.dot(act_turned, g_ref[:, cols], preferred_element_type=F32)
+        return carry
+
+    lax.fori_loop(0, width // 256, tile, 0)
+    copies = []
+    for block in range(8):
+        here = pl.ds(block * ROWS, ROWS)
+        there = pl.ds(pl.multiple_of(index[block] * ROWS, ROWS), ROWS)
+        copies.append(
+            pltpu.make_async_copy(part_ref.at[here, :], out_ref.at[there, :], sems.at[block])
+        )
+    for copy in copies:
+        copy.start()
+    for copy in copies:
+        copy.wait()
+
+
+def ffn(index, tokens, grads, slot_of, weights, out, cap):
+    width = grads[0].shape[1]
+    hidden = weights[0].shape[1]
+    shape = jax.ShapeDtypeStruct
+    alias = [] if out is None else [out]
+    result = pl.pallas_call(
+        ffn_kernel,
+        in_specs=[SMEM_SPEC] + [ANY_SPEC] * 16 + [VMEM_SPEC] * 6 + [ANY_SPEC] * len(alias),
+        out_specs=[ANY_SPEC] + [VMEM_SPEC] * 15,
+        out_shape=[
+            shape((32 * ROWS, width), BF),
+            shape((8 * cap, width), BF),
+            shape((8 * cap, width), BF),
+            shape((8 * cap, hidden), BF),
+            shape((8 * cap, hidden), BF),
+            shape((8 * cap, hidden), BF),
+            shape((256, width), F32),
+            shape((128, width), F32),
+        ]
+        + [shape((ROWS, width + 128), BF)] * 8,
+        scratch_shapes=[
+            pltpu.VMEM((8 * ROWS, width + 128), BF),
+            pltpu.VMEM((8 * ROWS, width), BF),
+            pltpu.VMEM((8 * ROWS, width), BF),
+            pltpu.VMEM((8 * cap, 256), BF),
+            pltpu.VMEM((8 * cap, 256), BF),
+            pltpu.VMEM((8 * cap, ROWS), BF),
+            pltpu.VMEM((8 * ROWS, ROWS), BF),
+            pltpu.VMEM((8 * cap, ROWS), F32),
+            pltpu.SemaphoreType.DMA((16,)),
+        ],
+        input_output_aliases={23: 0} if alias else {},
+        compiler_params=pltpu.CompilerParams(vmem_limit_bytes=LIMIT),
+        cost_estimate=pl.CostEstimate(
+            flops=20 * 10**9, bytes_accessed=40 * 10**6, transcendentals=10**6
+        ),
+        name="ffn",
+    )(index, *tokens, *grads, slot_of, *weights, *alias)
+    return result[0], result[1:8], result[8:]
+
+
+def rows_grad_kernel(left_ref, *refs):
+    out_ref = refs[8]
+    turned = left_ref[...].T
+    total = jnp.zeros(out_ref.shape, F32)
+    for block in range(8):
+        total = total + jnp.dot(
+            turned[:, block * ROWS : (block + 1) * ROWS],
+            refs[block][...],
+            preferred_element_type=F32,
+        )
+    out_ref[...] = total.astype(BF)
+
+
+def rows_grad(left, blocks):
+    width = blocks[0].shape[1]
+    return pl.pallas_call(
+        rows_grad_kernel,
+        grid=(width // 512,),
+        in_specs=[pl.BlockSpec(left.shape, lambda t: (0, 0))]
+        + [pl.BlockSpec((ROWS, 512), lambda t: (0, t))] * 8,
+        out_specs=pl.BlockSpec((left.shape[1], 512), lambda t: (0, t)),
+        out_shape=jax.ShapeDtypeStruct((left.shape[1], width), BF),
+        compiler_params=pltpu.CompilerParams(vmem_limit_bytes=LIMIT),
+        cost_estimate=pl.CostEstimate(
+            flops=10**9, bytes_accessed=6 * 10**6, transcendentals=0
+        ),
+        name="rows_grad",
+    )(left, *blocks)
+
+
+def local_tokens(
+    tokens,
+    attn_norm,
+    w_query,
+    w_latent,
+    latent_norm,
+    w_expand,
+    w_output,
+    ffn_norm,
+    w_router,
+    shared_gate,
+    shared_up,
+    shared_down,
+    expert_gate,
+    expert_up,
+    expert_down,
+    out_grad,
+    seq_length,
+    expert_ids,
+    fill_order,
+):
+    tok = tokens.shape[1]
+    width = tokens.shape[2]
+    n_dev = 32
+    n_experts = 16
+    n_blocks = n_dev
+    capacity = tok * TOPK // n_experts
+    pair_count = tok * TOPK
+    my_y = lax.axis_index("y")
+    my_x = lax.axis_index("x")
+    my_c = lax.axis_index("c")
+    my_z = lax.axis_index("z")
+    own_tokens = tokens[0]
+    input_rows = own_tokens.astype(F32)
+
+    route_ids = expert_ids[0]
+    flat_ids = route_ids.reshape(pair_count)
+    ranks = slot_rank(flat_ids, fill_order[0]).reshape(tok, TOPK)
+    kept = ranks < capacity
+    same = route_ids[:, :, None] == jnp.arange(n_experts, dtype=jnp.int32)[None, None, :]
+    slot_plus = jnp.sum(
+        jnp.where(same & kept[:, :, None], ranks[:, :, None] + 1, 0), axis=1
+    )
+    slot_table = (slot_plus - 1).astype(BF)
+
+    n_small = [tok, attn_norm.shape[0], ffn_norm.shape[0], latent_norm.shape[0], 16, w_router.size]
+    small_all = jnp.concatenate(
+        [
+            attn_norm,
+            ffn_norm,
+            latent_norm,
+            jnp.broadcast_to(seq_length.astype(BF), (16,)),
+            w_router.reshape(-1),
+        ]
+    )
+    to_each = jnp.concatenate(
+        [
+            jnp.concatenate([slot_table.T, slot_table.T], axis=0),
+            jnp.broadcast_to(small_all[None], (n_dev, small_all.shape[0])),
+        ],
+        axis=1,
+    )
+
+    def column_tiles(value, groups):
+        rows = value.shape[0]
+        view = jnp.transpose(value.reshape(rows, -1, ROWS), (1, 0, 2))
+        return view.reshape(groups, -1, ROWS)
+
+    def natural_rows(value, rows):
+        view = value.reshape(4, 2, 4, -1, rows, ROWS)
+        view = jnp.transpose(view, (1, 0, 2, 4, 3, 5))
+        return view.reshape(n_dev * rows, -1)
+
+    query_rows = w_query.shape[0] * 3
+    packed = jnp.concatenate([column_tiles(w_query, PAIRS), column_tiles(w_expand, PAIRS)], axis=1)
+    wl_all = lax.all_gather(w_latent, ALL, axis=0, tiled=True)
+    valid = (my_y * tok + jnp.arange(tok, dtype=jnp.int32) < seq_length[0]).astype(F32)
+    grad_y = out_grad[0].astype(F32) * valid[:, None]
+    grad_low = grad_y.astype(BF)
+    n_shared = shared_down.shape[0]
+    shared_pad = 128 - n_shared
+    n_half = expert_down.shape[1]
+    half_pad = -n_half % 256
+
+    def widen_columns(value, amount):
+        return jnp.pad(value, ((0, 0), (0, amount)))
+
+    own_low = own_tokens
+    tokens_go = Chain(gather_hops(own_low, "y"))
+    below_go = Chain(one_hop(shift_z(grad_low, 1)))
+    packed = spread(packed, PLANE)
+    packed, grad_low, w_output = tick((packed, grad_low, w_output), tokens_go, below_go)
+    packed_go = Chain(line_hops(packed))
+    zq_go = Chain(one_hop(swap_zq(w_output)))
+    small = spread(to_each, ALL)
+    grad_low, small = tick((grad_low, small), tokens_go, packed_go)
+    grads_go = [Chain(gather_hops(grad_low, "x"))]
+    grad_low, expert_gate, wl_all = tick(
+        (grad_low, expert_gate, wl_all), tokens_go, packed_go, zq_go, grads_go[0]
+    )
+
+    def halves(value):
+        first, second = value[0, :, :n_half], value[0, :, n_half:]
+        mine = jnp.where(my_y == 0, first, second)
+        return mine, Chain(one_hop(swap(jnp.where(my_y == 0, second, first), "y")))
+
+    def whole_rows(mine, chain):
+        other = chain.result[0]
+        both = jnp.concatenate(
+            [jnp.where(my_y == 0, mine, other), jnp.where(my_y == 0, other, mine)], axis=0
+        )
+        return widen_columns(both, half_pad)
+
+    gate_mine, gate_go = halves(expert_gate)
+    grads_go.append(Chain(gather_hops(below_go.result[0], "y")))
+    latent_at = jnp.arange(KVR + 256)
+    lane = (latent_at - KVR) % 128
+    head = (latent_at - KVR) // 128
+    latent_from = jnp.where(
+        latent_at < KVR,
+        latent_at,
+        jnp.where(lane // 32 % 2 == head, KVR + lane % 32 + lane // 64 * 32, -1),
+    )
+    widen = (jnp.arange(KVR + ROPE)[:, None] == latent_from[None, :]).astype(BF)
+    wl = matrix_product(wl_all, widen).astype(BF)
+    grad_low, wl = tick((grad_low, wl), packed_go, grads_go[0], grads_go[1])
+
+    cuts = [sum(n_small[: i + 1]) for i in range(len(n_small))]
+    slot_of = small[:, : cuts[0]].astype(F32)
+    attention_gain = small[:, cuts[0] : cuts[1]].reshape(-1).astype(F32)
+    feedforward_gain = small[:, cuts[1] : cuts[2]].reshape(-1).astype(F32)
+    latent_gain = small[:, cuts[2] : cuts[3]].reshape(-1).astype(F32)
+    lengths = small[:16, cuts[3]].astype(jnp.int32)
+    router = small[:, cuts[4] : cuts[5]].reshape(width, n_experts)
+    packed = packed_go.result
+    wq = natural_rows(packed[:, :, :query_rows], w_query.shape[0])
+    we = natural_rows(packed[:, :, query_rows:], w_expand.shape[0])
+    target = jnp.arange(384)
+    rope_at = target - 256
+    source = jnp.where(
+        target < 256,
+        target % 128 + target // 128 * 192,
+        128 + rope_at % 32 + rope_at // 32 % 2 * 192 + rope_at // 64 * 32,
+    )
+    reorder = (jnp.arange(384)[:, None] == source[None, :]).astype(BF)
+    wq = matrix_product(wq, reorder).astype(BF)
+    half_pos = jnp.arange(tok, dtype=jnp.int32)
+    pos_own = my_y * tok + half_pos
+    cos_own, sin_own = rope_tables(pos_own, ROPE)
+    cos_far, sin_far = rope_tables((1 - my_y) * tok + half_pos, ROPE)
+    cos_pair = jnp.concatenate([jnp.concatenate([cos_own, cos_far], axis=0)] * 4, axis=1)
+    sin_pair = jnp.concatenate([sin_own, sin_far], axis=0)
+    sin_pair = jnp.concatenate([-sin_pair, -sin_pair, sin_pair, sin_pair], axis=1)
+    my_seq = my_z * 4 + my_x * 2 + my_c
+    meta = jnp.stack(
+        [
+            lengths[my_seq],
+            lengths[my_z * 4 + (1 - my_x) * 2 + my_c],
+            lengths[my_z * 4 + my_x * 2 + (1 - my_c)],
+            lengths[my_z * 4 + (1 - my_x) * 2 + (1 - my_c)],
+            my_y.astype(jnp.int32),
+        ]
+    )
+    above_go = Chain(one_hop(shift_z(grad_low, -1)))
+    wq, wl, we, meta, grad_low, expert_up = tick(
+        (wq, wl, we, meta, grad_low, expert_up), grads_go[0], grads_go[1], above_go
+    )
+
+    wo_go = Chain(direct_hops(zq_go.result[0]))
+    grads_go.append(Chain(gather_hops(above_go.result[0], "x")))
+    up_mine, up_go = halves(expert_up)
+    kept_values = attend(
+        meta, tokens_go.result, attention_gain, latent_gain, wq, wl, we, cos_pair, sin_pair
+    )
+    kept_values, grad_low, shared_gate, shared_up = tick(
+        (kept_values, grad_low, shared_gate, shared_up), wo_go, grads_go[1], grads_go[2], gate_go
+    )
+    h_attn, query, latent, ropes, expand, attended, latent_raw = kept_values
+    wo = wo_go.result.reshape(2 * VDIM, width)
+    attended_parts = project(attended, wo)
+
+    def hidden_columns(value):
+        return jnp.transpose(value.reshape(value.shape[0], n_dev, n_shared), (1, 0, 2))
+
+    attended_parts = tick(attended_parts, grads_go[2])
+    middle_go = Chain(reduce_hops(attended_parts, "y"))
+    across_go = Chain(one_hop(shift_z(grad_low, 2)))
+    tick((), middle_go)
+    tick((), middle_go, grads_go[2])
+    tick((), middle_go, across_go)
+    grads_go.append(Chain(gather_hops(across_go.result[0], "y")))
+    middle = input_rows + middle_go.result
+
+    h_ffn = rms_norm(middle, feedforward_gain).astype(BF)
+    gates = jax.nn.softmax(matrix_product(h_ffn, router), axis=-1)
+    gates_high = gates.astype(BF)
+    gates_left = gates - gates_high.astype(F32)
+    gates_middle = gates_left.astype(BF)
+    gates_low = (gates_left - gates_middle.astype(F32)).astype(BF)
+    gates_rest = jnp.zeros((tok, 128 - 3 * n_experts), BF)
+    sent = jnp.concatenate([h_ffn, gates_high, gates_middle, gates_low, gates_rest], axis=1)
+
+    sent, shared_gate, shared_up = tick((sent, shared_gate, shared_up), grads_go[3])
+    shared_both = spread(
+        jnp.concatenate([hidden_columns(shared_gate), hidden_columns(shared_up)], axis=2), ALL
+    )
+    go = [Chain(gather_hops(sent, "y"))]
+    below_go = Chain(one_hop(shift_z(sent, 1)))
+    gate_w = whole_rows(gate_mine, gate_go)
+    down_w = jnp.pad(expert_down[0], ((0, half_pad), (0, 0)))
+    sent, gate_w, down_w = tick((sent, gate_w, down_w), go[0], grads_go[3], below_go)
+    across_go = Chain(one_hop(shift_z(sent, 2)))
+    go.append(Chain(gather_hops(below_go.result[0], "x")))
+    shared_out = jnp.pad(shared_down, ((0, shared_pad), (0, 0)))
+    sent, shared_both, shared_out = tick(
+        (sent, shared_both, shared_out), go[0], go[1], grads_go[3], up_go
+    )
+    above_go = Chain(one_hop(shift_z(sent, -1)))
+    shared_both = shared_both.reshape(width, 2 * n_shared)
+    shared_in = jnp.concatenate(
+        [
+            widen_columns(shared_both[:, :n_shared], shared_pad),
+            widen_columns(shared_both[:, n_shared:], shared_pad),
+        ],
+        axis=1,
+    )
+    weights = (gate_w, whole_rows(up_mine, up_go), down_w, shared_in, shared_out)
+    weights = tick(weights, go[0], go[1], across_go)
+    go.append(Chain(gather_hops(across_go.result[0])))
+    grads_go = [grads_go[0], grads_go[1], grads_go[3], grads_go[2]]
+
+    plane = jnp.stack(
+        [
+            (my_y ^ dy) * 16 + (my_x ^ dx) * 2 + (my_c ^ dc)
+            for dc in range(2)
+            for dx in range(2)
+            for dy in range(2)
+        ]
+    ).astype(jnp.int32)
+    saved = []
+    homes = []
+    out_part = None
+    for number in range(4):
+        index = plane + (my_z - STEPS[number]) % 4 * 4
+        index = jnp.concatenate([index, my_seq[None].astype(jnp.int32)])
+        results = ffn(
+            index, go[number].result, grads_go[number].result, slot_of, weights, out_part, capacity
+        )
+        more = [above_go] if number == 0 else []
+        out_part, kept_here, d_h_parts, weights = tick(
+            results + (weights,), *go[number + 1 :], *homes, *more
+        )
+        if number == 0:
+            go.append(Chain(gather_hops(above_go.result[0])))
+        saved.append(kept_here)
+        homes.append(Chain(home_hops(d_h_parts, None, STEPS[number])))
+
+    rows, grad_rows, act_weighted, d_gate_val, d_up_val = (
+        jnp.concatenate([item[i] for item in saved], axis=0) for i in range(5)
+    )
+
+    def column_halves(left, right):
+        value = dot_tn(left, right)[:, :n_half].astype(BF)
+        first, second = value[: width // 2], value[width // 2 :]
+        mine = jnp.where(my_y == 0, first, second)
+        return mine, Chain(one_hop(swap(jnp.where(my_y == 0, second, first), "y")))
+
+    def whole_columns(mine, chain):
+        other = chain.result[0]
+        return jnp.concatenate(
+            [jnp.where(my_y == 0, mine, other), jnp.where(my_y == 0, other, mine)], axis=1
+        ).astype(F32)
+
+    rows, grad_rows = tick((rows, grad_rows), *homes)
+    d_gate_mine, d_gate_go = column_halves(rows, d_gate_val)
+    rows, d_gate_mine, grad_rows = tick((rows, d_gate_mine, grad_rows), *homes)
+    d_up_mine, d_up_go = column_halves(rows, d_up_val)
+    d_up_mine, grad_rows = tick((d_up_mine, grad_rows), *homes)
+    d_shared_in = sum(item[5] for item in saved).astype(BF).T.reshape(n_dev, width // n_dev, 256)
+    d_shared_in = jnp.concatenate(
+        [d_shared_in[..., :n_shared], d_shared_in[..., 128 : 128 + n_shared]], axis=2
+    )
+    d_shared_down = sum(item[6] for item in saved)[:n_shared]
+    d_h_ffn = add(*(home.result for home in homes))
+    d_gates = d_h_ffn[:, width : width + n_experts] + d_h_ffn[:, width + 64 : width + 64 + n_experts]
+    d_h_ffn = d_h_ffn[:, :width]
+
+    d_logits = gates * (d_gates - jnp.sum(gates * d_gates, axis=-1, keepdims=True))
+    d_h_ffn = d_h_ffn + jnp.dot(
+        d_logits, router.astype(F32).T, precision=lax.Precision.HIGHEST
+    )
+    d_mid_norm, d_g_ffn = norm_back(middle, feedforward_gain, d_h_ffn)
+    grad_mid = grad_y + d_mid_norm
+
+    grad_mid = tick(grad_mid)
+    douts_go = Chain(gather_hops(grad_mid.astype(BF), "y"))
+    d_down_w = dot_tn(act_weighted, grad_rows)[:n_half]
+    d_down_w = tick(d_down_w, douts_go)
+    d_shared_in = tick(d_shared_in, douts_go)
+    d_router = jnp.dot(h_ffn.astype(F32).T, d_logits, precision=lax.Precision.HIGHEST)
+    d_router = tick(d_router, douts_go)
+    d_wo = rows_grad(attended, douts_go.result)
+    d_wo, out_part = tick((d_wo, out_part))
+    wo_go = Chain(sum_hops(d_wo.reshape(4, -1, width)))
+    output = lax.psum_scatter(out_part, ALL, scatter_dimension=0, tiled=True)
+    (d_query, d_expand), low_parts, hat_parts = tick(
+        attend_back(
+            meta, douts_go.result, query, ropes, expand, wq, we, wo, cos_pair, sin_pair
+        ),
+        wo_go,
+    )
+
+    def by_owner(value, rows_each):
+        view = value.astype(BF).reshape(2, 4, 4, rows_each, -1, ROWS)
+        return jnp.transpose(view, (1, 0, 2, 4, 3, 5)).reshape(4, 8, -1, ROWS)
+
+    low_go = Chain(reduce_hops(low_parts, "x"))
+    hat_go = Chain(reduce_hops(hat_parts, "y"))
+    d_query = dot_nt(d_query, reorder).astype(BF)
+    d_packed = jnp.concatenate(
+        [
+            by_owner(dot_tn(h_attn, d_query), w_query.shape[0]),
+            by_owner(dot_tn(latent, d_expand), w_expand.shape[0]),
+        ],
+        axis=2,
+    )
+    d_packed = tick(d_packed, low_go, hat_go, wo_go)
+    packed_go = Chain(sum_hops(d_packed))
+    tick((), low_go, hat_go, wo_go)
+    tick((), low_go, packed_go)
+    d_low = low_go.result
+    d_latent_raw, d_g_latent = norm_back(latent_raw, latent_gain, d_low[:, :KVR])
+    d_rope = jnp.concatenate([d_low[:, KVR : KVR + 32], d_low[:, KVR + 64 : KVR + 96]], axis=1)
+    d_rope_raw = rotate_back(d_rope, cos_own, sin_own)
+    d_latent_in = jnp.concatenate([d_latent_raw, d_rope_raw], axis=-1).astype(BF)
+    d_latent_in = tick(d_latent_in, hat_go, packed_go)
+    dlat_go = Chain(gather_hops(d_latent_in, "x"))
+    d_hattn = hat_go.result + dot_nt(d_latent_in, wl_all)
+    d_in_norm, d_g_attn = norm_back(input_rows, attention_gain, d_hattn)
+    input_grad = (grad_mid + d_in_norm).astype(BF)
+    early = jnp.concatenate([d_g_ffn.reshape(n_dev, -1), d_router.reshape(n_dev, -1)], axis=1)
+    small_grads = jnp.concatenate(
+        [early, d_g_attn.reshape(n_dev, -1), d_g_latent.reshape(n_dev, -1)], axis=1
+    )
+    input_grad, small_grads = tick((input_grad, small_grads), dlat_go)
+    tick((), dlat_go)
+    tick((), dlat_go, zq_back := Chain(one_hop(swap_zq(wo_go.result))))
+    my_pair = my_y * 4 + my_x * 2 + my_c
+    part_cols = w_latent.shape[1] // PAIRS
+    plane_dlat = jnp.concatenate(dlat_go.result, axis=0)
+    d_columns = lax.dynamic_slice_in_dim(
+        widen_columns(plane_dlat, 64), my_pair * part_cols, ROWS, axis=1
+    )
+    latent_go = Chain(sum_hops(by_owner(dot_tn(h_attn, d_columns), w_latent.shape[0])))
+    tick((), packed_go, latent_go)
+    tick((), latent_go)
+    tick((), latent_go, d_gate_go, d_up_go)
+    d_packed = spread(
+        jnp.concatenate([packed_go.result, latent_go.result], axis=1), PLANE
+    ).astype(F32)
+    split = w_query.shape[0] * 3
+    wq_grad = jnp.transpose(
+        d_packed[:, :split].reshape(PAIRS, 3, w_query.shape[0], ROWS), (2, 0, 1, 3)
+    ).reshape(w_query.shape)
+    we_grad = jnp.transpose(
+        d_packed[:, split : -w_latent.shape[0]].reshape(PAIRS, 4, w_expand.shape[0], ROWS),
+        (2, 0, 1, 3),
+    ).reshape(w_expand.shape)
+    wl_grad = jnp.transpose(
+        d_packed[:, -w_latent.shape[0] :, :part_cols], (1, 0, 2)
+    ).reshape(w_latent.shape)
+    wo_grad = zq_back.result[0].astype(F32)
+    d_shared_in = spread(d_shared_in, ALL).astype(F32)
+
+    def shared_columns(value):
+        return jnp.transpose(value, (1, 0, 2)).reshape(width // n_dev, n_dev * n_shared)
+
+    d_shared_gate = shared_columns(d_shared_in[..., :n_shared])
+    d_shared_up = shared_columns(d_shared_in[..., n_shared:])
+    d_expert_gate = whole_columns(d_gate_mine, d_gate_go)
+    d_expert_up = whole_columns(d_up_mine, d_up_go)
+    output = (middle + output.astype(F32)).astype(BF)
+    small_grads = jnp.sum(spread(small_grads, ALL), axis=0)
+    rows_each = width // n_dev
+    gffn_grad = small_grads[:rows_each]
+    router_grad = small_grads[rows_each : rows_each * (1 + n_experts)].reshape(rows_each, n_experts)
+    late = small_grads[rows_each * (1 + n_experts) :]
+    return (
+        output[None],
+        input_grad[None],
+        late[: width // n_dev],
+        wq_grad,
+        wl_grad,
+        late[width // n_dev :],
+        we_grad,
+        wo_grad,
+        gffn_grad,
+        router_grad,
+        d_shared_gate,
+        d_shared_up,
+        d_shared_down,
+        d_expert_gate[None],
+        d_expert_up[None],
+        d_down_w[None],
+    )
+
+
+def tokens_plan(mesh):
+    fine = Mesh(mesh.devices.reshape(2, 4, 2, 2), ALL)
+    rows = P(FSDP, "y", None)
+    vector = P(ALL)
+    matrix = P(ALL, None)
+    in_specs = (
+        rows,
+        vector,
+        matrix,
+        matrix,
+        vector,
+        matrix,
+        matrix,
+        vector,
+        matrix,
+        matrix,
+        matrix,
+        matrix,
+        rows,
+        rows,
+        rows,
+        rows,
+        P(FSDP),
+        rows,
+        P(FSDP, "y"),
+    )
+    out_specs = (
+        rows,
+        rows,
+        vector,
+        matrix,
+        matrix,
+        vector,
+        matrix,
+        matrix,
+        vector,
+        matrix,
+        matrix,
+        matrix,
+        matrix,
+        rows,
+        rows,
+        rows,
+    )
+    return jax.shard_map(
+        local_tokens, mesh=fine, in_specs=in_specs, out_specs=out_specs, check_vma=False
+    )
+
+
+def weights_plan(mesh):
     in_specs = (
         P("fsdp", "ctx", None),
         P(("ctx", "fsdp")),
@@ -413,4 +1417,10 @@
         P("fsdp", "ctx", None),
         P("fsdp", "ctx", None),
     )
-    return jax.shard_map(local, mesh=mesh, in_specs=in_specs, out_specs=out_specs, check_vma=False)
+    return jax.shard_map(local_weights, mesh=mesh, in_specs=in_specs, out_specs=out_specs, check_vma=False)
+
+
+def solution(mesh):
+    if mesh.shape["ctx"] == 2 and mesh.shape["fsdp"] == 16:
+        return tokens_plan(mesh)
+    return weights_plan(mesh)

time: 2990 us -> 1020 us (0.34)
  waiting for transfers between devices: 2190 us -> 372 us
  matrix products: 357 us -> 45.7 us
  Pallas kernels: 0 us -> 187 us
  starting transfers between devices: 48.2 us -> 207 us
  blocking collectives: 135 us -> 0 us
  local copies, waits for them, and re-layouts: 175 us -> 93.6 us
  other arithmetic: 55.3 us -> 88.5 us
    reduce_scatter x10 -> x1, waiting for transfers between devices: 1650 us -> 0.01 us  [local_tokens(): output = lax.psum_scatter(out_part, ALL, scatter_dimension=0, tiled=True)]
    all_gather x10 -> x1, waiting for transfers between devices: 377 us -> 0.01 us  [local_tokens(): wl_all = lax.all_gather(w_latent, ALL, axis=0, tiled=True)]
    ppermute x0 -> x159, waiting for transfers between devices: none -> 359 us  [the longest x124 236 us: swap(): return lax.ppermute(value, axis, [(0, 1), (1, 0)])]
    dot_general x143 -> x3, matrix products: 348 us -> 8.87 us  [matrix_product(): return jnp.dot(left, right, preferred_element_type=jnp.float32)]
    pallas_call x0 -> x8, Pallas kernels: none -> 187 us  [the longest x4 137 us: ffn(): pl.pallas_call(ffn_kernel, in_specs=[SMEM_SPEC] + [ANY_SPEC] * 16 + [VMEM...]
    ppermute x0 -> x159, starting transfers between devices: none -> 179 us  [the longest x124 125 us: swap(): return lax.ppermute(value, axis, [(0, 1), (1, 0)])]
    all_to_all x4 -> x6, waiting for transfers between devices: 140 us -> 12.4 us  [spread(): return lax.all_to_all(value, axes, split_axis=0, concat_axis=0, tiled=True)]
    unnamed x2 -> x0, blocking collectives: 84 us -> none
  transfers between devices with their start and end apart: 27 -> 167, of which waited for: 20 -> 45; matrix products, arithmetic and copies ran while one was open for 14% -> 21% of each run, Pallas kernels for 0% -> 18%
where the time goes in v2:
time: 1020 us; the launch traced here: 1010 us
  waiting for transfers between devices  372 us (36%)
  starting transfers between devices  207 us (20%)
  Pallas kernels  187 us (18%)
  local copies, waits for them, and re-layouts  93.6 us (9%)
  other arithmetic  88.5 us (9%)
  matrix products  45.7 us (4%)
  between operations  17.7 us (2%)
    ppermute x124, waiting for transfers between devices, swap(): return lax.ppermute(value, axis, [(0, 1), (1, 0)])  236 us
    pallas_call x4, Pallas kernels, ffn(): pl.pallas_call(ffn_kernel, in_specs=[SMEM_SPEC] + [ANY_SPEC] * 16 + [VMEM...  137 us
    ppermute x124, starting transfers between devices, swap(): return lax.ppermute(value, axis, [(0, 1), (1, 0)])  125 us
    ppermute x21, waiting for transfers between devices, shift_z(): return lax.ppermute(value, 'z', [(i, (i + step) % 4) for i in range(4)])  82.1 us
    dot_general x6, matrix products, dot_tn(): lax.dot_general(left, right, (((0,), (0,)), ((), ())), preferred_element_...  31.2 us
    all_to_all x6, starting transfers between devices, spread(): return lax.all_to_all(value, axes, split_axis=0, concat_axis=0, tiled=True)  28.1 us
    ppermute x21, starting transfers between devices, shift_z(): return lax.ppermute(value, 'z', [(i, (i + step) % 4) for i in range(4)])  26.3 us
  transfers between devices with their start and end apart: 167, of which 45 were waited for; matrix products, arithmetic and copies ran while one was open for 21% of the time, Pallas kernels for 18%

profile of v2, /device:TPU:1, one launch (start us, length us, event | category | flops | bytes accessed | tf_op | source)
XLA Modules:
  0.0 1011.5 jit_solution(6281087809269856428)
XLA Ops:
  29.4 6.9 all-to-all-start.1
  47.6 8.8 collective-permute-done.5
  66.3 6.2 collective-permute-done.12
  87.7 6.5 collective-permute-start.18
  105.3 6.2 convolution_convert_fusion.refs_11_
  145.7 11.5 %collective-permute-done.27 = bf16[64,2048]{1,0:T(8,128)(2,1)S(1)} collective-permute-done((bf16[64,2048]{1,0:T(8,128)(2,1)}, bf16[64,2048]{1,0:T(8,128)(2,1)S(1)}, u32[]{:S(2)}, u32[]{:S(2)}) %collective-permute-start.27) | collective-permute-done | bytes 262176 | tf_op jit(solution)/shard_map/ppermute | solution.py:402
  160.6 19.9 %attend.1 = (bf16[1024,2048]{1,0:T(8,128)(2,1)}, bf16[1024,384]{1,0:T(8,128)(2,1)}, bf16[1024,512]{1,0:T(8,128)(2,1)}, bf16[1024,256]{1,0:T(8,128)(2,1)}, bf16[1...) custom-call(s32[5]{0:T(128)} %stack.34.meta, bf16[128,2048]{1,0:T(8,128)(2,1)} %bitcast.185, ...), custom_call_target="tpu_custom_call" | custom-call | flops 14000000000 | bytes 24000000 | tf_op jit(solution)/shard_map/attend/pallas_call | solution.py:639
  205.7 10.0 collective-permute-done.41
  222.8 6.2 collective-permute-done.48.refs_8_
  234.9 34.2 %collective-permute-done.50.refs_9_ = bf16[128,2048]{1,0:T(8,128)(2,1)} collective-permute-done((bf16[128,2048]{1,0:T(8,128)(2,1)}, bf16[128,2048]{1,0:T(8,128)(2,1)}, u32[]{:S(2)}, u32[]{:S(2)}) %collective-permute-start.50) | collective-permute-done | bytes 524320 | tf_op jit(solution)/shard_map/ppermute | solution.py:389
  274.9 6.0 all-to-all-start.2
  295.8 13.8 %collective-permute-done.52.refs_1_ = bf16[128,2176]{1,0:T(8,128)(2,1)} collective-permute-done((bf16[128,2176]{1,0:T(8,128)(2,1)}, bf16[128,2176]{1,0:T(8,128)(2,1)}, u32[]{:S(2)}, u32[]{:S(2)}) %collective-permute-start.52) | collective-permute-done | bytes 557088 | tf_op jit(solution)/shard_map/ppermute | solution.py:389
  314.7 21.3 %collective-permute-done.55.refs_3_ = bf16[128,2176]{1,0:T(8,128)(2,1)S(1)} collective-permute-done((bf16[128,2176]{1,0:T(8,128)(2,1)}, bf16[128,2176]{1,0:T(8,128)(2,1)S(1)}, u32[]{:S(2)}, u32[]{:S(2)}) %collective-permute-start.55) | collective-permute-done | bytes 557088 | tf_op jit(solution)/shard_map/ppermute | solution.py:389
  348.5 16.6 %collective-permute-done.68.refs_0_ = bf16[128,2176]{1,0:T(8,128)(2,1)} collective-permute-done((bf16[128,2176]{1,0:T(8,128)(2,1)}, bf16[128,2176]{1,0:T(8,128)(2,1)}, u32[]{:S(2)}, u32[]{:S(2)}) %collective-permute-start.68) | collective-permute-done | bytes 557088 | tf_op jit(solution)/shard_map/ppermute | solution.py:402
  371.6 7.2 collective-permute-done.67.refs_3_
  383.9 34.2 %ffn.4 = (bf16[4096,2048]{1,0:T(8,128)(2,1)}, bf16[384,2048]{1,0:T(8,128)(2,1)}, bf16[384,2048]{1,0:T(8,128)(2,1)}, bf16[384,768]{1,0:T(8,128)(2,1)}, bf16[384,7...) custom-call(s32[9]{0:T(128)} %get-tuple-element.1004.index, ...), custom_call_target="tpu_custom_call" | custom-call | flops 20000000000 | bytes 40000000 | tf_op jit(solution)/shard_map/ffn/pallas_call | solution.py:858
  425.5 34.2 %ffn.5 = (bf16[4096,2048]{1,0:T(8,128)(2,1)}, bf16[384,2048]{1,0:T(8,128)(2,1)}, bf16[384,2048]{1,0:T(8,128)(2,1)}, bf16[384,768]{1,0:T(8,128)(2,1)}, bf16[384,7...) custom-call(s32[9]{0:T(128)} %get-tuple-element.1005.index, ...), custom_call_target="tpu_custom_call", output_to_operand_aliasing={{0}: (23, {})} | custom-call | flops 20000000000 | bytes 40000000 | tf_op jit(solution)/shard_map/ffn/pallas_call | solution.py:858
  466.4 8.7 collective-permute-done.92
  478.5 9.6 collective-permute-done.94
  490.2 34.2 %ffn.6 = (bf16[4096,2048]{1,0:T(8,128)(2,1)}, bf16[384,2048]{1,0:T(8,128)(2,1)}, bf16[384,2048]{1,0:T(8,128)(2,1)}, bf16[384,768]{1,0:T(8,128)(2,1)}, bf16[384,7...) custom-call(s32[9]{0:T(128)} %get-tuple-element.1006.index, ...), custom_call_target="tpu_custom_call", output_to_operand_aliasing={{0}: (23, {})} | custom-call | flops 20000000000 | bytes 40000000 | tf_op jit(solution)/shard_map/ffn/pallas_call | solution.py:858
  531.0 7.6 collective-permute-done.99
  542.8 34.1 %ffn.7 = (bf16[4096,2048]{1,0:T(8,128)(2,1)}, bf16[384,2048]{1,0:T(8,128)(2,1)}, bf16[384,2048]{1,0:T(8,128)(2,1)}, bf16[384,768]{1,0:T(8,128)(2,1)}, bf16[384,7...) custom-call(s32[9]{0:T(128)} %get-tuple-element.1007.index, ...), custom_call_target="tpu_custom_call", output_to_operand_aliasing={{0}: (23, {})} | custom-call | flops 20000000000 | bytes 40000000 | tf_op jit(solution)/shard_map/ffn/pallas_call | solution.py:858
  603.7 7.3 collective-permute-done.109
  623.5 14.4 %collective-permute-done.114 = bf16[128,2176]{1,0:T(8,128)(2,1)S(1)} collective-permute-done((bf16[128,2176]{1,0:T(8,128)(2,1)S(1)}, bf16[128,2176]{1,0:T(8,128)(2,1)S(1)}, u32[]{:S(2)}, u32[]{:S(2)}) %collective-permute-start.114) | collective-permute-done | bytes 557088 | tf_op jit(solution)/shard_map/ppermute | solution.py:402
  654.9 6.5 fusion.6
  683.2 6.0 rows_grad.1
  693.8 18.5 %attend_back.1 = (bf16[1024,384]{1,0:T(8,128)(2,1)}, bf16[1024,512]{1,0:T(8,128)(2,1)}, bf16[128,640]{1,0:T(8,128)(2,1)}, bf16[128,640]{1,0:T(8,128)(2,1)}, bf16...) custom-call(s32[5]{0:T(128)} %stack.34.meta, ...), custom_call_target="tpu_custom_call" | custom-call | flops 14000000000 | bytes 24000000 | tf_op jit(solution)/shard_map/attend_back/pallas_call | solution.py:719
  728.6 6.5 convolution_convert_fusion.3
  782.7 108.2 %collective-permute-done.138 = bf16[128,2048]{1,0:T(8,128)(2,1)} collective-permute-done((bf16[128,2048]{1,0:T(8,128)(2,1)S(1)}, bf16[128,2048]{1,0:T(8,128)(2,1)}, u32[]{:S(2)}, u32[]{:S(2)}) %collective-permute-start.138) | collective-permute-done | bytes 524320 | tf_op jit(solution)/shard_map/ppermute | solution.py:389
  903.0 9.3 collective-permute-done.143
  919.8 7.6 collective-permute-start.149
  950.4 22.7 %collective-permute-done.147 = bf16[8,256,128]{2,1,0:T(8,128)(2,1)S(1)} collective-permute-done((bf16[8,256,128]{2,1,0:T(8,128)(2,1)S(1)}, bf16[8,256,128]{2,1,0:T(8,128)(2,1)S(1)}, u32[]{:S(2)}, u32[]{:S(2)}) %collective-permute-start.147) | collective-permute-done | bytes 524320 | tf_op jit(solution)/shard_map/ppermute | solution.py:402
  (849 shorter events, 443.0 us)
Async XLA Ops:
  7.2 90.9 %all-gather.2.cloned.1.call-start = ((), (), s32[]{:S(2)}) async-start(), calls=%async_computation.7 | async-start | bytes 2703360 | tf_op jit(solution)/shard_map/all_gather | solution.py:999
  7.9 56.1 %collective-permute-start.6 = (bf16[128,2048]{1,0:T(8,128)(2,1)}, bf16[128,2048]{1,0:T(8,128)(2,1)}, u32[]{:S(2)}, u32[]{:S(2)}) collective-permute-start(bf16[128,2048]{1,0:T(8,128)(2,1)} %bitcast.182), channel_id=1, source_target_pairs={{0,1},{1,0},{2,3},{3,2},{4,5},{5,4},{6,7},{7,6},{8,9},{9,8},{10,11... | collective-permute-start | bytes 1572872 | tf_op jit(solution)/shard_map/ppermute | solution.py:389
  139.9 40.7 %collective-permute-start.35 = (bf16[1024,704]{0,1:T(8,128)(2,1)}, bf16[1024,704]{0,1:T(8,128)(2,1)}, u32[]{:S(2)}, u32[]{:S(2)}) collective-permute-start(bf16[1024,704]{0,1:T(8,128)(2,1)} %copy.230), channel_id=1, source_target_pairs={{0,16},{16,0},{1,17},{17,1},{2,18},{18,2},{3,19},{19,3},{4,20},{20... | collective-permute-start | bytes 4325384 | tf_op jit(solution)/shard_map/ppermute | solution.py:389
  143.7 36.8 %collective-permute-start.31 = (bf16[128,2048]{1,0:T(8,128)(2,1)}, bf16[128,2048]{1,0:T(8,128)(2,1)S(1)}, u32[]{:S(2)}, u32[]{:S(2)}) collective-permute-start(bf16[128,2048]{1,0:T(8,128)(2,1)} %collective-permute-done.18.refs_10_), channel_id=1, source_target_pairs={{0,1},{1,0},{2,3},{3,2},{4,5},{5,4},{6,7},{7,6},{8,9},{9,8},{10,11... | collective-permute-start | bytes 1572872 | tf_op jit(solution)/shard_map/ppermute | solution.py:389
  221.9 89.2 %collective-permute-start.62 = (bf16[1024,704]{0,1:T(8,128)(2,1)}, bf16[1024,704]{0,1:T(8,128)(2,1)}, u32[]{:S(2)}, u32[]{:S(2)}) collective-permute-start(bf16[1024,704]{0,1:T(8,128)(2,1)} %copy.237), channel_id=1, source_target_pairs={{0,16},{16,0},{1,17},{17,1},{2,18},{18,2},{3,19},{19,3},{4,20},{20... | collective-permute-start | bytes 4325384 | tf_op jit(solution)/shard_map/ppermute | solution.py:389
  229.0 40.2 %collective-permute-start.50 = (bf16[128,2048]{1,0:T(8,128)(2,1)}, bf16[128,2048]{1,0:T(8,128)(2,1)}, u32[]{:S(2)}, u32[]{:S(2)}) collective-permute-start(bf16[128,2048]{1,0:T(8,128)(2,1)} %collective-permute-done.48.refs_8_), channel_id=1, source_target_pairs={{0,16},{16,0},{1,17},{17,1},{2,18},{18,2},{3,19},{19,3},{4,20},{20... | collective-permute-start | bytes 1572872 | tf_op jit(solution)/shard_map/ppermute | solution.py:389
  230.3 38.9 %collective-permute-start.49 = (bf16[128,2048]{1,0:T(8,128)(2,1)}, bf16[128,2048]{1,0:T(8,128)(2,1)}, u32[]{:S(2)}, u32[]{:S(2)}) collective-permute-start(bf16[128,2048]{1,0:T(8,128)(2,1)} %collective-permute-done.48.refs_8_), channel_id=1, source_target_pairs={{0,2},{2,0},{1,3},{3,1},{4,6},{6,4},{5,7},{7,5},{8,10},{10,8},{9,1... | collective-permute-start | bytes 1572872 | tf_op jit(solution)/shard_map/ppermute | solution.py:389
  274.9 65.0 %all-to-all-start.2 = ((bf16[32,64,176]{2,1,0:T(8,128)(2,1)}), bf16[32,64,176]{2,1,0:T(8,128)(2,1)}, u32[]{:S(2)}, u32[]{:S(2)}) async-start(bf16[32,64,176]{2,1,0:T(8,128)(2,1)} %pad_maximum_fusion.9), calls=%async_computation.2 | async-start | bytes 2097152 | tf_op jit(solution)/shard_map/all_to_all | solution.py:398
  280.9 721.6 %reduce-scatter.2.cloned.1.call-start = ((), (), s32[]{:S(2)}) async-start(), calls=%async_computation.8 | async-start | bytes 17301504 | tf_op jit(solution)/shard_map/reduce_scatter | solution.py:1228
  314.5 50.6 %collective-permute-start.65 = (bf16[128,2176]{1,0:T(8,128)(2,1)}, bf16[128,2176]{1,0:T(8,128)(2,1)}, u32[]{:S(2)}, u32[]{:S(2)}) collective-permute-start(bf16[128,2176]{1,0:T(8,128)(2,1)} %collective-permute-done.51.refs_2_), channel_id=1, source_target_pairs={{0,1},{1,0},{2,3},{3,2},{4,5},{5,4},{6,7},{7,6},{8,9},{9,8},{10,11... | collective-permute-start | bytes 1671176 | tf_op jit(solution)/shard_map/ppermute | solution.py:389
  378.8 41.5 %collective-permute-start.77 = (bf16[128,2176]{1,0:T(8,128)(2,1)}, bf16[128,2176]{1,0:T(8,128)(2,1)S(1)}, u32[]{:S(2)}, u32[]{:S(2)}) collective-permute-start(bf16[128,2176]{1,0:T(8,128)(2,1)} %collective-permute-done.68.refs_0_), channel_id=1, source_target_pairs={{0,1},{1,0},{2,3},{3,2},{4,5},{5,4},{6,7},{7,6},{8,9},{9,8},{10,11... | collective-permute-start | bytes 1671176 | tf_op jit(solution)/shard_map/ppermute | solution.py:389
  380.2 37.9 %collective-permute-start.75 = (bf16[128,2176]{1,0:T(8,128)(2,1)}, bf16[128,2176]{1,0:T(8,128)(2,1)}, u32[]{:S(2)}, u32[]{:S(2)}) collective-permute-start(bf16[128,2176]{1,0:T(8,128)(2,1)} %collective-permute-done.68.refs_0_), channel_id=1, source_target_pairs={{0,18},{2,16},{16,2},{18,0},{1,19},{3,17},{17,3},{19,1},{4,22},{6,... | collective-permute-start | bytes 1671176 | tf_op jit(solution)/shard_map/ppermute | solution.py:433
  380.7 37.4 %collective-permute-start.74 = (bf16[128,2176]{1,0:T(8,128)(2,1)}, bf16[128,2176]{1,0:T(8,128)(2,1)}, u32[]{:S(2)}, u32[]{:S(2)}) collective-permute-start(bf16[128,2176]{1,0:T(8,128)(2,1)} %collective-permute-done.68.refs_0_), channel_id=1, source_target_pairs={{0,2},{2,0},{1,3},{3,1},{4,6},{6,4},{5,7},{7,5},{8,10},{10,8},{9,1... | collective-permute-start | bytes 1671176 | tf_op jit(solution)/shard_map/ppermute | solution.py:389
  382.2 36.0 %collective-permute-start.73 = (bf16[128,2176]{1,0:T(8,128)(2,1)}, bf16[128,2176]{1,0:T(8,128)(2,1)S(1)}, u32[]{:S(2)}, u32[]{:S(2)}) collective-permute-start(bf16[128,2176]{1,0:T(8,128)(2,1)} %collective-permute-done.68.refs_0_), channel_id=1, source_target_pairs={{0,16},{16,0},{1,17},{17,1},{2,18},{18,2},{3,19},{19,3},{4,20},{20... | collective-permute-start | bytes 1671176 | tf_op jit(solution)/shard_map/ppermute | solution.py:389
  420.8 39.1 %collective-permute-start.83 = (bf16[128,2176]{1,0:T(8,128)(2,1)}, bf16[128,2176]{1,0:T(8,128)(2,1)}, u32[]{:S(2)}, u32[]{:S(2)}) collective-permute-start(bf16[128,2176]{1,0:T(8,128)(2,1)} %collective-permute-done.76.refs_0_), channel_id=1, source_target_pairs={{0,18},{2,16},{16,2},{18,0},{1,19},{3,17},{17,3},{19,1},{4,22},{6,... | collective-permute-start | bytes 1671176 | tf_op jit(solution)/shard_map/ppermute | solution.py:433
  421.6 38.3 %collective-permute-start.82 = (bf16[128,2176]{1,0:T(8,128)(2,1)}, bf16[128,2176]{1,0:T(8,128)(2,1)}, u32[]{:S(2)}, u32[]{:S(2)}) collective-permute-start(bf16[128,2176]{1,0:T(8,128)(2,1)} %collective-permute-done.76.refs_0_), channel_id=1, source_target_pairs={{0,2},{2,0},{1,3},{3,1},{4,6},{6,4},{5,7},{7,5},{8,10},{10,8},{9,1... | collective-permute-start | bytes 1671176 | tf_op jit(solution)/shard_map/ppermute | solution.py:389
  422.8 37.1 %collective-permute-start.81 = (bf16[128,2176]{1,0:T(8,128)(2,1)}, bf16[128,2176]{1,0:T(8,128)(2,1)}, u32[]{:S(2)}, u32[]{:S(2)}) collective-permute-start(bf16[128,2176]{1,0:T(8,128)(2,1)} %collective-permute-done.76.refs_0_), channel_id=1, source_target_pairs={{0,16},{16,0},{1,17},{17,1},{2,18},{18,2},{3,19},{19,3},{4,20},{20... | collective-permute-start | bytes 1671176 | tf_op jit(solution)/shard_map/ppermute | solution.py:389
  423.5 36.3 %collective-permute-start.79 = (bf16[128,2176]{1,0:T(8,128)(2,1)}, bf16[128,2176]{1,0:T(8,128)(2,1)}, u32[]{:S(2)}, u32[]{:S(2)}) collective-permute-start(bf16[128,2176]{1,0:T(8,128)(2,1)} %collective-permute-done.74.refs_2_), channel_id=1, source_target_pairs={{0,1},{1,0},{2,3},{3,2},{4,5},{5,4},{6,7},{7,6},{8,9},{9,8},{10,11... | collective-permute-start | bytes 1671176 | tf_op jit(solution)/shard_map/ppermute | solution.py:389
  475.1 49.3 %collective-permute-start.97 = (bf16[128,2176]{1,0:T(8,128)(2,1)}, bf16[128,2176]{1,0:T(8,128)(2,1)}, u32[]{:S(2)}, u32[]{:S(2)}) collective-permute-start(bf16[128,2176]{1,0:T(8,128)(2,1)} %get-tuple-element.642), channel_id=1, source_target_pairs={{0,1},{1,0},{2,3},{3,2},{4,5},{5,4},{6,7},{7,6},{8,9},{9,8},{10,11... | collective-permute-start | bytes 1671176 | tf_op jit(solution)/shard_map/ppermute | solution.py:389
  476.4 48.1 %collective-permute-start.98 = (bf16[128,2176]{1,0:T(8,128)(2,1)}, bf16[128,2176]{1,0:T(8,128)(2,1)}, u32[]{:S(2)}, u32[]{:S(2)}) collective-permute-start(bf16[128,2176]{1,0:T(8,128)(2,1)} %get-tuple-element.643), channel_id=1, source_target_pairs={{0,1},{1,0},{2,3},{3,2},{4,5},{5,4},{6,7},{7,6},{8,9},{9,8},{10,11... | collective-permute-start | bytes 1671176 | tf_op jit(solution)/shard_map/ppermute | solution.py:389
  488.1 36.4 %collective-permute-start.89 = (bf16[128,2176]{1,0:T(8,128)(2,1)}, bf16[128,2176]{1,0:T(8,128)(2,1)}, u32[]{:S(2)}, u32[]{:S(2)}) collective-permute-start(bf16[128,2176]{1,0:T(8,128)(2,1)} %collective-permute-done.81.refs_1_), channel_id=1, source_target_pairs={{0,1},{1,0},{2,3},{3,2},{4,5},{5,4},{6,7},{7,6},{8,9},{9,8},{10,11... | collective-permute-start | bytes 1671176 | tf_op jit(solution)/shard_map/ppermute | solution.py:389
  528.0 49.0 %collective-permute-start.101 = (bf16[128,2176]{1,0:T(8,128)(2,1)S(1)}, bf16[128,2176]{1,0:T(8,128)(2,1)}, u32[]{:S(2)}, u32[]{:S(2)}) collective-permute-start(bf16[128,2176]{1,0:T(8,128)(2,1)S(1)} %add_convert_fusion.10), channel_id=1, source_target_pairs={{0,18},{2,16},{16,2},{18,0},{1,19},{3,17},{17,3},{19,1},{4,22},{6,... | collective-permute-start | bytes 1671176 | tf_op jit(solution)/shard_map/ppermute | solution.py:433
  530.0 47.0 %collective-permute-start.102 = (bf16[128,2176]{1,0:T(8,128)(2,1)}, bf16[128,2176]{1,0:T(8,128)(2,1)}, u32[]{:S(2)}, u32[]{:S(2)}) collective-permute-start(bf16[128,2176]{1,0:T(8,128)(2,1)} %get-tuple-element.686), channel_id=1, source_target_pairs={{0,1},{1,0},{2,3},{3,2},{4,5},{5,4},{6,7},{7,6},{8,9},{9,8},{10,11... | collective-permute-start | bytes 1671176 | tf_op jit(solution)/shard_map/ppermute | solution.py:389
  531.0 46.0 %collective-permute-start.103 = (bf16[128,2176]{1,0:T(8,128)(2,1)}, bf16[128,2176]{1,0:T(8,128)(2,1)}, u32[]{:S(2)}, u32[]{:S(2)}) collective-permute-start(bf16[128,2176]{1,0:T(8,128)(2,1)} %get-tuple-element.687), channel_id=1, source_target_pairs={{0,1},{1,0},{2,3},{3,2},{4,5},{5,4},{6,7},{7,6},{8,9},{9,8},{10,11... | collective-permute-start | bytes 1671176 | tf_op jit(solution)/shard_map/ppermute | solution.py:389
  538.6 38.4 %collective-permute-start.104 = (bf16[128,2176]{1,0:T(8,128)(2,1)}, bf16[128,2176]{1,0:T(8,128)(2,1)}, u32[]{:S(2)}, u32[]{:S(2)}) collective-permute-start(bf16[128,2176]{1,0:T(8,128)(2,1)} %get-tuple-element.688), channel_id=1, source_target_pairs={{0,1},{1,0},{2,3},{3,2},{4,5},{5,4},{6,7},{7,6},{8,9},{9,8},{10,11... | collective-permute-start | bytes 1671176 | tf_op jit(solution)/shard_map/ppermute | solution.py:389
  540.4 36.7 %collective-permute-start.105 = (bf16[128,2176]{1,0:T(8,128)(2,1)}, bf16[128,2176]{1,0:T(8,128)(2,1)}, u32[]{:S(2)}, u32[]{:S(2)}) collective-permute-start(bf16[128,2176]{1,0:T(8,128)(2,1)} %get-tuple-element.689), channel_id=1, source_target_pairs={{0,1},{1,0},{2,3},{3,2},{4,5},{5,4},{6,7},{7,6},{8,9},{9,8},{10,11... | collective-permute-start | bytes 1671176 | tf_op jit(solution)/shard_map/ppermute | solution.py:389
  720.7 46.8 %all-to-all-start.5 = ((bf16[32,64,176]{2,1,0:T(8,128)(2,1)}), bf16[32,64,176]{2,1,0:T(8,128)(2,1)}, u32[]{:S(2)}, u32[]{:S(2)}) async-start(bf16[32,64,176]{2,1,0:T(8,128)(2,1)} %pad_maximum_fusion.10), calls=%async_computation.6 | async-start | bytes 2097152 | tf_op jit(solution)/shard_map/all_to_all | solution.py:398
  749.7 225.8 %collective-permute-start.157 = (bf16[1024,704]{0,1:T(8,128)(2,1)}, bf16[1024,704]{0,1:T(8,128)(2,1)}, u32[]{:S(2)}, u32[]{:S(2)}) collective-permute-start(bf16[1024,704]{0,1:T(8,128)(2,1)} %copy.248), channel_id=1, source_target_pairs={{0,16},{16,0},{1,17},{17,1},{2,18},{18,2},{3,19},{19,3},{4,20},{20... | collective-permute-start | bytes 4325384 | tf_op jit(solution)/shard_map/ppermute | solution.py:389
  751.1 224.4 %collective-permute-start.158 = (bf16[1024,704]{0,1:T(8,128)(2,1)}, bf16[1024,704]{0,1:T(8,128)(2,1)}, u32[]{:S(2)}, u32[]{:S(2)}) collective-permute-start(bf16[1024,704]{0,1:T(8,128)(2,1)} %copy.249), channel_id=1, source_target_pairs={{0,16},{16,0},{1,17},{17,1},{2,18},{18,2},{3,19},{19,3},{4,20},{20... | collective-permute-start | bytes 4325384 | tf_op jit(solution)/shard_map/ppermute | solution.py:389
  756.7 134.2 %collective-permute-start.138 = (bf16[128,2048]{1,0:T(8,128)(2,1)S(1)}, bf16[128,2048]{1,0:T(8,128)(2,1)}, u32[]{:S(2)}, u32[]{:S(2)}) collective-permute-start(bf16[128,2048]{1,0:T(8,128)(2,1)S(1)} %add_convert_fusion.18), channel_id=1, source_target_pairs={{0,16},{16,0},{1,17},{17,1},{2,18},{18,2},{3,19},{19,3},{4,20},{20... | collective-permute-start | bytes 1572872 | tf_op jit(solution)/shard_map/ppermute | solution.py:389
  780.1 119.0 %collective-permute-start.136 = (bf16[128,640]{1,0:T(8,128)(2,1)}, bf16[128,640]{1,0:T(8,128)(2,1)S(1)}, u32[]{:S(2)}, u32[]{:S(2)}) collective-permute-start(bf16[128,640]{1,0:T(8,128)(2,1)} %add_convert_fusion.25), channel_id=1, source_target_pairs={{0,2},{2,0},{1,3},{3,1},{4,6},{6,4},{5,7},{7,5},{8,10},{10,8},{9,1... | collective-permute-start | bytes 491528 | tf_op jit(solution)/shard_map/ppermute | solution.py:389
  782.6 116.6 %collective-permute-start.141 = (bf16[8,256,128]{2,1,0:T(8,128)(2,1)}, bf16[8,256,128]{2,1,0:T(8,128)(2,1)S(1)}, u32[]{:S(2)}, u32[]{:S(2)}) collective-permute-start(bf16[8,256,128]{2,1,0:T(8,128)(2,1)} %get-tuple-element.969), channel_id=1, source_target_pairs={{0,4},{4,8},{8,12},{12,0},{1,5},{5,9},{9,13},{13,1},{2,6},{6,10},{... | collective-permute-start | bytes 1572872 | tf_op jit(solution)/shard_map/ppermute | solution.py:402
  (293 other events, 3862.6 us)
Sparse Core Ops, SparseCore 0:
  10.9 69.3 all-gather.1
  689.4 204.5 reduce-scatter.1

commit v3 on v2

--- a/solution.py
+++ b/solution.py
@@ -429,51 +429,42 @@
     return (yield list(parts))
 
 
-def swap_both(value):
-    return lax.ppermute(value, ("y", "x"), [(i, 3 - i) for i in range(4)])
-
-
-def gather_hops(block, last=None):
-    if last is None:
-        near = yield [swap(block, "y"), swap(block, "x"), swap_both(block)]
-        near = [block, *near]
-        far = yield [swap(part, "c") for part in near]
-        return near + far
-    by_x, by_y = yield [swap(block, "x"), swap(block, "y")]
-    (diag,) = yield [swap(by_x, "y") if last == "y" else swap(by_y, "x")]
-    near = [block, by_y, by_x, diag]
-    far = yield [swap(part, "c") for part in near]
-    return near + far
+def finish(chain):
+    while not chain.ended:
+        chain.advance(chain.pending)
+    return chain.result
+
+
+def run(hops):
+    return finish(Chain(hops))
+
+
+def gather_hops(block):
+    (by_y,) = yield [swap(block, "y")]
+    pair = jnp.concatenate([block, by_y], axis=0)
+    (by_x,) = yield [swap(pair, "x")]
+    near = jnp.concatenate([pair, by_x], axis=0)
+    (far,) = yield [swap(near, "c")]
+    return near, far
 
 
 def add(*parts):
     return sum(part.astype(F32) for part in parts)
 
 
-def reduce_hops(parts, first):
-    got = yield [swap(part, "c") for part in parts[4:]]
-    diag = add(parts[3], got[3]).astype(BF)
-    if first is None:
-        came = yield [
-            swap(add(parts[1], got[1]).astype(BF), "y"),
-            swap(add(parts[2], got[2]).astype(BF), "x"),
-            swap_both(diag),
-        ]
-        return add(parts[0], got[0], *came)
-    if first == "y":
-        (got_diag,) = yield [swap(diag, "y")]
-        to_y = add(parts[1], got[1]).astype(BF)
-        to_x = add(parts[2], got[2], got_diag).astype(BF)
-    else:
-        (got_diag,) = yield [swap(diag, "x")]
-        to_x = add(parts[2], got[2]).astype(BF)
-        to_y = add(parts[1], got[1], got_diag).astype(BF)
-    got_x, got_y = yield [swap(to_x, "x"), swap(to_y, "y")]
-    return add(parts[0], got[0], got_x, got_y)
-
-
-def home_hops(parts, first, step):
-    total = yield from reduce_hops(parts, first)
+def reduce_hops(parts, links=("x", "y")):
+    near, far = parts
+    half = near.shape[0] // 2
+    (got,) = yield [swap(far, "c")]
+    pair = add(near[:half], got[:half])
+    (got,) = yield [swap(add(near[half:], got[half:]).astype(BF), links[0])]
+    pair = add(pair, got)
+    (got,) = yield [swap(pair[half // 2 :].astype(BF), links[1])]
+    return add(pair[: half // 2], got)
+
+
+def home_hops(parts, step, links=("x", "y")):
+    total = yield from reduce_hops(parts, links)
     if step:
         (total,) = yield [shift_z(total.astype(BF), -step)]
     return total
@@ -509,11 +500,13 @@
     return result
 
 
-def sum_hops(value):
+def sum_hops(value, at_once):
     came = [lax.dynamic_index_in_dim(value, at_plane(0), 0, keepdims=False)]
-    for step in (1, 3, 2):
-        part = lax.dynamic_index_in_dim(value, at_plane(step), 0, keepdims=False)
-        came += yield [shift_z(part, step)]
+    for steps in ((1, 2, 3),) if at_once else ((1,), (3,), (2,)):
+        came += yield [
+            shift_z(lax.dynamic_index_in_dim(value, at_plane(step), 0, keepdims=False), step)
+            for step in steps
+        ]
     return add(*came).astype(BF)
 
 
@@ -561,11 +554,11 @@
 
 
 def attend_kernel(meta, *refs):
-    tokens = refs[:8]
-    gain, latent_gain, wq, wl, we, cos_ref, sin_ref = refs[8:15]
-    h_ref, query_ref, latent_ref, rope_ref, expand_ref, attended_ref, raw_ref = refs[15:22]
+    tokens = refs[:2]
+    gain, latent_gain, wq, wl, we, cos_ref, sin_ref = refs[2:9]
+    h_ref, query_ref, latent_ref, rope_ref, expand_ref, attended_ref, raw_ref = refs[9:]
     for block in range(8):
-        value = tokens[block][...].astype(F32)
+        value = tokens[block // 4][pl.ds(block % 4 * ROWS, ROWS), :].astype(F32)
         inverse = lax.rsqrt(jnp.mean(value * value, axis=-1, keepdims=True) + EPSILON)
         h_ref[pl.ds(block * ROWS, ROWS), :] = (value * inverse * gain[...]).astype(BF)
 
@@ -611,8 +604,8 @@
     def project(step, carry):
         cols = columns(step, 256)
         part = jnp.dot(attended_ref[...], wo[:, cols], preferred_element_type=F32).astype(BF)
-        for block in range(8):
-            outs[block][:, cols] = part[block * ROWS : (block + 1) * ROWS]
+        outs[0][:, cols] = part[: 4 * ROWS]
+        outs[1][:, cols] = part[4 * ROWS :]
         return carry
 
     lax.fori_loop(0, wo.shape[1] // 256, project, 0)
@@ -623,8 +616,8 @@
     return pl.pallas_call(
         project_kernel,
         in_specs=[VMEM_SPEC] * 2,
-        out_specs=[VMEM_SPEC] * 8,
-        out_shape=[jax.ShapeDtypeStruct((ROWS, width), BF)] * 8,
+        out_specs=[VMEM_SPEC] * 2,
+        out_shape=[jax.ShapeDtypeStruct((4 * ROWS, width), BF)] * 2,
         compiler_params=pltpu.CompilerParams(vmem_limit_bytes=LIMIT),
         cost_estimate=pl.CostEstimate(
             flops=10**9, bytes_accessed=6 * 10**6, transcendentals=0
@@ -638,7 +631,7 @@
     shape = jax.ShapeDtypeStruct
     return pl.pallas_call(
         attend_kernel,
-        in_specs=[SMEM_SPEC] + [VMEM_SPEC] * 15,
+        in_specs=[SMEM_SPEC] + [VMEM_SPEC] * 9,
         out_specs=[VMEM_SPEC] * 7,
         out_shape=[
             shape((8 * ROWS, width), BF),
@@ -658,16 +651,16 @@
 
 
 def attend_back_kernel(meta, *refs):
-    douts = refs[:8]
-    query_ref, rope_ref, expand_ref, wq, we, wo, cos_ref, sin_ref = refs[8:16]
-    dq_ref, dkv_ref = refs[16:18]
-    lows = refs[18:26]
-    hats = refs[26:34]
-    dout_ref, datt_ref, low_ref = refs[34:37]
+    douts = refs[:2]
+    query_ref, rope_ref, expand_ref, wq, we, wo, cos_ref, sin_ref = refs[2:10]
+    dq_ref, dkv_ref = refs[10:12]
+    lows = refs[12:14]
+    hats = refs[14:16]
+    datt_ref, low_ref = refs[16:]
     scale = (NOPE + ROPE) ** (-0.5)
-    for block in range(8):
-        dout_ref[pl.ds(block * ROWS, ROWS), :] = douts[block][...]
-    datt_ref[...] = dot_nt(dout_ref[...], wo[...]).astype(BF)
+    for side in range(2):
+        rows = pl.ds(side * 4 * ROWS, 4 * ROWS)
+        datt_ref[rows, :] = dot_nt(douts[side][...], wo[...]).astype(BF)
 
     def sequence(seq, carry):
         rows = pl.ds(pl.multiple_of(seq * SEQ, SEQ), SEQ)
@@ -700,14 +693,14 @@
         return carry
 
     lax.fori_loop(0, 4, sequence, 0)
-    for block in range(8):
-        lows[block][...] = low_ref[pl.ds(block * ROWS, ROWS), :]
+    for side in range(2):
+        lows[side][...] = low_ref[pl.ds(side * 4 * ROWS, 4 * ROWS), :]
 
     def project(step, carry):
         cols = columns(step, 256)
         part = dot_nt(dq_ref[...], wq[cols, :]).astype(BF)
-        for block in range(8):
-            hats[block][:, cols] = part[block * ROWS : (block + 1) * ROWS]
+        hats[0][:, cols] = part[: 4 * ROWS]
+        hats[1][:, cols] = part[4 * ROWS :]
         return carry
 
     lax.fori_loop(0, wq.shape[0] // 256, project, 0)
@@ -718,16 +711,15 @@
     shape = jax.ShapeDtypeStruct
     out = pl.pallas_call(
         attend_back_kernel,
-        in_specs=[SMEM_SPEC] + [VMEM_SPEC] * 16,
-        out_specs=[VMEM_SPEC] * 18,
+        in_specs=[SMEM_SPEC] + [VMEM_SPEC] * 10,
+        out_specs=[VMEM_SPEC] * 6,
         out_shape=[
             shape((8 * ROWS, 384), BF),
             shape((8 * ROWS, 512), BF),
         ]
-        + [shape((ROWS, KVR + 128), BF)] * 8
-        + [shape((ROWS, width), BF)] * 8,
+        + [shape((4 * ROWS, KVR + 128), BF)] * 2
+        + [shape((4 * ROWS, width), BF)] * 2,
         scratch_shapes=[
-            pltpu.VMEM((8 * ROWS, width), BF),
             pltpu.VMEM((8 * ROWS, 256), BF),
             pltpu.VMEM((8 * ROWS, KVR + 128), BF),
         ],
@@ -737,7 +729,7 @@
         ),
         name="attend_back",
     )(meta, *douts, query, ropes, expand, wq, we, wo, cosine, sine)
-    return out[:2], out[2:10], out[10:]
+    return out[:2], out[2:4], out[4:]
 
 
 def taken_slots(slot_ref, index, block, cap):
@@ -746,20 +738,20 @@
 
 
 def ffn_kernel(index, *refs):
-    tokens = refs[:8]
-    grads = refs[8:16]
-    slot_ref, wg, wu, wd, si, sd = refs[16:22]
-    refs = refs[23:] if len(refs) == 48 else refs[22:]
-    out_ref, rows_ref, grows_ref, aw_ref, dg_ref, du_ref, dsi_ref, dsd_ref = refs[:8]
-    dhs = refs[8:16]
-    h_ref, g_ref, part_ref, pair_ref, drow_ref, dslot_ref, put_ref, weight_ref, sems = refs[16:25]
+    tokens = refs[:2]
+    grads = refs[2:4]
+    slot_ref, wg, wu, wd, si, sd = refs[4:10]
+    rows_ref, grows_ref, aw_ref, dg_ref, du_ref, dsi_ref, dsd_ref = refs[10:17]
+    dhs = refs[17:19]
+    outs = refs[19:21]
+    h_ref, g_ref, pair_ref, drow_ref, dslot_ref, put_ref, weight_ref, sems = refs[21:]
     cap = rows_ref.shape[0] // 8
     width = g_ref.shape[1]
     copies = []
-    for block in range(8):
-        here = pl.ds(block * ROWS, ROWS)
-        copies.append(pltpu.make_async_copy(tokens[block], h_ref.at[here, :], sems.at[block]))
-        copies.append(pltpu.make_async_copy(grads[block], g_ref.at[here, :], sems.at[8 + block]))
+    for side in range(2):
+        here = pl.ds(side * 4 * ROWS, 4 * ROWS)
+        copies.append(pltpu.make_async_copy(tokens[side], h_ref.at[here, :], sems.at[side]))
+        copies.append(pltpu.make_async_copy(grads[side], g_ref.at[here, :], sems.at[2 + side]))
     for copy in copies:
         copy.start()
     for copy in copies:
@@ -798,7 +790,7 @@
     ).astype(BF)
     for block in range(8):
         here = pl.ds(block * ROWS, ROWS)
-        dhs[block][:, width:] = jnp.dot(
+        dhs[block // 4][pl.ds(block % 4 * ROWS, ROWS), width:] = jnp.dot(
             put_ref[here, :cap], dslot_ref[pl.ds(block * cap, cap), :], preferred_element_type=F32
         ).astype(BF)
     shared = jnp.dot(h_ref[:, :width], si[...], preferred_element_type=F32)
@@ -823,12 +815,14 @@
         for block in range(8):
             here = slice(block * ROWS, (block + 1) * ROWS)
             inside = slice(block * cap, (block + 1) * cap)
+            half = pl.ds(block % 4 * ROWS, ROWS)
             put = put_ref[here, :cap]
-            part_ref[here, cols] = (
+            place = pl.ds((0, 2, 1, 3)[block % 4] * ROWS, ROWS)
+            outs[block // 4][place, cols] = (
                 from_shared[here]
                 + jnp.dot(put, pair_ref[inside, :], preferred_element_type=F32)
             ).astype(BF)
-            dhs[block][:, cols] = (
+            dhs[block // 4][half, cols] = (
                 back_shared[here]
                 + jnp.dot(put, drow_ref[inside, :], preferred_element_type=F32)
             ).astype(BF)
@@ -837,30 +831,17 @@
         return carry
 
     lax.fori_loop(0, width // 256, tile, 0)
-    copies = []
-    for block in range(8):
-        here = pl.ds(block * ROWS, ROWS)
-        there = pl.ds(pl.multiple_of(index[block] * ROWS, ROWS), ROWS)
-        copies.append(
-            pltpu.make_async_copy(part_ref.at[here, :], out_ref.at[there, :], sems.at[block])
-        )
-    for copy in copies:
-        copy.start()
-    for copy in copies:
-        copy.wait()
-
-
-def ffn(index, tokens, grads, slot_of, weights, out, cap):
+
+
+def ffn(index, tokens, grads, slot_of, weights, cap):
     width = grads[0].shape[1]
     hidden = weights[0].shape[1]
     shape = jax.ShapeDtypeStruct
-    alias = [] if out is None else [out]
     result = pl.pallas_call(
         ffn_kernel,
-        in_specs=[SMEM_SPEC] + [ANY_SPEC] * 16 + [VMEM_SPEC] * 6 + [ANY_SPEC] * len(alias),
-        out_specs=[ANY_SPEC] + [VMEM_SPEC] * 15,
+        in_specs=[SMEM_SPEC] + [ANY_SPEC] * 4 + [VMEM_SPEC] * 6,
+        out_specs=[VMEM_SPEC] * 11,
         out_shape=[
-            shape((32 * ROWS, width), BF),
             shape((8 * cap, width), BF),
             shape((8 * cap, width), BF),
             shape((8 * cap, hidden), BF),
@@ -869,48 +850,43 @@
             shape((256, width), F32),
             shape((128, width), F32),
         ]
-        + [shape((ROWS, width + 128), BF)] * 8,
+        + [shape((4 * ROWS, width + 128), BF)] * 2
+        + [shape((4 * ROWS, width), BF)] * 2,
         scratch_shapes=[
             pltpu.VMEM((8 * ROWS, width + 128), BF),
-            pltpu.VMEM((8 * ROWS, width), BF),
             pltpu.VMEM((8 * ROWS, width), BF),
             pltpu.VMEM((8 * cap, 256), BF),
             pltpu.VMEM((8 * cap, 256), BF),
             pltpu.VMEM((8 * cap, ROWS), BF),
             pltpu.VMEM((8 * ROWS, ROWS), BF),
             pltpu.VMEM((8 * cap, ROWS), F32),
-            pltpu.SemaphoreType.DMA((16,)),
+            pltpu.SemaphoreType.DMA((4,)),
         ],
-        input_output_aliases={23: 0} if alias else {},
         compiler_params=pltpu.CompilerParams(vmem_limit_bytes=LIMIT),
         cost_estimate=pl.CostEstimate(
             flops=20 * 10**9, bytes_accessed=40 * 10**6, transcendentals=10**6
         ),
         name="ffn",
-    )(index, *tokens, *grads, slot_of, *weights, *alias)
-    return result[0], result[1:8], result[8:]
-
-
-def rows_grad_kernel(left_ref, *refs):
-    out_ref = refs[8]
+    )(index, *tokens, *grads, slot_of, *weights)
+    return result[:7], result[7:9], result[9:]
+
+
+def rows_grad_kernel(left_ref, near_ref, far_ref, out_ref):
     turned = left_ref[...].T
-    total = jnp.zeros(out_ref.shape, F32)
-    for block in range(8):
-        total = total + jnp.dot(
-            turned[:, block * ROWS : (block + 1) * ROWS],
-            refs[block][...],
-            preferred_element_type=F32,
-        )
-    out_ref[...] = total.astype(BF)
-
-
-def rows_grad(left, blocks):
-    width = blocks[0].shape[1]
+    half = near_ref.shape[0]
+    out_ref[...] = (
+        jnp.dot(turned[:, :half], near_ref[...], preferred_element_type=F32)
+        + jnp.dot(turned[:, half:], far_ref[...], preferred_element_type=F32)
+    ).astype(BF)
+
+
+def rows_grad(left, rows):
+    width = rows[0].shape[1]
     return pl.pallas_call(
         rows_grad_kernel,
         grid=(width // 512,),
         in_specs=[pl.BlockSpec(left.shape, lambda t: (0, 0))]
-        + [pl.BlockSpec((ROWS, 512), lambda t: (0, t))] * 8,
+        + [pl.BlockSpec((4 * ROWS, 512), lambda t: (0, t))] * 2,
         out_specs=pl.BlockSpec((left.shape[1], 512), lambda t: (0, t)),
         out_shape=jax.ShapeDtypeStruct((left.shape[1], width), BF),
         compiler_params=pltpu.CompilerParams(vmem_limit_bytes=LIMIT),
@@ -918,7 +894,7 @@
             flops=10**9, bytes_accessed=6 * 10**6, transcendentals=0
         ),
         name="rows_grad",
-    )(left, *blocks)
+    )(left, *rows)
 
 
 def local_tokens(
@@ -1008,34 +984,36 @@
     def widen_columns(value, amount):
         return jnp.pad(value, ((0, 0), (0, amount)))
 
-    own_low = own_tokens
-    tokens_go = Chain(gather_hops(own_low, "y"))
-    below_go = Chain(one_hop(shift_z(grad_low, 1)))
-    packed = spread(packed, PLANE)
-    packed, grad_low, w_output = tick((packed, grad_low, w_output), tokens_go, below_go)
-    packed_go = Chain(line_hops(packed))
-    zq_go = Chain(one_hop(swap_zq(w_output)))
-    small = spread(to_each, ALL)
-    grad_low, small = tick((grad_low, small), tokens_go, packed_go)
-    grads_go = [Chain(gather_hops(grad_low, "x"))]
-    grad_low, expert_gate, wl_all = tick(
-        (grad_low, expert_gate, wl_all), tokens_go, packed_go, zq_go, grads_go[0]
-    )
-
     def halves(value):
         first, second = value[0, :, :n_half], value[0, :, n_half:]
         mine = jnp.where(my_y == 0, first, second)
-        return mine, Chain(one_hop(swap(jnp.where(my_y == 0, second, first), "y")))
-
-    def whole_rows(mine, chain):
-        other = chain.result[0]
+        return mine, swap(jnp.where(my_y == 0, second, first), "y")
+
+    def whole_rows(mine, other):
         both = jnp.concatenate(
             [jnp.where(my_y == 0, mine, other), jnp.where(my_y == 0, other, mine)], axis=0
         )
         return widen_columns(both, half_pad)
 
+    def hidden_columns(value):
+        return jnp.transpose(value.reshape(value.shape[0], n_dev, n_shared), (1, 0, 2))
+
+    tokens_go = Chain(gather_hops(own_tokens))
+    below_go = Chain(one_hop(shift_z(grad_low, 1)))
+    packed = spread(packed, PLANE)
+    packed, grad_low, w_output, expert_gate = tick(
+        (packed, grad_low, w_output, expert_gate), tokens_go, below_go
+    )
+    packed_go = Chain(line_hops(packed))
+    small = spread(to_each, ALL)
+    grad_low = tick(grad_low, tokens_go, packed_go)
+    grads_here = Chain(gather_hops(grad_low))
+    small, grad_low, wl_all, expert_gate = tick(
+        (small, grad_low, wl_all, expert_gate), tokens_go, packed_go, grads_here
+    )
+    tokens_here = tokens_go.result
     gate_mine, gate_go = halves(expert_gate)
-    grads_go.append(Chain(gather_hops(below_go.result[0], "y")))
+    zq = swap_zq(w_output)
     latent_at = jnp.arange(KVR + 256)
     lane = (latent_at - KVR) % 128
     head = (latent_at - KVR) // 128
@@ -1046,8 +1024,9 @@
     )
     widen = (jnp.arange(KVR + ROPE)[:, None] == latent_from[None, :]).astype(BF)
     wl = matrix_product(wl_all, widen).astype(BF)
-    grad_low, wl = tick((grad_low, wl), packed_go, grads_go[0], grads_go[1])
-
+    grad_low, wl, gate_mine, zq = tick((grad_low, wl, gate_mine, zq), packed_go, grads_here)
+    packed = packed_go.result
+    below_go = Chain(gather_hops(below_go.result[0]))
     cuts = [sum(n_small[: i + 1]) for i in range(len(n_small))]
     slot_of = small[:, : cuts[0]].astype(F32)
     attention_gain = small[:, cuts[0] : cuts[1]].reshape(-1).astype(F32)
@@ -1055,7 +1034,6 @@
     latent_gain = small[:, cuts[2] : cuts[3]].reshape(-1).astype(F32)
     lengths = small[:16, cuts[3]].astype(jnp.int32)
     router = small[:, cuts[4] : cuts[5]].reshape(width, n_experts)
-    packed = packed_go.result
     wq = natural_rows(packed[:, :, :query_rows], w_query.shape[0])
     we = natural_rows(packed[:, :, query_rows:], w_expand.shape[0])
     target = jnp.arange(384)
@@ -1084,34 +1062,32 @@
             my_y.astype(jnp.int32),
         ]
     )
+    start = (wq, wl, we, meta, grad_low, zq, expert_up, shared_gate, shared_up)
+    start = tick(start, grads_here, below_go)
+    wq, wl, we, meta, grad_low, zq, expert_up, shared_gate, shared_up = start
+    up_mine, up_go = halves(expert_up)
+
+    wo = run(direct_hops(zq)).reshape(2 * VDIM, width)
     above_go = Chain(one_hop(shift_z(grad_low, -1)))
-    wq, wl, we, meta, grad_low, expert_up = tick(
-        (wq, wl, we, meta, grad_low, expert_up), grads_go[0], grads_go[1], above_go
-    )
-
-    wo_go = Chain(direct_hops(zq_go.result[0]))
-    grads_go.append(Chain(gather_hops(above_go.result[0], "x")))
-    up_mine, up_go = halves(expert_up)
     kept_values = attend(
-        meta, tokens_go.result, attention_gain, latent_gain, wq, wl, we, cos_pair, sin_pair
-    )
-    kept_values, grad_low, shared_gate, shared_up = tick(
-        (kept_values, grad_low, shared_gate, shared_up), wo_go, grads_go[1], grads_go[2], gate_go
-    )
+        meta, tokens_here, attention_gain, latent_gain, wq, wl, we, cos_pair, sin_pair
+    )
+    kept_values, up_mine, grad_low, gate_go = tick(
+        (kept_values, up_mine, grad_low, gate_go), above_go, below_go
+    )
+    shared_both = spread(
+        jnp.concatenate([hidden_columns(shared_gate), hidden_columns(shared_up)], axis=2), ALL
+    )
+    across_go = Chain(one_hop(shift_z(grad_low, 2)))
+    above_go = Chain(gather_hops(above_go.result[0]))
     h_attn, query, latent, ropes, expand, attended, latent_raw = kept_values
-    wo = wo_go.result.reshape(2 * VDIM, width)
-    attended_parts = project(attended, wo)
-
-    def hidden_columns(value):
-        return jnp.transpose(value.reshape(value.shape[0], n_dev, n_shared), (1, 0, 2))
-
-    attended_parts = tick(attended_parts, grads_go[2])
-    middle_go = Chain(reduce_hops(attended_parts, "y"))
-    across_go = Chain(one_hop(shift_z(grad_low, 2)))
+    attended_parts = tick(project(attended, wo), above_go, below_go)
+    grads_here = [grads_here.result, below_go.result]
+    middle_go = Chain(reduce_hops(attended_parts))
     tick((), middle_go)
-    tick((), middle_go, grads_go[2])
-    tick((), middle_go, across_go)
-    grads_go.append(Chain(gather_hops(across_go.result[0], "y")))
+    up_go, shared_both = tick((up_go, shared_both), middle_go)
+    tick((), middle_go, above_go, across_go)
+    across_go = Chain(gather_hops(across_go.result[0]))
     middle = input_rows + middle_go.result
 
     h_ffn = rms_norm(middle, feedforward_gain).astype(BF)
@@ -1123,22 +1099,14 @@
     gates_rest = jnp.zeros((tok, 128 - 3 * n_experts), BF)
     sent = jnp.concatenate([h_ffn, gates_high, gates_middle, gates_low, gates_rest], axis=1)
 
-    sent, shared_gate, shared_up = tick((sent, shared_gate, shared_up), grads_go[3])
-    shared_both = spread(
-        jnp.concatenate([hidden_columns(shared_gate), hidden_columns(shared_up)], axis=2), ALL
-    )
-    go = [Chain(gather_hops(sent, "y"))]
+    sent = tick(sent, above_go, across_go)
+    go = [Chain(gather_hops(sent))]
     below_go = Chain(one_hop(shift_z(sent, 1)))
     gate_w = whole_rows(gate_mine, gate_go)
     down_w = jnp.pad(expert_down[0], ((0, half_pad), (0, 0)))
-    sent, gate_w, down_w = tick((sent, gate_w, down_w), go[0], grads_go[3], below_go)
-    across_go = Chain(one_hop(shift_z(sent, 2)))
-    go.append(Chain(gather_hops(below_go.result[0], "x")))
-    shared_out = jnp.pad(shared_down, ((0, shared_pad), (0, 0)))
-    sent, shared_both, shared_out = tick(
-        (sent, shared_both, shared_out), go[0], go[1], grads_go[3], up_go
-    )
-    above_go = Chain(one_hop(shift_z(sent, -1)))
+    sent, gate_w, down_w = tick((sent, gate_w, down_w), go[0], below_go, across_go)
+    across_sent = Chain(one_hop(shift_z(sent, 2)))
+    go.append(Chain(gather_hops(below_go.result[0])))
     shared_both = shared_both.reshape(width, 2 * n_shared)
     shared_in = jnp.concatenate(
         [
@@ -1147,10 +1115,17 @@
         ],
         axis=1,
     )
+    shared_out = jnp.pad(shared_down, ((0, shared_pad), (0, 0)))
+    sent, shared_in, shared_out = tick(
+        (sent, shared_in, shared_out), go[0], go[1], across_sent, across_go
+    )
+    above_sent = Chain(one_hop(shift_z(sent, -1)))
+    go.append(Chain(gather_hops(across_sent.result[0])))
     weights = (gate_w, whole_rows(up_mine, up_go), down_w, shared_in, shared_out)
-    weights = tick(weights, go[0], go[1], across_go)
-    go.append(Chain(gather_hops(across_go.result[0])))
-    grads_go = [grads_go[0], grads_go[1], grads_go[3], grads_go[2]]
+    weights = tick(weights, go[0], go[1], go[2], above_sent)
+    go.append(Chain(gather_hops(above_sent.result[0])))
+    grads_here.append(across_go.result)
+    grads_here.append(above_go.result)
 
     plane = jnp.stack(
         [
@@ -1162,21 +1137,19 @@
     ).astype(jnp.int32)
     saved = []
     homes = []
-    out_part = None
+    outs = []
     for number in range(4):
         index = plane + (my_z - STEPS[number]) % 4 * 4
         index = jnp.concatenate([index, my_seq[None].astype(jnp.int32)])
         results = ffn(
-            index, go[number].result, grads_go[number].result, slot_of, weights, out_part, capacity
+            index, go[number].result, grads_here[number], slot_of, weights, capacity
         )
-        more = [above_go] if number == 0 else []
-        out_part, kept_here, d_h_parts, weights = tick(
-            results + (weights,), *go[number + 1 :], *homes, *more
+        kept_here, d_h_parts, out_parts, weights = tick(
+            results + (weights,), *go[number + 1 :], *homes, *outs[number // 3 :]
         )
-        if number == 0:
-            go.append(Chain(gather_hops(above_go.result[0])))
         saved.append(kept_here)
-        homes.append(Chain(home_hops(d_h_parts, None, STEPS[number])))
+        homes.append(Chain(home_hops(d_h_parts, STEPS[number])))
+        outs.append(Chain(home_hops(out_parts, STEPS[number], ("y", "x"))))
 
     rows, grad_rows, act_weighted, d_gate_val, d_up_val = (
         jnp.concatenate([item[i] for item in saved], axis=0) for i in range(5)
@@ -1185,25 +1158,19 @@
     def column_halves(left, right):
         value = dot_tn(left, right)[:, :n_half].astype(BF)
         first, second = value[: width // 2], value[width // 2 :]
-        mine = jnp.where(my_y == 0, first, second)
-        return mine, Chain(one_hop(swap(jnp.where(my_y == 0, second, first), "y")))
-
-    def whole_columns(mine, chain):
-        other = chain.result[0]
+        return jnp.where(my_y == 0, first, second), jnp.where(my_y == 0, second, first)
+
+    def whole_columns(mine, other):
         return jnp.concatenate(
             [jnp.where(my_y == 0, mine, other), jnp.where(my_y == 0, other, mine)], axis=1
         ).astype(F32)
 
-    rows, grad_rows = tick((rows, grad_rows), *homes)
+    rows, grad_rows = tick((rows, grad_rows), *homes, outs[3])
     d_gate_mine, d_gate_go = column_halves(rows, d_gate_val)
     rows, d_gate_mine, grad_rows = tick((rows, d_gate_mine, grad_rows), *homes)
     d_up_mine, d_up_go = column_halves(rows, d_up_val)
-    d_up_mine, grad_rows = tick((d_up_mine, grad_rows), *homes)
-    d_shared_in = sum(item[5] for item in saved).astype(BF).T.reshape(n_dev, width // n_dev, 256)
-    d_shared_in = jnp.concatenate(
-        [d_shared_in[..., :n_shared], d_shared_in[..., 128 : 128 + n_shared]], axis=2
-    )
-    d_shared_down = sum(item[6] for item in saved)[:n_shared]
+    d_up_mine, grad_rows = tick((d_up_mine, grad_rows), *homes, outs[1])
+    grad_rows = tick(grad_rows, *homes, outs[0])
     d_h_ffn = add(*(home.result for home in homes))
     d_gates = d_h_ffn[:, width : width + n_experts] + d_h_ffn[:, width + 64 : width + 64 + n_experts]
     d_h_ffn = d_h_ffn[:, :width]
@@ -1216,29 +1183,30 @@
     grad_mid = grad_y + d_mid_norm
 
     grad_mid = tick(grad_mid)
-    douts_go = Chain(gather_hops(grad_mid.astype(BF), "y"))
+    douts_go = Chain(gather_hops(grad_mid.astype(BF)))
     d_down_w = dot_tn(act_weighted, grad_rows)[:n_half]
-    d_down_w = tick(d_down_w, douts_go)
-    d_shared_in = tick(d_shared_in, douts_go)
+    d_down_w = tick(d_down_w, douts_go, outs[1])
     d_router = jnp.dot(h_ffn.astype(F32).T, d_logits, precision=lax.Precision.HIGHEST)
-    d_router = tick(d_router, douts_go)
+    d_router, d_gate_go = tick((d_router, d_gate_go), douts_go)
+    d_gate_go = swap(d_gate_go, "y")
+    d_gate_mine = tick(d_gate_mine, douts_go)
     d_wo = rows_grad(attended, douts_go.result)
-    d_wo, out_part = tick((d_wo, out_part))
-    wo_go = Chain(sum_hops(d_wo.reshape(4, -1, width)))
-    output = lax.psum_scatter(out_part, ALL, scatter_dimension=0, tiled=True)
+    d_wo = tick(d_wo)
+    wo_go = Chain(sum_hops(d_wo.reshape(4, -1, width), True))
     (d_query, d_expand), low_parts, hat_parts = tick(
         attend_back(
             meta, douts_go.result, query, ropes, expand, wq, we, wo, cos_pair, sin_pair
         ),
         wo_go,
+        outs[2],
     )
 
     def by_owner(value, rows_each):
         view = value.astype(BF).reshape(2, 4, 4, rows_each, -1, ROWS)
         return jnp.transpose(view, (1, 0, 2, 4, 3, 5)).reshape(4, 8, -1, ROWS)
 
-    low_go = Chain(reduce_hops(low_parts, "x"))
-    hat_go = Chain(reduce_hops(hat_parts, "y"))
+    low_go = Chain(reduce_hops(low_parts))
+    hat_go = Chain(reduce_hops(hat_parts))
     d_query = dot_nt(d_query, reorder).astype(BF)
     d_packed = jnp.concatenate(
         [
@@ -1247,17 +1215,25 @@
         ],
         axis=2,
     )
-    d_packed = tick(d_packed, low_go, hat_go, wo_go)
-    packed_go = Chain(sum_hops(d_packed))
-    tick((), low_go, hat_go, wo_go)
-    tick((), low_go, packed_go)
+    d_packed, shared_sums, d_gate_go, d_up_go = tick(
+        (d_packed, [item[5:7] for item in saved], d_gate_go, d_up_go), low_go, hat_go, outs[2]
+    )
+    d_up_go = swap(d_up_go, "y")
+    d_packed = run(sum_hops(d_packed, True))
+    d_shared_in = sum(item[0] for item in shared_sums).astype(BF).T
+    d_shared_in = d_shared_in.reshape(n_dev, width // n_dev, 256)
+    d_shared_in = jnp.concatenate(
+        [d_shared_in[..., :n_shared], d_shared_in[..., 128 : 128 + n_shared]], axis=2
+    )
+    d_shared_in, d_up_go = tick((d_shared_in, d_up_go), low_go, hat_go)
+    d_shared_down = sum(item[1] for item in shared_sums)[:n_shared]
+    d_shared_down = tick(d_shared_down, low_go, hat_go, outs[3])
     d_low = low_go.result
     d_latent_raw, d_g_latent = norm_back(latent_raw, latent_gain, d_low[:, :KVR])
     d_rope = jnp.concatenate([d_low[:, KVR : KVR + 32], d_low[:, KVR + 64 : KVR + 96]], axis=1)
     d_rope_raw = rotate_back(d_rope, cos_own, sin_own)
     d_latent_in = jnp.concatenate([d_latent_raw, d_rope_raw], axis=-1).astype(BF)
-    d_latent_in = tick(d_latent_in, hat_go, packed_go)
-    dlat_go = Chain(gather_hops(d_latent_in, "x"))
+    dlat_here = run(gather_hops(d_latent_in))
     d_hattn = hat_go.result + dot_nt(d_latent_in, wl_all)
     d_in_norm, d_g_attn = norm_back(input_rows, attention_gain, d_hattn)
     input_grad = (grad_mid + d_in_norm).astype(BF)
@@ -1265,21 +1241,18 @@
     small_grads = jnp.concatenate(
         [early, d_g_attn.reshape(n_dev, -1), d_g_latent.reshape(n_dev, -1)], axis=1
     )
-    input_grad, small_grads = tick((input_grad, small_grads), dlat_go)
-    tick((), dlat_go)
-    tick((), dlat_go, zq_back := Chain(one_hop(swap_zq(wo_go.result))))
+    small_grads = spread(small_grads, ALL)
+    wo_back = swap_zq(wo_go.result)
     my_pair = my_y * 4 + my_x * 2 + my_c
     part_cols = w_latent.shape[1] // PAIRS
-    plane_dlat = jnp.concatenate(dlat_go.result, axis=0)
+    plane_dlat = jnp.concatenate(dlat_here, axis=0)
     d_columns = lax.dynamic_slice_in_dim(
         widen_columns(plane_dlat, 64), my_pair * part_cols, ROWS, axis=1
     )
-    latent_go = Chain(sum_hops(by_owner(dot_tn(h_attn, d_columns), w_latent.shape[0])))
-    tick((), packed_go, latent_go)
-    tick((), latent_go)
-    tick((), latent_go, d_gate_go, d_up_go)
+    latent_go = Chain(sum_hops(by_owner(dot_tn(h_attn, d_columns), w_latent.shape[0]), True))
+    d_packed = tick(d_packed, latent_go, outs[2], outs[3])
     d_packed = spread(
-        jnp.concatenate([packed_go.result, latent_go.result], axis=1), PLANE
+        jnp.concatenate([d_packed, latent_go.result], axis=1), PLANE
     ).astype(F32)
     split = w_query.shape[0] * 3
     wq_grad = jnp.transpose(
@@ -1292,7 +1265,7 @@
     wl_grad = jnp.transpose(
         d_packed[:, -w_latent.shape[0] :, :part_cols], (1, 0, 2)
     ).reshape(w_latent.shape)
-    wo_grad = zq_back.result[0].astype(F32)
+    wo_grad = wo_back.astype(F32)
     d_shared_in = spread(d_shared_in, ALL).astype(F32)
 
     def shared_columns(value):
@@ -1302,8 +1275,8 @@
     d_shared_up = shared_columns(d_shared_in[..., n_shared:])
     d_expert_gate = whole_columns(d_gate_mine, d_gate_go)
     d_expert_up = whole_columns(d_up_mine, d_up_go)
-    output = (middle + output.astype(F32)).astype(BF)
-    small_grads = jnp.sum(spread(small_grads, ALL), axis=0)
+    output = add(middle, *(finish(out) for out in outs)).astype(BF)
+    small_grads = jnp.sum(small_grads, axis=0)
     rows_each = width // n_dev
     gffn_grad = small_grads[:rows_each]
     router_grad = small_grads[rows_each : rows_each * (1 + n_experts)].reshape(rows_each, n_experts)

time: 1020 us -> 1010 us (level)
  waiting for transfers between devices: 372 us -> 305 us
  other arithmetic: 88.5 us -> 137 us
  local copies, waits for them, and re-layouts: 93.6 us -> 132 us
  starting transfers between devices: 207 us -> 169 us
  blocking collectives: 0 us -> 13 us
    ppermute x124 -> x70, waiting for transfers between devices: 236 us -> 161 us  [swap(): return lax.ppermute(value, axis, [(0, 1), (1, 0)])]
    ppermute x124 -> x70, starting transfers between devices: 125 us -> 74.6 us  [swap(): return lax.ppermute(value, axis, [(0, 1), (1, 0)])]
    all_to_all x6 -> x5, waiting for transfers between devices: 12.4 us -> 45.6 us  [spread(): return lax.all_to_all(value, axes, split_axis=0, concat_axis=0, tiled=True)]
    add x2 -> x13, other arithmetic: 1.54 us -> 24.9 us  [add(): return sum((part.astype(F32) for part in parts))]
    ppermute x6 -> x0, waiting for transfers between devices: 16.9 us -> none  [swap_both(): return lax.ppermute(value, ('y', 'x'), [(i, 3 - i) for i in range(4)])]
    concatenate x1 -> x10, local copies, waits for them, and re-layouts: 0.02 us -> 14.6 us  [the longest x9 13.8 us: gather_hops(): near = jnp.concatenate([pair, by_x], axis=0)]
    concatenate x1 -> x15, other arithmetic: 0.88 us -> 14.4 us  [the longest x11 8.13 us: gather_hops(): pair = jnp.concatenate([block, by_y], axis=0)]
    all_to_all x0 -> x1, blocking collectives: none -> 13 us  [spread(): return lax.all_to_all(value, axes, split_axis=0, concat_axis=0, tiled=True)]
  transfers between devices with their start and end apart: 167 -> 108, of which waited for: 45 -> 36; matrix products, arithmetic and copies ran while one was open for 21% -> 27% of each run, Pallas kernels for 18% -> 18%
where the time goes in v3:
time: 1010 us; the launch traced here: 998 us
  waiting for transfers between devices  305 us (30%)
  Pallas kernels  178 us (18%)
  starting transfers between devices  169 us (17%)
  other arithmetic  137 us (14%)
  local copies, waits for them, and re-layouts  132 us (13%)
  matrix products  46 us (5%)
  between operations  17.5 us (2%)
  blocking collectives  13 us (1%)
    ppermute x70, waiting for transfers between devices, swap(): return lax.ppermute(value, axis, [(0, 1), (1, 0)])  161 us
    pallas_call x4, Pallas kernels, ffn(): pl.pallas_call(ffn_kernel, in_specs=[SMEM_SPEC] + [ANY_SPEC] * 4 + [VMEM_...  129 us
    ppermute x24, waiting for transfers between devices, shift_z(): return lax.ppermute(value, 'z', [(i, (i + step) % 4) for i in range(4)])  78.9 us
    ppermute x70, starting transfers between devices, swap(): return lax.ppermute(value, axis, [(0, 1), (1, 0)])  74.6 us
    all_to_all x5, waiting for transfers between devices, spread(): return lax.all_to_all(value, axes, split_axis=0, concat_axis=0, tiled=True)  45.6 us
    ppermute x24, starting transfers between devices, shift_z(): return lax.ppermute(value, 'z', [(i, (i + step) % 4) for i in range(4)])  37.8 us
    dot_general x6, matrix products, dot_tn(): lax.dot_general(left, right, (((0,), (0,)), ((), ())), preferred_element_...  32.5 us
    unnamed x268, local copies, waits for them, and re-layouts  31 us
  transfers between devices with their start and end apart: 108, of which 36 were waited for; matrix products, arithmetic and copies ran while one was open for 27% of the time, Pallas kernels for 18%

profile of v3, /device:TPU:1, one launch (start us, length us, event | category | flops | bytes accessed | tf_op | source)
XLA Modules:
  0.0 997.9 jit_solution(16880014518946380193)
XLA Ops:
  14.9 13.0 %all_to_all.41 = bf16[8,256,128]{2,1,0:T(8,128)(2,1)S(1)} all-to-all(bf16[8,256,128]{2,1,0:T(8,128)(2,1)S(1)} %pad_maximum_fusion.25), channel_id=1, replica_groups=mesh['y'=2,'z'=4,'x'=2,'c'=2] {'y','x','c'}, dimensions={0} | all-to-all | bytes 1048576 | tf_op jit(solution)/shard_map/all_to_all | solution.py:398
  35.4 8.5 collective-permute-done.3
  103.7 11.8 %collective-permute-done.12 = bf16[256,2048]{1,0:T(8,128)(2,1)S(1)} collective-permute-done((bf16[256,2048]{1,0:T(8,128)(2,1)S(1)}, bf16[256,2048]{1,0:T(8,128)(2,1)S(1)}, u32[]{:S(2)}, u32[]{:S(2)}) %collective-permute-start.12) | collective-permute-done | bytes 1048608 | tf_op jit(solution)/shard_map/ppermute | solution.py:389
  152.9 20.1 %attend.1 = (bf16[1024,2048]{1,0:T(8,128)(2,1)}, bf16[1024,384]{1,0:T(8,128)(2,1)}, bf16[1024,512]{1,0:T(8,128)(2,1)}, bf16[1024,256]{1,0:T(8,128)(2,1)}, bf16[1...) custom-call(s32[5]{0:T(128)} %stack.34.meta, bf16[512,2048]{1,0:T(8,128)(2,1)} %pad_maximum_fusion.8.refs_0_, ...), custom_call_target="tpu_custom_call" | custom-call | flops 14000000000 | bytes 24000000 | tf_op jit(solution)/shard_map/attend/pallas_call | solution.py:632
  192.6 10.0 %collective-permute-done.19 = bf16[64,2048]{1,0:T(8,128)(2,1)S(1)} collective-permute-done((bf16[64,2048]{1,0:T(8,128)(2,1)}, bf16[64,2048]{1,0:T(8,128)(2,1)S(1)}, u32[]{:S(2)}, u32[]{:S(2)}) %collective-permute-start.19) | collective-permute-done | bytes 262176 | tf_op jit(solution)/shard_map/ppermute | solution.py:402
  226.6 7.3 all-to-all-start.2
  241.8 29.8 %all-to-all-done.2 = bf16[32,64,176]{2,1,0:T(8,128)(2,1)S(1)} async-done(((bf16[32,64,176]{2,1,0:T(8,128)(2,1)}), bf16[32,64,176]{2,1,0:T(8,128)(2,1)S(1)}, u32[]{:S(2)}, u32[]{:S(2)}) %all-to-all-start.2) | async-done | bytes 720928 | tf_op jit(solution)/shard_map/all_to_all | solution.py:398
  281.9 10.5 %collective-permute-done.27 = bf16[256,2048]{1,0:T(8,128)(2,1)} collective-permute-done((bf16[256,2048]{1,0:T(8,128)(2,1)}, bf16[256,2048]{1,0:T(8,128)(2,1)}, u32[]{:S(2)}, u32[]{:S(2)}) %collective-permute-start.27) | collective-permute-done | bytes 1048608 | tf_op jit(solution)/shard_map/ppermute | solution.py:389
  308.3 11.4 %collective-permute-done.30 = bf16[128,2048]{1,0:T(8,128)(2,1)} collective-permute-done((bf16[128,2048]{1,0:T(8,128)(2,1)}, bf16[128,2048]{1,0:T(8,128)(2,1)}, u32[]{:S(2)}, u32[]{:S(2)}) %collective-permute-start.30) | collective-permute-done | bytes 524320 | tf_op jit(solution)/shard_map/ppermute | solution.py:389
  327.7 7.8 collective-permute-done.31
  338.1 6.9 collective-permute-done.33
  356.1 8.3 collective-permute-done.35
  364.4 14.1 %collective-permute-done.36 = bf16[128,2176]{1,0:T(8,128)(2,1)S(1)} collective-permute-done((bf16[128,2176]{1,0:T(8,128)(2,1)S(1)}, bf16[128,2176]{1,0:T(8,128)(2,1)S(1)}, u32[]{:S(2)}, u32[]{:S(2)}) %collective-permute-start.36) | collective-permute-done | bytes 557088 | tf_op jit(solution)/shard_map/ppermute | solution.py:402
  394.8 7.8 collective-permute-done.40
  403.9 6.9 collective-permute-done.39
  415.9 32.5 %ffn.4 = (bf16[384,2048]{1,0:T(8,128)(2,1)}, bf16[384,2048]{1,0:T(8,128)(2,1)}, bf16[384,768]{1,0:T(8,128)(2,1)}, bf16[384,768]{1,0:T(8,128)(2,1)}, bf16[384,768...) custom-call(s32[9]{0:T(128)} %get-tuple-element.746.index, ...), custom_call_target="tpu_custom_call" | custom-call | flops 20000000000 | bytes 40000000 | tf_op jit(solution)/shard_map/ffn/pallas_call | solution.py:840
  453.6 32.1 %ffn.5 = (bf16[384,2048]{1,0:T(8,128)(2,1)}, bf16[384,2048]{1,0:T(8,128)(2,1)}, bf16[384,768]{1,0:T(8,128)(2,1)}, bf16[384,768]{1,0:T(8,128)(2,1)}, bf16[384,768...) custom-call(s32[9]{0:T(128)} %get-tuple-element.747.index, ...), custom_call_target="tpu_custom_call" | custom-call | flops 20000000000 | bytes 40000000 | tf_op jit(solution)/shard_map/ffn/pallas_call | solution.py:840
  497.0 32.0 %ffn.6 = (bf16[384,2048]{1,0:T(8,128)(2,1)}, bf16[384,2048]{1,0:T(8,128)(2,1)}, bf16[384,768]{1,0:T(8,128)(2,1)}, bf16[384,768]{1,0:T(8,128)(2,1)}, bf16[384,768...) custom-call(s32[9]{0:T(128)} %get-tuple-element.748.index, ...), custom_call_target="tpu_custom_call" | custom-call | flops 20000000000 | bytes 40000000 | tf_op jit(solution)/shard_map/ffn/pallas_call | solution.py:840
  540.8 32.1 %ffn.7 = (bf16[384,2048]{1,0:T(8,128)(2,1)}, bf16[384,2048]{1,0:T(8,128)(2,1)}, bf16[384,768]{1,0:T(8,128)(2,1)}, bf16[384,768]{1,0:T(8,128)(2,1)}, bf16[384,768...) custom-call(s32[9]{0:T(128)} %get-tuple-element.749.index, ...), custom_call_target="tpu_custom_call" | custom-call | flops 20000000000 | bytes 40000000 | tf_op jit(solution)/shard_map/ffn/pallas_call | solution.py:840
  588.9 15.1 %collective-permute-done.60 = bf16[256,2176]{1,0:T(8,128)(2,1)S(1)} collective-permute-done((bf16[256,2176]{1,0:T(8,128)(2,1)S(1)}, bf16[256,2176]{1,0:T(8,128)(2,1)S(1)}, u32[]{:S(2)}, u32[]{:S(2)}) %collective-permute-start.60) | collective-permute-done | bytes 1114144 | tf_op jit(solution)/shard_map/ppermute | solution.py:389
  613.5 6.9 convolution_convert_fusion.2
  622.4 15.6 %collective-permute-done.65 = bf16[256,2176]{1,0:T(8,128)(2,1)S(1)} collective-permute-done((bf16[256,2176]{1,0:T(8,128)(2,1)S(1)}, bf16[256,2176]{1,0:T(8,128)(2,1)S(1)}, u32[]{:S(2)}, u32[]{:S(2)}) %collective-permute-start.65) | collective-permute-done | bytes 1114144 | tf_op jit(solution)/shard_map/ppermute | solution.py:389
  641.1 6.9 convolution_convert_fusion.1
  650.0 13.6 %collective-permute-done.66 = bf16[128,2176]{1,0:T(8,128)(2,1)S(1)} collective-permute-done((bf16[128,2176]{1,0:T(8,128)(2,1)S(1)}, bf16[128,2176]{1,0:T(8,128)(2,1)S(1)}, u32[]{:S(2)}, u32[]{:S(2)}) %collective-permute-start.66) | collective-permute-done | bytes 557088 | tf_op jit(solution)/shard_map/ppermute | solution.py:402
  670.7 6.9 collective-permute-done.70
  684.6 6.6 fusion.6
  693.7 19.9 %collective-permute-done.73 = bf16[256,2048]{1,0:T(8,128)(2,1)S(1)} collective-permute-done((bf16[256,2048]{1,0:T(8,128)(2,1)S(1)}, bf16[256,2048]{1,0:T(8,128)(2,1)S(1)}, u32[]{:S(2)}, u32[]{:S(2)}) %collective-permute-start.73) | collective-permute-done | bytes 1048608 | tf_op jit(solution)/shard_map/ppermute | solution.py:389
  737.4 18.5 %attend_back.1 = (bf16[1024,384]{1,0:T(8,128)(2,1)}, bf16[1024,512]{1,0:T(8,128)(2,1)}, bf16[512,640]{1,0:T(8,128)(2,1)}, bf16[512,640]{1,0:T(8,128)(2,1)}, bf16...) custom-call(s32[5]{0:T(128)} %stack.34.meta, bf16[512,2048]{1,0:T(8,128)(2,1)} %pad_maximum_fusion.9.refs_0_.near_ref, ...), custom_call_target="tpu_custom_call" | custom-call | flops 14000000000 | bytes 24000000 | tf_op jit(solution)/shard_map/attend_back/pallas_call | solution.py:712
  772.2 7.0 collective-permute-start.101
  830.2 27.7 %collective-permute-done.84 = bf16[8,256,128]{2,1,0:T(8,128)(2,1)} collective-permute-done((bf16[8,256,128]{2,1,0:T(8,128)(2,1)}, bf16[8,256,128]{2,1,0:T(8,128)(2,1)}, u32[]{:S(2)}, u32[]{:S(2)}) %collective-permute-start.84) | collective-permute-done | bytes 524320 | tf_op jit(solution)/shard_map/ppermute | solution.py:402
  884.2 11.1 %collective-permute-done.90 = bf16[128,2048]{1,0:T(8,128)(2,1)S(1)} collective-permute-done((bf16[128,2048]{1,0:T(8,128)(2,1)}, bf16[128,2048]{1,0:T(8,128)(2,1)S(1)}, u32[]{:S(2)}, u32[]{:S(2)}) %collective-permute-start.90) | collective-permute-done | bytes 524320 | tf_op jit(solution)/shard_map/ppermute | solution.py:389
  945.3 15.7 %all-to-all-done.5 = bf16[32,64,176]{2,1,0:T(8,128)(2,1)} async-done(((bf16[32,64,176]{2,1,0:T(8,128)(2,1)}), bf16[32,64,176]{2,1,0:T(8,128)(2,1)}, u32[]{:S(2)}, u32[]{:S(2)}) %all-to-all-start.5) | async-done | bytes 720928 | tf_op jit(solution)/shard_map/all_to_all | solution.py:398
  (705 shorter events, 506.0 us)
Async XLA Ops:
  7.2 80.3 %all-gather.2.cloned.1.call-start = ((), (), s32[]{:S(2)}) async-start(), calls=%async_computation.6 | async-start | bytes 2703360 | tf_op jit(solution)/shard_map/all_gather | solution.py:975
  82.9 64.4 %collective-permute-start.14 = (bf16[128,2048]{1,0:T(8,128)(2,1)}, bf16[128,2048]{1,0:T(8,128)(2,1)}, u32[]{:S(2)}, u32[]{:S(2)}) collective-permute-start(bf16[128,2048]{1,0:T(8,128)(2,1)} %collective-permute-done.1), channel_id=1, source_target_pairs={{0,16},{16,0},{1,17},{17,1},{2,18},{18,2},{3,19},{19,3},{4,20},{20... | collective-permute-start | bytes 1572872 | tf_op jit(solution)/shard_map/ppermute | solution.py:389
  128.4 50.0 %collective-permute-start.15 = (bf16[1024,704]{0,1:T(8,128)(2,1)}, bf16[1024,704]{0,1:T(8,128)(2,1)}, u32[]{:S(2)}, u32[]{:S(2)}) collective-permute-start(bf16[1024,704]{0,1:T(8,128)(2,1)} %copy.239), channel_id=1, source_target_pairs={{0,16},{16,0},{1,17},{17,1},{2,18},{18,2},{3,19},{19,3},{4,20},{20... | collective-permute-start | bytes 4325384 | tf_op jit(solution)/shard_map/ppermute | solution.py:389
  181.1 35.2 %collective-permute-start.22 = (bf16[512,2048]{1,0:T(8,128)(2,1)}, bf16[512,2048]{1,0:T(8,128)(2,1)}, u32[]{:S(2)}, u32[]{:S(2)}) collective-permute-start(bf16[512,2048]{1,0:T(8,128)(2,1)} %constant_dynamic-update-slice_fusion.3.refs_2_), channel_id=1, source_target_pairs={{0,1},{1,0},{2,3},{3,2},{4,5},{5,4},{6,7},{7,6},{8,9},{9,8},{10,11... | collective-permute-start | bytes 6291464 | tf_op jit(solution)/shard_map/ppermute | solution.py:389
  220.0 51.6 %collective-permute-start.24 = (bf16[1024,704]{0,1:T(8,128)(2,1)}, bf16[1024,704]{0,1:T(8,128)(2,1)}, u32[]{:S(2)}, u32[]{:S(2)}) collective-permute-start(bf16[1024,704]{0,1:T(8,128)(2,1)} %copy.240), channel_id=1, source_target_pairs={{0,16},{16,0},{1,17},{17,1},{2,18},{18,2},{3,19},{19,3},{4,20},{20... | collective-permute-start | bytes 4325384 | tf_op jit(solution)/shard_map/ppermute | solution.py:389
  226.6 44.9 %all-to-all-start.2 = ((bf16[32,64,176]{2,1,0:T(8,128)(2,1)}), bf16[32,64,176]{2,1,0:T(8,128)(2,1)S(1)}, u32[]{:S(2)}, u32[]{:S(2)}) async-start(bf16[32,64,176]{2,1,0:T(8,128)(2,1)} %pad_maximum_fusion.18), calls=%async_computation.2 | async-start | bytes 2097152 | tf_op jit(solution)/shard_map/all_to_all | solution.py:398
  237.0 34.6 %collective-permute-start.25 = (bf16[256,2048]{1,0:T(8,128)(2,1)}, bf16[256,2048]{1,0:T(8,128)(2,1)}, u32[]{:S(2)}, u32[]{:S(2)}) collective-permute-start(bf16[256,2048]{1,0:T(8,128)(2,1)} %add_convert_fusion.10), channel_id=1, source_target_pairs={{0,2},{2,0},{1,3},{3,1},{4,6},{6,4},{5,7},{7,5},{8,10},{10,8},{9,1... | collective-permute-start | bytes 3145736 | tf_op jit(solution)/shard_map/ppermute | solution.py:389
  238.3 43.6 %collective-permute-start.28 = (bf16[128,2048]{1,0:T(8,128)(2,1)S(1)}, bf16[128,2048]{1,0:T(8,128)(2,1)S(1)}, u32[]{:S(2)}, u32[]{:S(2)}) collective-permute-start(bf16[128,2048]{1,0:T(8,128)(2,1)S(1)} %fusion.56), channel_id=1, source_target_pairs={{0,8},{4,12},{8,0},{12,4},{1,9},{5,13},{9,1},{13,5},{2,10},{6,14},... | collective-permute-start | bytes 1572872 | tf_op jit(solution)/shard_map/ppermute | solution.py:402
  241.5 51.0 %collective-permute-start.27 = (bf16[256,2048]{1,0:T(8,128)(2,1)}, bf16[256,2048]{1,0:T(8,128)(2,1)}, u32[]{:S(2)}, u32[]{:S(2)}) collective-permute-start(bf16[256,2048]{1,0:T(8,128)(2,1)} %pad_maximum_fusion.19), channel_id=1, source_target_pairs={{0,2},{2,0},{1,3},{3,1},{4,6},{6,4},{5,7},{7,5},{8,10},{10,8},{9,1... | collective-permute-start | bytes 3145736 | tf_op jit(solution)/shard_map/ppermute | solution.py:389
  411.9 38.2 %collective-permute-start.42 = (bf16[512,2176]{1,0:T(8,128)(2,1)}, bf16[512,2176]{1,0:T(8,128)(2,1)}, u32[]{:S(2)}, u32[]{:S(2)}) collective-permute-start(bf16[512,2176]{1,0:T(8,128)(2,1)} %constant_dynamic-update-slice_fusion.15.refs_0_), channel_id=1, source_target_pairs={{0,1},{1,0},{2,3},{3,2},{4,5},{5,4},{6,7},{7,6},{8,9},{9,8},{10,11... | collective-permute-start | bytes 6684680 | tf_op jit(solution)/shard_map/ppermute | solution.py:389
  414.5 35.6 %collective-permute-start.43 = (bf16[256,2176]{1,0:T(8,128)(2,1)}, bf16[256,2176]{1,0:T(8,128)(2,1)S(1)}, u32[]{:S(2)}, u32[]{:S(2)}) collective-permute-start(bf16[256,2176]{1,0:T(8,128)(2,1)} %pad_maximum_fusion.13), channel_id=1, source_target_pairs={{0,2},{2,0},{1,3},{3,1},{4,6},{6,4},{5,7},{7,5},{8,10},{10,8},{9,1... | collective-permute-start | bytes 3342344 | tf_op jit(solution)/shard_map/ppermute | solution.py:389
  415.6 34.4 %collective-permute-start.44 = (bf16[128,2176]{1,0:T(8,128)(2,1)S(1)}, bf16[128,2176]{1,0:T(8,128)(2,1)S(1)}, u32[]{:S(2)}, u32[]{:S(2)}) collective-permute-start(bf16[128,2176]{1,0:T(8,128)(2,1)S(1)} %collective-permute-done.41), channel_id=1, source_target_pairs={{0,16},{16,0},{1,17},{17,1},{2,18},{18,2},{3,19},{19,3},{4,20},{20... | collective-permute-start | bytes 1671176 | tf_op jit(solution)/shard_map/ppermute | solution.py:389
  451.3 35.3 %collective-permute-start.45 = (bf16[512,2176]{1,0:T(8,128)(2,1)}, bf16[512,2176]{1,0:T(8,128)(2,1)}, u32[]{:S(2)}, u32[]{:S(2)}) collective-permute-start(bf16[512,2176]{1,0:T(8,128)(2,1)} %constant_dynamic-update-slice_fusion.18.refs_0_), channel_id=1, source_target_pairs={{0,1},{1,0},{2,3},{3,2},{4,5},{5,4},{6,7},{7,6},{8,9},{9,8},{10,11... | collective-permute-start | bytes 6684680 | tf_op jit(solution)/shard_map/ppermute | solution.py:389
  489.7 39.3 %collective-permute-start.49 = (bf16[512,2176]{1,0:T(8,128)(2,1)}, bf16[512,2176]{1,0:T(8,128)(2,1)}, u32[]{:S(2)}, u32[]{:S(2)}) collective-permute-start(bf16[512,2176]{1,0:T(8,128)(2,1)} %constant_dynamic-update-slice_fusion.21.refs_0_), channel_id=1, source_target_pairs={{0,1},{1,0},{2,3},{3,2},{4,5},{5,4},{6,7},{7,6},{8,9},{9,8},{10,11... | collective-permute-start | bytes 6684680 | tf_op jit(solution)/shard_map/ppermute | solution.py:389
  491.3 37.7 %collective-permute-start.50 = (bf16[256,2176]{1,0:T(8,128)(2,1)}, bf16[256,2176]{1,0:T(8,128)(2,1)}, u32[]{:S(2)}, u32[]{:S(2)}) collective-permute-start(bf16[256,2176]{1,0:T(8,128)(2,1)} %add_convert_fusion.3), channel_id=1, source_target_pairs={{0,2},{2,0},{1,3},{3,1},{4,6},{6,4},{5,7},{7,5},{8,10},{10,8},{9,1... | collective-permute-start | bytes 3342344 | tf_op jit(solution)/shard_map/ppermute | solution.py:389
  492.7 36.4 %collective-permute-start.51 = (bf16[512,2176]{1,0:T(8,128)(2,1)}, bf16[512,2176]{1,0:T(8,128)(2,1)S(1)}, u32[]{:S(2)}, u32[]{:S(2)}) collective-permute-start(bf16[512,2176]{1,0:T(8,128)(2,1)} %get-tuple-element.439), channel_id=1, source_target_pairs={{0,1},{1,0},{2,3},{3,2},{4,5},{5,4},{6,7},{7,6},{8,9},{9,8},{10,11... | collective-permute-start | bytes 6684680 | tf_op jit(solution)/shard_map/ppermute | solution.py:389
  493.2 35.9 %collective-permute-start.53 = (bf16[512,2048]{1,0:T(8,128)(2,1)}, bf16[512,2048]{1,0:T(8,128)(2,1)}, u32[]{:S(2)}, u32[]{:S(2)}) collective-permute-start(bf16[512,2048]{1,0:T(8,128)(2,1)} %get-tuple-element.440), channel_id=1, source_target_pairs={{0,1},{1,0},{2,3},{3,2},{4,5},{5,4},{6,7},{7,6},{8,9},{9,8},{10,11... | collective-permute-start | bytes 6291464 | tf_op jit(solution)/shard_map/ppermute | solution.py:389
  533.7 39.1 %collective-permute-start.54 = (bf16[128,2176]{1,0:T(8,128)(2,1)}, bf16[128,2176]{1,0:T(8,128)(2,1)S(1)}, u32[]{:S(2)}, u32[]{:S(2)}) collective-permute-start(bf16[128,2176]{1,0:T(8,128)(2,1)} %slice.654), channel_id=1, source_target_pairs={{0,16},{16,0},{1,17},{17,1},{2,18},{18,2},{3,19},{19,3},{4,20},{20... | collective-permute-start | bytes 1671176 | tf_op jit(solution)/shard_map/ppermute | solution.py:389
  535.3 37.6 %collective-permute-start.55 = (bf16[256,2176]{1,0:T(8,128)(2,1)}, bf16[256,2176]{1,0:T(8,128)(2,1)}, u32[]{:S(2)}, u32[]{:S(2)}) collective-permute-start(bf16[256,2176]{1,0:T(8,128)(2,1)} %add_convert_fusion.2), channel_id=1, source_target_pairs={{0,2},{2,0},{1,3},{3,1},{4,6},{6,4},{5,7},{7,5},{8,10},{10,8},{9,1... | collective-permute-start | bytes 3342344 | tf_op jit(solution)/shard_map/ppermute | solution.py:389
  535.4 37.5 %collective-permute-start.56 = (bf16[512,2176]{1,0:T(8,128)(2,1)}, bf16[512,2176]{1,0:T(8,128)(2,1)}, u32[]{:S(2)}, u32[]{:S(2)}) collective-permute-start(bf16[512,2176]{1,0:T(8,128)(2,1)} %get-tuple-element.466), channel_id=1, source_target_pairs={{0,1},{1,0},{2,3},{3,2},{4,5},{5,4},{6,7},{7,6},{8,9},{9,8},{10,11... | collective-permute-start | bytes 6684680 | tf_op jit(solution)/shard_map/ppermute | solution.py:389
  536.8 36.2 %collective-permute-start.58 = (bf16[512,2048]{1,0:T(8,128)(2,1)}, bf16[512,2048]{1,0:T(8,128)(2,1)}, u32[]{:S(2)}, u32[]{:S(2)}) collective-permute-start(bf16[512,2048]{1,0:T(8,128)(2,1)} %get-tuple-element.469), channel_id=1, source_target_pairs={{0,1},{1,0},{2,3},{3,2},{4,5},{5,4},{6,7},{7,6},{8,9},{9,8},{10,11... | collective-permute-start | bytes 6291464 | tf_op jit(solution)/shard_map/ppermute | solution.py:389
  582.3 67.7 %collective-permute-start.68 = (bf16[128,2048]{1,0:T(8,128)(2,1)S(1)}, bf16[128,2048]{1,0:T(8,128)(2,1)S(1)}, u32[]{:S(2)}, u32[]{:S(2)}) collective-permute-start(bf16[128,2048]{1,0:T(8,128)(2,1)S(1)} %slice.659), channel_id=1, source_target_pairs={{0,2},{2,0},{1,3},{3,1},{4,6},{6,4},{5,7},{7,5},{8,10},{10,8},{9,1... | collective-permute-start | bytes 1572872 | tf_op jit(solution)/shard_map/ppermute | solution.py:389
  756.0 43.0 %collective-permute-start.81 = (bf16[512,2048]{1,0:T(8,128)(2,1)}, bf16[512,2048]{1,0:T(8,128)(2,1)}, u32[]{:S(2)}, u32[]{:S(2)}) collective-permute-start(bf16[512,2048]{1,0:T(8,128)(2,1)} %get-tuple-element.542), channel_id=1, source_target_pairs={{0,1},{1,0},{2,3},{3,2},{4,5},{5,4},{6,7},{7,6},{8,9},{9,8},{10,11... | collective-permute-start | bytes 6291464 | tf_op jit(solution)/shard_map/ppermute | solution.py:389
  763.2 35.9 %collective-permute-start.79 = (bf16[1024,704]{0,1:T(8,128)(2,1)}, bf16[1024,704]{0,1:T(8,128)(2,1)}, u32[]{:S(2)}, u32[]{:S(2)}) collective-permute-start(bf16[1024,704]{0,1:T(8,128)(2,1)} %copy.253), channel_id=1, source_target_pairs={{0,16},{16,0},{1,17},{17,1},{2,18},{18,2},{3,19},{19,3},{4,20},{20... | collective-permute-start | bytes 4325384 | tf_op jit(solution)/shard_map/ppermute | solution.py:389
  805.2 58.9 %collective-permute-start.86 = (bf16[1024,704]{0,1:T(8,128)(2,1)}, bf16[1024,704]{0,1:T(8,128)(2,1)}, u32[]{:S(2)}, u32[]{:S(2)}) collective-permute-start(bf16[1024,704]{0,1:T(8,128)(2,1)} %copy.255), channel_id=1, source_target_pairs={{0,16},{16,0},{1,17},{17,1},{2,18},{18,2},{3,19},{19,3},{4,20},{20... | collective-permute-start | bytes 4325384 | tf_op jit(solution)/shard_map/ppermute | solution.py:389
  809.6 54.6 %collective-permute-start.88 = (bf16[256,2048]{1,0:T(8,128)(2,1)}, bf16[256,2048]{1,0:T(8,128)(2,1)}, u32[]{:S(2)}, u32[]{:S(2)}) collective-permute-start(bf16[256,2048]{1,0:T(8,128)(2,1)} %add_convert_fusion.5), channel_id=1, source_target_pairs={{0,2},{2,0},{1,3},{3,1},{4,6},{6,4},{5,7},{7,5},{8,10},{10,8},{9,1... | collective-permute-start | bytes 3145736 | tf_op jit(solution)/shard_map/ppermute | solution.py:389
  813.1 44.8 %collective-permute-start.84 = (bf16[8,256,128]{2,1,0:T(8,128)(2,1)}, bf16[8,256,128]{2,1,0:T(8,128)(2,1)}, u32[]{:S(2)}, u32[]{:S(2)}) collective-permute-start(bf16[8,256,128]{2,1,0:T(8,128)(2,1)} %get-tuple-element.711), channel_id=1, source_target_pairs={{0,8},{4,12},{8,0},{12,4},{1,9},{5,13},{9,1},{13,5},{2,10},{6,14},... | collective-permute-start | bytes 1572872 | tf_op jit(solution)/shard_map/ppermute | solution.py:402
  813.3 45.9 %collective-permute-start.83 = (bf16[8,256,128]{2,1,0:T(8,128)(2,1)}, bf16[8,256,128]{2,1,0:T(8,128)(2,1)}, u32[]{:S(2)}, u32[]{:S(2)}) collective-permute-start(bf16[8,256,128]{2,1,0:T(8,128)(2,1)} %get-tuple-element.709), channel_id=1, source_target_pairs={{0,4},{4,8},{8,12},{12,0},{1,5},{5,9},{9,13},{13,1},{2,6},{6,10},{... | collective-permute-start | bytes 1572872 | tf_op jit(solution)/shard_map/ppermute | solution.py:402
  827.3 36.8 %collective-permute-start.87 = (bf16[256,640]{1,0:T(8,128)(2,1)S(1)}, bf16[256,640]{1,0:T(8,128)(2,1)S(1)}, u32[]{:S(2)}, u32[]{:S(2)}) collective-permute-start(bf16[256,640]{1,0:T(8,128)(2,1)S(1)} %add_convert_fusion.11), channel_id=1, source_target_pairs={{0,2},{2,0},{1,3},{3,1},{4,6},{6,4},{5,7},{7,5},{8,10},{10,8},{9,1... | collective-permute-start | bytes 983048 | tf_op jit(solution)/shard_map/ppermute | solution.py:389
  859.2 104.7 %collective-permute-start.98 = (bf16[128,2048]{1,0:T(8,128)(2,1)}, bf16[128,2048]{1,0:T(8,128)(2,1)}, u32[]{:S(2)}, u32[]{:S(2)}) collective-permute-start(bf16[128,2048]{1,0:T(8,128)(2,1)} %fusion.45), channel_id=1, source_target_pairs={{0,8},{4,12},{8,0},{12,4},{1,9},{5,13},{9,1},{13,5},{2,10},{6,14},... | collective-permute-start | bytes 1572872 | tf_op jit(solution)/shard_map/ppermute | solution.py:402
  918.2 45.6 %collective-permute-start.99 = (bf16[128,2048]{1,0:T(8,128)(2,1)}, bf16[128,2048]{1,0:T(8,128)(2,1)}, u32[]{:S(2)}, u32[]{:S(2)}) collective-permute-start(bf16[128,2048]{1,0:T(8,128)(2,1)} %slice.655), channel_id=1, source_target_pairs={{0,2},{2,0},{1,3},{3,1},{4,6},{6,4},{5,7},{7,5},{8,10},{10,8},{9,1... | collective-permute-start | bytes 1572872 | tf_op jit(solution)/shard_map/ppermute | solution.py:389
  924.1 37.0 %all-to-all-start.5 = ((bf16[32,64,176]{2,1,0:T(8,128)(2,1)}), bf16[32,64,176]{2,1,0:T(8,128)(2,1)}, u32[]{:S(2)}, u32[]{:S(2)}) async-start(bf16[32,64,176]{2,1,0:T(8,128)(2,1)} %pad_maximum_fusion.22), calls=%async_computation.5 | async-start | bytes 2097152 | tf_op jit(solution)/shard_map/all_to_all | solution.py:398
  (197 other events, 2739.1 us)
Sparse Core Ops, SparseCore 0:
  10.9 63.1 all-gather.1
